TPU v7x, 32 devices: a whole 2x2x4 slice. The times are simulated.
32 devices in a mesh: sec: 4 (over x, core), dev: 8 (over z, y).
Axes of the slice: x: 2, y: 2, z: 4, core: 2. Of those that a mesh axis runs over, the one named last changes fastest.
Arguments:
- tokens: bfloat16 [256, 7168], P('dev', 'sec'), may hold values from -6 to 6
- routes: int32 [256, 8], P('dev'), may hold values from 0 to 23, all different within a row; in each aligned block of 32 rows (0 to 31, 32 to 63, ...) at most 16 rows name the same one
- scores: float32 [256, 8], P('dev'), may hold values from 0.25 to 1
- gate_up_codes: int32 [32, 2, 2, 896, 1024], P(('sec', 'dev')), may hold values from 0 to 255, as said below
- down_codes: int32 [32, 2, 128, 7168], P(('sec', 'dev')), may hold values from 0 to 255, as said below
- model_signs: int32 [32, 2, 7168], P(('sec', 'dev')), may hold values from 0 to 1, as said below
- hidden_signs: int32 [32, 1024], P(('sec', 'dev')), may hold values from 0 to 1, as said below
- gate_up_books: bfloat16 [2, 2, 256, 8], replicated, may hold values from -0.046875 to 0.046875
- down_books: bfloat16 [2, 256, 8], replicated, may hold values from -0.125 to 0.125
Outputs:
- mixed: bfloat16 [256, 7168], P('dev', 'sec')
Inputs may be any that keep to these rules, and one draw needn't show every extreme that they name: `gate_up_codes`: stacked experts 0 to 7 are equal copies of the shared expert; stacked expert 8 + e is routed expert e. `down_codes`: stacked as in gate_up_codes. `model_signs`: stacked as in gate_up_codes. `hidden_signs`: stacked as in gate_up_codes. `routes`: each token names 8 different routed experts; within each aligned block of 32 tokens no expert is named by more than 16 tokens.
All inputs are finite; a program needn't handle non-finite values.
Results may differ from a plain program's by a relative error of at most 0.0096.
Values may be sent and summed in bfloat16 or wider, within the bound.
No kernel may reach another device: no remote copies, remote signals or barrier semaphores. Data moves between devices by JAX's collectives and lax.ppermute only.
A program may use at most 192 MiB of HBM per device.

v0:
```python
import math

import jax
import jax.numpy as jnp
import numpy as np
from jax import lax
from jax.sharding import PartitionSpec as P

HAD = 128


routed_scale = 2.5


def hadamard_table(length):
    sylvester = np.ones((1, 1), np.float32)
    while sylvester.shape[0] < length:
        sylvester = np.concatenate(
            [np.concatenate([sylvester, sylvester], 1), np.concatenate([sylvester, -sylvester], 1)],
            0,
        )
    return sylvester


def rotate_rows(values):
    row_count, row_width = values.shape
    sylvester = jnp.asarray(hadamard_table(HAD), jnp.bfloat16)
    blocks = values.reshape(row_count, row_width // HAD, HAD)
    turned = jnp.einsum("rbi,ij->rbj", blocks, sylvester, preferred_element_type=jnp.float32)
    return (turned * (1.0 / math.sqrt(HAD))).reshape(row_count, row_width).astype(jnp.bfloat16)


def rotate_exact(values):
    row_count, row_width = values.shape
    sylvester = jnp.asarray(hadamard_table(HAD), jnp.float32)
    blocks = values.reshape(row_count, row_width // HAD, HAD)
    turned = jnp.einsum("rbi,ij->rbj", blocks, sylvester, precision=lax.Precision.HIGHEST)
    return (turned * (1.0 / math.sqrt(HAD))).reshape(row_count, row_width)


def dequant_pair(code_words, codebooks):
    groups = code_words.shape[2]
    hidden_width = code_words.shape[3]
    group_width = codebooks.shape[3]
    step_groups = math.gcd(groups, 32)
    levels = jnp.arange(codebooks.shape[2], dtype=jnp.int32)

    def decode_block(block_index, decoded_all):
        code_block = lax.dynamic_slice_in_dim(code_words, block_index * step_groups, step_groups, 2)
        onehot = (code_block[..., None] == levels).astype(jnp.bfloat16)
        decoded = jnp.einsum(
            "mcghk,mckj->mgjh", onehot, codebooks, preferred_element_type=jnp.float32
        )
        decoded = decoded.astype(jnp.bfloat16).reshape(2, step_groups * group_width, hidden_width)
        return lax.dynamic_update_slice_in_dim(
            decoded_all, decoded, block_index * step_groups * group_width, 1
        )

    initial = jnp.zeros((2, groups * group_width, hidden_width), jnp.bfloat16)
    return lax.fori_loop(0, groups // step_groups, decode_block, initial)


def dequant_down(code_words, codebooks):
    groups = code_words.shape[1]
    model_width = code_words.shape[2]
    group_width = codebooks.shape[2]
    step_groups = math.gcd(groups, 8)
    levels = jnp.arange(codebooks.shape[1], dtype=jnp.int32)

    def decode_block(block_index, decoded_all):
        code_block = lax.dynamic_slice_in_dim(code_words, block_index * step_groups, step_groups, 1)
        onehot = (code_block[..., None] == levels).astype(jnp.bfloat16)
        decoded = jnp.einsum("cghk,ckj->gjh", onehot, codebooks, preferred_element_type=jnp.float32)
        decoded = decoded.astype(jnp.bfloat16).reshape(step_groups * group_width, model_width)
        return lax.dynamic_update_slice_in_dim(
            decoded_all, decoded, block_index * step_groups * group_width, 0
        )

    initial = jnp.zeros((groups * group_width, model_width), jnp.bfloat16)
    return lax.fori_loop(0, groups // step_groups, decode_block, initial)


def expert_apply(row_block, weights_in, weights_down, sign_model, sign_hidden):
    front_sign = (2 * sign_model[0] - 1).astype(jnp.bfloat16)
    back_sign = (2 * sign_model[1] - 1).astype(jnp.float32)
    middle_sign = (2 * sign_hidden - 1).astype(jnp.bfloat16)
    turned = rotate_rows(row_block * front_sign)
    projected = jnp.einsum("rd,mdh->mrh", turned, weights_in, preferred_element_type=jnp.float32)
    hidden = (jax.nn.silu(projected[0]) * projected[1]).astype(jnp.bfloat16)
    folded = rotate_rows(hidden * middle_sign)
    outcome = jnp.dot(folded, weights_down, preferred_element_type=jnp.float32)
    return (back_sign * rotate_exact(outcome)).astype(jnp.bfloat16)


def route_slots(routes, experts_total):
    hits = (routes[:, :, None] == jnp.arange(experts_total, dtype=jnp.int32)).astype(jnp.int32)
    counted = jnp.sum(hits, axis=1)
    before = jnp.cumsum(counted, axis=0) - counted
    return jnp.sum(hits * before[:, None, :], axis=2)


def select_matrix(row_index, row_total):
    matches = (jnp.arange(row_total, dtype=jnp.int32)[:, None, None] == row_index[None]).astype(
        jnp.int32
    )
    return jnp.sum(matches, axis=2).astype(jnp.bfloat16)


def weight_matrix(row_index, gates, row_total):
    matches = row_index[:, :, None] == jnp.arange(row_total, dtype=jnp.int32)
    return jnp.sum(jnp.where(matches, gates.astype(jnp.float32)[:, :, None], 0.0), axis=1).astype(
        jnp.bfloat16
    )


def per_device(
    tokens,
    routes,
    scores,
    gate_up_codes,
    down_codes,
    model_signs,
    hidden_signs,
    gate_up_books,
    down_books,
):
    sections = lax.axis_size("sec")
    devices = lax.axis_size("dev")
    section = lax.axis_index("sec")
    token_count = routes.shape[0]
    capacity = 4 * token_count // devices
    slot_count = devices * capacity
    experts_total = (sections - 1) * devices
    quarter = tokens.shape[1]
    weights_in = dequant_pair(gate_up_codes[0], gate_up_books)
    weights_down = dequant_down(down_codes[0], down_books)
    slots = route_slots(routes, experts_total)
    global_row = routes * capacity + slots
    local_row = global_row - (section - 1) * slot_count
    gates = (routed_scale * scores / jnp.sum(scores, axis=1, keepdims=True)).astype(jnp.bfloat16)
    full_rows = lax.all_gather(tokens, "sec", axis=1, tiled=True)
    outgoing = jnp.dot(
        select_matrix(local_row, slot_count), full_rows, preferred_element_type=jnp.float32
    ).astype(jnp.bfloat16)
    arrived = lax.all_to_all(
        outgoing.reshape(devices, capacity, quarter * sections),
        "dev",
        split_axis=0,
        concat_axis=0,
        tiled=True,
    )
    own_rows = jnp.pad(full_rows, ((0, slot_count - token_count), (0, 0)))
    expert_input = jnp.where(
        section == 0, own_rows, arrived.reshape(slot_count, quarter * sections)
    )
    results = expert_apply(expert_input, weights_in, weights_down, model_signs[0], hidden_signs[0])
    by_section = lax.all_to_all(
        results.reshape(slot_count, sections, quarter),
        "sec",
        split_axis=1,
        concat_axis=1,
        tiled=True,
    )
    routed_part = by_section[:, 1:, :].reshape(devices, capacity, sections - 1, quarter)
    returned = lax.all_to_all(routed_part, "dev", split_axis=0, concat_axis=0, tiled=True)
    column = (routes % devices * capacity + slots) * (sections - 1) + routes // devices
    combine = weight_matrix(column, gates, slot_count * (sections - 1))
    routed_sum = jnp.dot(
        combine,
        returned.reshape(slot_count * (sections - 1), quarter),
        preferred_element_type=jnp.float32,
    )
    total = by_section[:token_count, 0, :].astype(jnp.float32) + routed_sum
    return total.astype(jnp.bfloat16)


def solution(mesh):
    in_specs = (
        P("dev", "sec"),
        P("dev", None),
        P("dev", None),
        P(("sec", "dev"), None, None, None, None),
        P(("sec", "dev"), None, None, None),
        P(("sec", "dev"), None, None),
        P(("sec", "dev"), None),
        P(),
        P(),
    )
    out_specs = P("dev", "sec")
    return jax.shard_map(
        per_device, mesh=mesh, in_specs=in_specs, out_specs=out_specs, check_vma=False
    )
```

profile of v0, /device:TPU:0, one launch (start us, length us, event | category | flops | bytes accessed | tf_op | source)
XLA Modules:
  0.0 1663.4 jit_solution(14500562836952906535)
XLA Ops:
  54.6 953.5 %while.32 = (s32[]{:T(128)}, bf16[2,7168,1024]{2,1,0:T(8,128)(2,1)}, s32[2,2,896,1024]{3,1,2,0:T(2,128)}, bf16[2,2,256,8]{2,3,1,0:T(8,128)(2,1)S(1)}, s32[]{:T(1...) while((s32[]{:T(128)}, bf16[2,7168,1024]{2,1,0:T(8,128)(2,1)}, ...), condition=%wide.region_1.0_spmd.clone, body=%wide.region_0.0_spmd.clone.sunk | while | flops 570949632 | bytes 2638033 | solution.py:60
  55.6 33.0 %fusion.56 = bf16[2,7168,1024]{2,1,0:T(8,128)(2,1)} fusion(bf16[2,7168,1024]{2,1,0:T(8,128)(2,1)} %get-tuple-element.372, s32[]{:T(128)S(6)} %select_n.94, s32[2,2,32,1024]{3,1,2,0:T(2,128)S(1)} %constant_dynamic-slice_fusion.4, bf16[2,2,256,8]{2,3,1,0:T(8,128)(2,1)S(1)} %get-tuple-element.384), kind=kOutput, calls=%fused_computation.7.clone.2 | convolution fusion | flops 570949632 | bytes 1589252 | tf_op jit(solution)/shard_map/while/body/eval_jaxpr/mcghk,mckj->mgjh/dot_general | solution.py:51
  89.7 33.0 %fusion.56 = bf16[2,7168,1024]{2,1,0:T(8,128)(2,1)} fusion(bf16[2,7168,1024]{2,1,0:T(8,128)(2,1)} %get-tuple-element.372, s32[]{:T(128)S(6)} %select_n.94, s32[2,2,32,1024]{3,1,2,0:T(2,128)S(1)} %constant_dynamic-slice_fusion.4, bf16[2,2,256,8]{2,3,1,0:T(8,128)(2,1)S(1)} %get-tuple-element.384), kind=kOutput, calls=%fused_computation.7.clone.2 | convolution fusion | flops 570949632 | bytes 1589252 | tf_op jit(solution)/shard_map/while/body/eval_jaxpr/mcghk,mckj->mgjh/dot_general | solution.py:51
  123.8 33.0 %fusion.56 = bf16[2,7168,1024]{2,1,0:T(8,128)(2,1)} fusion(bf16[2,7168,1024]{2,1,0:T(8,128)(2,1)} %get-tuple-element.372, s32[]{:T(128)S(6)} %select_n.94, s32[2,2,32,1024]{3,1,2,0:T(2,128)S(1)} %constant_dynamic-slice_fusion.4, bf16[2,2,256,8]{2,3,1,0:T(8,128)(2,1)S(1)} %get-tuple-element.384), kind=kOutput, calls=%fused_computation.7.clone.2 | convolution fusion | flops 570949632 | bytes 1589252 | tf_op jit(solution)/shard_map/while/body/eval_jaxpr/mcghk,mckj->mgjh/dot_general | solution.py:51
  157.8 33.0 %fusion.56 = bf16[2,7168,1024]{2,1,0:T(8,128)(2,1)} fusion(bf16[2,7168,1024]{2,1,0:T(8,128)(2,1)} %get-tuple-element.372, s32[]{:T(128)S(6)} %select_n.94, s32[2,2,32,1024]{3,1,2,0:T(2,128)S(1)} %constant_dynamic-slice_fusion.4, bf16[2,2,256,8]{2,3,1,0:T(8,128)(2,1)S(1)} %get-tuple-element.384), kind=kOutput, calls=%fused_computation.7.clone.2 | convolution fusion | flops 570949632 | bytes 1589252 | tf_op jit(solution)/shard_map/while/body/eval_jaxpr/mcghk,mckj->mgjh/dot_general | solution.py:51
  191.9 33.0 %fusion.56 = bf16[2,7168,1024]{2,1,0:T(8,128)(2,1)} fusion(bf16[2,7168,1024]{2,1,0:T(8,128)(2,1)} %get-tuple-element.372, s32[]{:T(128)S(6)} %select_n.94, s32[2,2,32,1024]{3,1,2,0:T(2,128)S(1)} %constant_dynamic-slice_fusion.4, bf16[2,2,256,8]{2,3,1,0:T(8,128)(2,1)S(1)} %get-tuple-element.384), kind=kOutput, calls=%fused_computation.7.clone.2 | convolution fusion | flops 570949632 | bytes 1589252 | tf_op jit(solution)/shard_map/while/body/eval_jaxpr/mcghk,mckj->mgjh/dot_general | solution.py:51
  225.9 33.0 %fusion.56 = bf16[2,7168,1024]{2,1,0:T(8,128)(2,1)} fusion(bf16[2,7168,1024]{2,1,0:T(8,128)(2,1)} %get-tuple-element.372, s32[]{:T(128)S(6)} %select_n.94, s32[2,2,32,1024]{3,1,2,0:T(2,128)S(1)} %constant_dynamic-slice_fusion.4, bf16[2,2,256,8]{2,3,1,0:T(8,128)(2,1)S(1)} %get-tuple-element.384), kind=kOutput, calls=%fused_computation.7.clone.2 | convolution fusion | flops 570949632 | bytes 1589252 | tf_op jit(solution)/shard_map/while/body/eval_jaxpr/mcghk,mckj->mgjh/dot_general | solution.py:51
  260.0 33.0 %fusion.56 = bf16[2,7168,1024]{2,1,0:T(8,128)(2,1)} fusion(bf16[2,7168,1024]{2,1,0:T(8,128)(2,1)} %get-tuple-element.372, s32[]{:T(128)S(6)} %select_n.94, s32[2,2,32,1024]{3,1,2,0:T(2,128)S(1)} %constant_dynamic-slice_fusion.4, bf16[2,2,256,8]{2,3,1,0:T(8,128)(2,1)S(1)} %get-tuple-element.384), kind=kOutput, calls=%fused_computation.7.clone.2 | convolution fusion | flops 570949632 | bytes 1589252 | tf_op jit(solution)/shard_map/while/body/eval_jaxpr/mcghk,mckj->mgjh/dot_general | solution.py:51
  294.0 33.0 %fusion.56 = bf16[2,7168,1024]{2,1,0:T(8,128)(2,1)} fusion(bf16[2,7168,1024]{2,1,0:T(8,128)(2,1)} %get-tuple-element.372, s32[]{:T(128)S(6)} %select_n.94, s32[2,2,32,1024]{3,1,2,0:T(2,128)S(1)} %constant_dynamic-slice_fusion.4, bf16[2,2,256,8]{2,3,1,0:T(8,128)(2,1)S(1)} %get-tuple-element.384), kind=kOutput, calls=%fused_computation.7.clone.2 | convolution fusion | flops 570949632 | bytes 1589252 | tf_op jit(solution)/shard_map/while/body/eval_jaxpr/mcghk,mckj->mgjh/dot_general | solution.py:51
  328.1 33.0 %fusion.56 = bf16[2,7168,1024]{2,1,0:T(8,128)(2,1)} fusion(bf16[2,7168,1024]{2,1,0:T(8,128)(2,1)} %get-tuple-element.372, s32[]{:T(128)S(6)} %select_n.94, s32[2,2,32,1024]{3,1,2,0:T(2,128)S(1)} %constant_dynamic-slice_fusion.4, bf16[2,2,256,8]{2,3,1,0:T(8,128)(2,1)S(1)} %get-tuple-element.384), kind=kOutput, calls=%fused_computation.7.clone.2 | convolution fusion | flops 570949632 | bytes 1589252 | tf_op jit(solution)/shard_map/while/body/eval_jaxpr/mcghk,mckj->mgjh/dot_general | solution.py:51
  362.1 33.0 %fusion.56 = bf16[2,7168,1024]{2,1,0:T(8,128)(2,1)} fusion(bf16[2,7168,1024]{2,1,0:T(8,128)(2,1)} %get-tuple-element.372, s32[]{:T(128)S(6)} %select_n.94, s32[2,2,32,1024]{3,1,2,0:T(2,128)S(1)} %constant_dynamic-slice_fusion.4, bf16[2,2,256,8]{2,3,1,0:T(8,128)(2,1)S(1)} %get-tuple-element.384), kind=kOutput, calls=%fused_computation.7.clone.2 | convolution fusion | flops 570949632 | bytes 1589252 | tf_op jit(solution)/shard_map/while/body/eval_jaxpr/mcghk,mckj->mgjh/dot_general | solution.py:51
  396.2 33.0 %fusion.56 = bf16[2,7168,1024]{2,1,0:T(8,128)(2,1)} fusion(bf16[2,7168,1024]{2,1,0:T(8,128)(2,1)} %get-tuple-element.372, s32[]{:T(128)S(6)} %select_n.94, s32[2,2,32,1024]{3,1,2,0:T(2,128)S(1)} %constant_dynamic-slice_fusion.4, bf16[2,2,256,8]{2,3,1,0:T(8,128)(2,1)S(1)} %get-tuple-element.384), kind=kOutput, calls=%fused_computation.7.clone.2 | convolution fusion | flops 570949632 | bytes 1589252 | tf_op jit(solution)/shard_map/while/body/eval_jaxpr/mcghk,mckj->mgjh/dot_general | solution.py:51
  430.2 33.0 %fusion.56 = bf16[2,7168,1024]{2,1,0:T(8,128)(2,1)} fusion(bf16[2,7168,1024]{2,1,0:T(8,128)(2,1)} %get-tuple-element.372, s32[]{:T(128)S(6)} %select_n.94, s32[2,2,32,1024]{3,1,2,0:T(2,128)S(1)} %constant_dynamic-slice_fusion.4, bf16[2,2,256,8]{2,3,1,0:T(8,128)(2,1)S(1)} %get-tuple-element.384), kind=kOutput, calls=%fused_computation.7.clone.2 | convolution fusion | flops 570949632 | bytes 1589252 | tf_op jit(solution)/shard_map/while/body/eval_jaxpr/mcghk,mckj->mgjh/dot_general | solution.py:51
  464.3 33.0 %fusion.56 = bf16[2,7168,1024]{2,1,0:T(8,128)(2,1)} fusion(bf16[2,7168,1024]{2,1,0:T(8,128)(2,1)} %get-tuple-element.372, s32[]{:T(128)S(6)} %select_n.94, s32[2,2,32,1024]{3,1,2,0:T(2,128)S(1)} %constant_dynamic-slice_fusion.4, bf16[2,2,256,8]{2,3,1,0:T(8,128)(2,1)S(1)} %get-tuple-element.384), kind=kOutput, calls=%fused_computation.7.clone.2 | convolution fusion | flops 570949632 | bytes 1589252 | tf_op jit(solution)/shard_map/while/body/eval_jaxpr/mcghk,mckj->mgjh/dot_general | solution.py:51
  498.3 33.0 %fusion.56 = bf16[2,7168,1024]{2,1,0:T(8,128)(2,1)} fusion(bf16[2,7168,1024]{2,1,0:T(8,128)(2,1)} %get-tuple-element.372, s32[]{:T(128)S(6)} %select_n.94, s32[2,2,32,1024]{3,1,2,0:T(2,128)S(1)} %constant_dynamic-slice_fusion.4, bf16[2,2,256,8]{2,3,1,0:T(8,128)(2,1)S(1)} %get-tuple-element.384), kind=kOutput, calls=%fused_computation.7.clone.2 | convolution fusion | flops 570949632 | bytes 1589252 | tf_op jit(solution)/shard_map/while/body/eval_jaxpr/mcghk,mckj->mgjh/dot_general | solution.py:51
  532.4 33.0 %fusion.56 = bf16[2,7168,1024]{2,1,0:T(8,128)(2,1)} fusion(bf16[2,7168,1024]{2,1,0:T(8,128)(2,1)} %get-tuple-element.372, s32[]{:T(128)S(6)} %select_n.94, s32[2,2,32,1024]{3,1,2,0:T(2,128)S(1)} %constant_dynamic-slice_fusion.4, bf16[2,2,256,8]{2,3,1,0:T(8,128)(2,1)S(1)} %get-tuple-element.384), kind=kOutput, calls=%fused_computation.7.clone.2 | convolution fusion | flops 570949632 | bytes 1589252 | tf_op jit(solution)/shard_map/while/body/eval_jaxpr/mcghk,mckj->mgjh/dot_general | solution.py:51
  566.4 33.0 %fusion.56 = bf16[2,7168,1024]{2,1,0:T(8,128)(2,1)} fusion(bf16[2,7168,1024]{2,1,0:T(8,128)(2,1)} %get-tuple-element.372, s32[]{:T(128)S(6)} %select_n.94, s32[2,2,32,1024]{3,1,2,0:T(2,128)S(1)} %constant_dynamic-slice_fusion.4, bf16[2,2,256,8]{2,3,1,0:T(8,128)(2,1)S(1)} %get-tuple-element.384), kind=kOutput, calls=%fused_computation.7.clone.2 | convolution fusion | flops 570949632 | bytes 1589252 | tf_op jit(solution)/shard_map/while/body/eval_jaxpr/mcghk,mckj->mgjh/dot_general | solution.py:51
  600.5 33.0 %fusion.56 = bf16[2,7168,1024]{2,1,0:T(8,128)(2,1)} fusion(bf16[2,7168,1024]{2,1,0:T(8,128)(2,1)} %get-tuple-element.372, s32[]{:T(128)S(6)} %select_n.94, s32[2,2,32,1024]{3,1,2,0:T(2,128)S(1)} %constant_dynamic-slice_fusion.4, bf16[2,2,256,8]{2,3,1,0:T(8,128)(2,1)S(1)} %get-tuple-element.384), kind=kOutput, calls=%fused_computation.7.clone.2 | convolution fusion | flops 570949632 | bytes 1589252 | tf_op jit(solution)/shard_map/while/body/eval_jaxpr/mcghk,mckj->mgjh/dot_general | solution.py:51
  634.5 33.0 %fusion.56 = bf16[2,7168,1024]{2,1,0:T(8,128)(2,1)} fusion(bf16[2,7168,1024]{2,1,0:T(8,128)(2,1)} %get-tuple-element.372, s32[]{:T(128)S(6)} %select_n.94, s32[2,2,32,1024]{3,1,2,0:T(2,128)S(1)} %constant_dynamic-slice_fusion.4, bf16[2,2,256,8]{2,3,1,0:T(8,128)(2,1)S(1)} %get-tuple-element.384), kind=kOutput, calls=%fused_computation.7.clone.2 | convolution fusion | flops 570949632 | bytes 1589252 | tf_op jit(solution)/shard_map/while/body/eval_jaxpr/mcghk,mckj->mgjh/dot_general | solution.py:51
  668.6 33.0 %fusion.56 = bf16[2,7168,1024]{2,1,0:T(8,128)(2,1)} fusion(bf16[2,7168,1024]{2,1,0:T(8,128)(2,1)} %get-tuple-element.372, s32[]{:T(128)S(6)} %select_n.94, s32[2,2,32,1024]{3,1,2,0:T(2,128)S(1)} %constant_dynamic-slice_fusion.4, bf16[2,2,256,8]{2,3,1,0:T(8,128)(2,1)S(1)} %get-tuple-element.384), kind=kOutput, calls=%fused_computation.7.clone.2 | convolution fusion | flops 570949632 | bytes 1589252 | tf_op jit(solution)/shard_map/while/body/eval_jaxpr/mcghk,mckj->mgjh/dot_general | solution.py:51
  702.7 33.0 %fusion.56 = bf16[2,7168,1024]{2,1,0:T(8,128)(2,1)} fusion(bf16[2,7168,1024]{2,1,0:T(8,128)(2,1)} %get-tuple-element.372, s32[]{:T(128)S(6)} %select_n.94, s32[2,2,32,1024]{3,1,2,0:T(2,128)S(1)} %constant_dynamic-slice_fusion.4, bf16[2,2,256,8]{2,3,1,0:T(8,128)(2,1)S(1)} %get-tuple-element.384), kind=kOutput, calls=%fused_computation.7.clone.2 | convolution fusion | flops 570949632 | bytes 1589252 | tf_op jit(solution)/shard_map/while/body/eval_jaxpr/mcghk,mckj->mgjh/dot_general | solution.py:51
  736.7 33.0 %fusion.56 = bf16[2,7168,1024]{2,1,0:T(8,128)(2,1)} fusion(bf16[2,7168,1024]{2,1,0:T(8,128)(2,1)} %get-tuple-element.372, s32[]{:T(128)S(6)} %select_n.94, s32[2,2,32,1024]{3,1,2,0:T(2,128)S(1)} %constant_dynamic-slice_fusion.4, bf16[2,2,256,8]{2,3,1,0:T(8,128)(2,1)S(1)} %get-tuple-element.384), kind=kOutput, calls=%fused_computation.7.clone.2 | convolution fusion | flops 570949632 | bytes 1589252 | tf_op jit(solution)/shard_map/while/body/eval_jaxpr/mcghk,mckj->mgjh/dot_general | solution.py:51
  770.8 33.0 %fusion.56 = bf16[2,7168,1024]{2,1,0:T(8,128)(2,1)} fusion(bf16[2,7168,1024]{2,1,0:T(8,128)(2,1)} %get-tuple-element.372, s32[]{:T(128)S(6)} %select_n.94, s32[2,2,32,1024]{3,1,2,0:T(2,128)S(1)} %constant_dynamic-slice_fusion.4, bf16[2,2,256,8]{2,3,1,0:T(8,128)(2,1)S(1)} %get-tuple-element.384), kind=kOutput, calls=%fused_computation.7.clone.2 | convolution fusion | flops 570949632 | bytes 1589252 | tf_op jit(solution)/shard_map/while/body/eval_jaxpr/mcghk,mckj->mgjh/dot_general | solution.py:51
  804.8 33.0 %fusion.56 = bf16[2,7168,1024]{2,1,0:T(8,128)(2,1)} fusion(bf16[2,7168,1024]{2,1,0:T(8,128)(2,1)} %get-tuple-element.372, s32[]{:T(128)S(6)} %select_n.94, s32[2,2,32,1024]{3,1,2,0:T(2,128)S(1)} %constant_dynamic-slice_fusion.4, bf16[2,2,256,8]{2,3,1,0:T(8,128)(2,1)S(1)} %get-tuple-element.384), kind=kOutput, calls=%fused_computation.7.clone.2 | convolution fusion | flops 570949632 | bytes 1589252 | tf_op jit(solution)/shard_map/while/body/eval_jaxpr/mcghk,mckj->mgjh/dot_general | solution.py:51
  838.9 33.0 %fusion.56 = bf16[2,7168,1024]{2,1,0:T(8,128)(2,1)} fusion(bf16[2,7168,1024]{2,1,0:T(8,128)(2,1)} %get-tuple-element.372, s32[]{:T(128)S(6)} %select_n.94, s32[2,2,32,1024]{3,1,2,0:T(2,128)S(1)} %constant_dynamic-slice_fusion.4, bf16[2,2,256,8]{2,3,1,0:T(8,128)(2,1)S(1)} %get-tuple-element.384), kind=kOutput, calls=%fused_computation.7.clone.2 | convolution fusion | flops 570949632 | bytes 1589252 | tf_op jit(solution)/shard_map/while/body/eval_jaxpr/mcghk,mckj->mgjh/dot_general | solution.py:51
  872.9 33.0 %fusion.56 = bf16[2,7168,1024]{2,1,0:T(8,128)(2,1)} fusion(bf16[2,7168,1024]{2,1,0:T(8,128)(2,1)} %get-tuple-element.372, s32[]{:T(128)S(6)} %select_n.94, s32[2,2,32,1024]{3,1,2,0:T(2,128)S(1)} %constant_dynamic-slice_fusion.4, bf16[2,2,256,8]{2,3,1,0:T(8,128)(2,1)S(1)} %get-tuple-element.384), kind=kOutput, calls=%fused_computation.7.clone.2 | convolution fusion | flops 570949632 | bytes 1589252 | tf_op jit(solution)/shard_map/while/body/eval_jaxpr/mcghk,mckj->mgjh/dot_general | solution.py:51
  907.0 33.0 %fusion.56 = bf16[2,7168,1024]{2,1,0:T(8,128)(2,1)} fusion(bf16[2,7168,1024]{2,1,0:T(8,128)(2,1)} %get-tuple-element.372, s32[]{:T(128)S(6)} %select_n.94, s32[2,2,32,1024]{3,1,2,0:T(2,128)S(1)} %constant_dynamic-slice_fusion.4, bf16[2,2,256,8]{2,3,1,0:T(8,128)(2,1)S(1)} %get-tuple-element.384), kind=kOutput, calls=%fused_computation.7.clone.2 | convolution fusion | flops 570949632 | bytes 1589252 | tf_op jit(solution)/shard_map/while/body/eval_jaxpr/mcghk,mckj->mgjh/dot_general | solution.py:51
  941.0 33.0 %fusion.56 = bf16[2,7168,1024]{2,1,0:T(8,128)(2,1)} fusion(bf16[2,7168,1024]{2,1,0:T(8,128)(2,1)} %get-tuple-element.372, s32[]{:T(128)S(6)} %select_n.94, s32[2,2,32,1024]{3,1,2,0:T(2,128)S(1)} %constant_dynamic-slice_fusion.4, bf16[2,2,256,8]{2,3,1,0:T(8,128)(2,1)S(1)} %get-tuple-element.384), kind=kOutput, calls=%fused_computation.7.clone.2 | convolution fusion | flops 570949632 | bytes 1589252 | tf_op jit(solution)/shard_map/while/body/eval_jaxpr/mcghk,mckj->mgjh/dot_general | solution.py:51
  975.1 33.0 %fusion.56 = bf16[2,7168,1024]{2,1,0:T(8,128)(2,1)} fusion(bf16[2,7168,1024]{2,1,0:T(8,128)(2,1)} %get-tuple-element.372, s32[]{:T(128)S(6)} %select_n.94, s32[2,2,32,1024]{3,1,2,0:T(2,128)S(1)} %constant_dynamic-slice_fusion.4, bf16[2,2,256,8]{2,3,1,0:T(8,128)(2,1)S(1)} %get-tuple-element.384), kind=kOutput, calls=%fused_computation.7.clone.2 | convolution fusion | flops 570949632 | bytes 1589252 | tf_op jit(solution)/shard_map/while/body/eval_jaxpr/mcghk,mckj->mgjh/dot_general | solution.py:51
  1026.7 507.9 %while.33 = (s32[]{:T(128)}, bf16[1024,7168]{1,0:T(8,128)(2,1)}, s32[2,128,7168]{2,0,1:T(2,128)}, bf16[2,256,8]{1,2,0:T(8,128)(2,1)S(1)}, s32[]{:T(128)}, /*inde...) while((s32[]{:T(128)}, bf16[1024,7168]{1,0:T(8,128)(2,1)}, s32[2,128,7168]{2,0,1:T(2,128)}, ...), condition=%wide.region_7.8_spmd.clone, body=%wide.region_6.7_spmd.clone.sunk | while | flops 499580928 | bytes 2302161 | solution.py:80
  1440.4 30.7 %fusion.58 = bf16[1024,7168]{1,0:T(8,128)(2,1)} fusion(bf16[1024,7168]{1,0:T(8,128)(2,1)} %get-tuple-element.402, s32[]{:T(128)S(6)} %select_n.96, s32[2,8,7168]{2,0,1:T(2,128)S(1)} %constant_dynamic-slice_fusion.5, bf16[2,256,8]{1,2,0:T(8,128)(2,1)S(1)} %get-tuple-element.414), kind=kOutput, calls=%fused_computation.16.clone.2 | convolution fusion | flops 499580928 | bytes 1384452 | tf_op jit(solution)/shard_map/while/body/eval_jaxpr/cghk,ckj->gjh/dot_general | solution.py:73
  1627.4 32.0 %all-to-all-done.2 = bf16[8,16,3,1792]{3,1,2,0:T(8,128)(2,1)S(1)} async-done(((bf16[8,16,3,1792]{3,1,2,0:T(8,128)(2,1)}), bf16[8,16,3,1792]{3,1,2,0:T(8,128)(2,1)S(1)}, u32[]{:S(2)}, u32[]{:S(2)}) %all-to-all-start.2) | async-done | bytes 1376288 | tf_op jit(solution)/shard_map/all_to_all | solution.py:165
  (126 shorter events, 677.1 us)
Async XLA Ops:
  8.5 36.2 %copy-start.1 = (bf16[32,7168]{1,0:T(8,128)(2,1)}, bf16[32,7168]{1,0:T(8,128)(2,1)S(1)}, u32[]{:S(2)}) copy-start(bf16[32,7168]{1,0:T(8,128)(2,1)S(1)} %all_gather.3) | copy-start | bytes 1376260
  13.5 1541.4 %all-to-all-start = ((bf16[8,16,7168]{2,1,0:T(8,128)(2,1)}), bf16[8,16,7168]{2,1,0:T(8,128)(2,1)}, u32[]{:S(2)}, u32[]{:S(2)}) async-start(bf16[8,16,7168]{2,1,0:T(8,128)(2,1)} %bitcast.1), calls=%async_computation | async-start | bytes 3670016 | tf_op jit(solution)/shard_map/all_to_all | solution.py:145
  44.7 9.9 copy-start.9
  1019.8 6.9 copy-start.10
  1534.6 20.1 %copy-start.4 = (s32[1,2,7168]{2,1,0:T(2,128)S(1)}, s32[1,2,7168]{2,1,0:T(2,128)}, u32[]{:S(2)}) copy-start(s32[1,2,7168]{2,1,0:T(2,128)} %param.21) | copy-start | bytes 172036
  1534.6 20.2 %copy-start.8 = (s32[1,1024]{1,0:T(1,128)S(1)}, s32[1,1024]{1,0:T(1,128)}, u32[]{:S(2)}) copy-start(s32[1,1024]{1,0:T(1,128)} %param.22) | copy-start | bytes 12292
  1534.6 20.4 %copy-start.2 = (bf16[32,7168]{1,0:T(8,128)(2,1)S(1)}, bf16[32,7168]{1,0:T(8,128)(2,1)}, u32[]{:S(2)}) copy-start(bf16[32,7168]{1,0:T(8,128)(2,1)} %copy-done.1) | copy-start | bytes 1376260
  1554.6 2.3 copy-start.5
  1572.0 8.4 copy-start.3
  1618.4 1.3 copy-start
  1619.7 7.3 copy-start.6
  1619.7 7.4 copy-start.7
  1621.0 38.4 %all-to-all-start.2 = ((bf16[8,16,3,1792]{3,1,2,0:T(8,128)(2,1)}), bf16[8,16,3,1792]{3,1,2,0:T(8,128)(2,1)S(1)}, u32[]{:S(2)}, u32[]{:S(2)}) async-start(bf16[8,16,3,1792]{3,1,2,0:T(8,128)(2,1)} %copy.74), calls=%async_computation.2 | async-start | bytes 2752512 | tf_op jit(solution)/shard_map/all_to_all | solution.py:165
where the time goes:
time: 1670 us; the launch traced here: 1660 us
  matrix products  1450 us (87%)
  local copies, waits for them, and re-layouts  132 us (8%)
  blocking collectives  33.8 us (2%)
  waiting for transfers between devices  32 us (2%)
    dot_general x28, matrix products, decode_block(): jnp.einsum('mcghk,mckj->mgjh', onehot, codebooks, preferred_element_type=...  923 us
    dot_general x16, matrix products, decode_block(): jnp.einsum('cghk,ckj->gjh', onehot, codebooks, preferred_element_type=jnp...  491 us
    dynamic_slice x44, local copies, waits for them, and re-layouts, decode_block(): lax.dynamic_slice_in_dim(code_words, block_index * step_groups, step_grou...  46.9 us
    unnamed x24, local copies, waits for them, and re-layouts  38.4 us
  transfers between devices with their start and end apart: 2, of which 1 were waited for; matrix products, arithmetic and copies ran while one was open for 92% of the time, Pallas kernels for 0%

commit v1 on v0

v1 whole, which is shorter than its diff:
```python
import math

import jax
import jax.numpy as jnp
import numpy as np
from jax import lax
from jax.experimental import pallas as pl
from jax.experimental.pallas import tpu as pltpu
from jax.sharding import PartitionSpec as P

HAD = 128
LANES = 128
ROWS = 16
VMEM = 56 << 20
ROUTED_SCALE = 2.5
UNIT = 1.0 / math.sqrt(HAD)
f32, bf16, i16, i32 = jnp.float32, jnp.bfloat16, jnp.int16, jnp.int32


def hadamard_table(length):
    sylvester = np.ones((1, 1), np.float32)
    while sylvester.shape[0] < length:
        sylvester = np.concatenate(
            [np.concatenate([sylvester, sylvester], 1), np.concatenate([sylvester, -sylvester], 1)],
            0,
        )
    return sylvester


def coded_order(group):
    return np.arange(HAD).reshape(HAD // group, group).T.reshape(-1)


def dot(left, right):
    return jnp.dot(left, right, preferred_element_type=f32)


def lookup(table, index):
    dims = lax.GatherDimensionNumbers(
        offset_dims=(),
        collapsed_slice_dims=(1,),
        start_index_map=(1,),
        operand_batching_dims=(0,),
        start_indices_batching_dims=(0,),
    )
    return lax.gather(
        table, index[..., None], dims, (1, 1), mode=lax.GatherScatterMode.PROMISE_IN_BOUNDS
    )


def book_tables(books):
    lead = books.shape[:-2]
    entries, group = books.shape[-2:]
    halves = entries // LANES
    turned = jnp.swapaxes(books, -1, -2).reshape(lead + (group, halves, 1, LANES))
    return jnp.broadcast_to(turned, lead + (group, halves, ROWS, LANES))


def decode_tile(code_words, table, group):
    sums = [None] * group
    for book in range(2):
        words = code_words(book).astype(i16)
        low = words & (LANES - 1)
        upper = words > LANES - 1
        found = [
            (lookup(table(book, i, 0), low), lookup(table(book, i, 1), low)) for i in range(group)
        ]
        for i in range(group):
            value = jnp.where(upper, found[i][1], found[i][0])
            sums[i] = value if book == 0 else sums[i] + value
    return sums


def decode_in(section, codes, tables, weights, order, place):
    _, mats, books, groups, hidden = codes.shape
    sections = 4
    group = tables.shape[2]
    share = groups // sections
    cols = 256

    def body(section_ref, codes_ref, tables_ref, *rest):
        out = rest[-1]
        for h in range(cols // LANES):
            lanes = slice(h * LANES, (h + 1) * LANES)
            for g in range(share // ROWS):
                tiles = decode_tile(
                    lambda c: codes_ref[0, 0, c, g * ROWS : (g + 1) * ROWS, lanes],
                    lambda c, i, half: tables_ref[0, c, i, half],
                    group,
                )
                for i in range(group):
                    at = (g * group + i) * ROWS
                    out[0, at : at + ROWS, lanes] = tiles[i]

    in_specs = [
        pl.BlockSpec(
            (1, 1, books, share, cols), lambda m, h, s: (0, m, 0, jnp.bitwise_xor(s[0], order), h)
        ),
        pl.BlockSpec((1,) + tables.shape[1:], lambda m, h, s: (m, 0, 0, 0, 0, 0)),
    ]
    operands = [section, codes, tables]
    aliases = {}
    if weights is not None:
        in_specs.append(pl.BlockSpec(memory_space=pl.ANY))
        operands.append(weights)
        aliases = {3: 0}
    return pl.pallas_call(
        body,
        grid_spec=pltpu.PrefetchScalarGridSpec(
            num_scalar_prefetch=1,
            grid=(mats, hidden // cols),
            in_specs=in_specs,
            out_specs=pl.BlockSpec((1, share * group, cols), lambda m, h, s: (m, place, h)),
        ),
        out_shape=jax.ShapeDtypeStruct((mats, groups * group, hidden), bf16),
        input_output_aliases=aliases,
        compiler_params=pltpu.CompilerParams(vmem_limit_bytes=VMEM),
        name="decode_in",
    )(*operands)


def rotate(values, table):
    parts = []
    for b in range(values.shape[1] // HAD):
        parts.append((dot(values[:, b * HAD : (b + 1) * HAD], table) * UNIT).astype(bf16))
    return jnp.concatenate(parts, 1)


def project(pick, pieces, weights, front, middle, had):
    slots, token_total = pick.shape
    steps = len(pieces)
    width = pieces[0].shape[1]
    hidden = weights.shape[2]

    def body(*refs):
        pick_ref, *piece_refs = refs[: 1 + steps]
        weights_ref, front_ref, middle_ref, had_ref, out, total, picked = refs[1 + steps :]
        step = pl.program_id(0)
        for at in range(steps):

            @pl.when(step == at)
            def _():
                picked[...] = piece_refs[at][...]

        rows = dot(pick_ref[...], picked[...]).astype(bf16) * front_ref[0]
        turned = rotate(rows, had_ref[...])
        for m in range(2):
            part = dot(turned, weights_ref[m])
            total[m] = jnp.where(step == 0, part, total[m] + part)

        @pl.when(step == steps - 1)
        def _():
            acted = (jax.nn.silu(total[0]) * total[1]).astype(bf16)
            out[...] = rotate(acted * middle_ref[...], had_ref[...])

    whole = lambda shape: pl.BlockSpec(shape, lambda s: (0,) * len(shape))
    return pl.pallas_call(
        body,
        grid=(steps,),
        in_specs=[whole(pick.shape)]
        + [whole(p.shape) for p in pieces]
        + [
            pl.BlockSpec((2, width, hidden), lambda s: (0, s, 0)),
            pl.BlockSpec((1, 1, width), lambda s: (s, 0, 0)),
            whole(middle.shape),
            whole(had.shape),
        ],
        out_specs=whole((slots, hidden)),
        out_shape=jax.ShapeDtypeStruct((slots, hidden), bf16),
        scratch_shapes=[
            pltpu.VMEM((2, slots, hidden), f32),
            pltpu.VMEM((token_total, width), bf16),
        ],
        compiler_params=pltpu.CompilerParams(vmem_limit_bytes=VMEM),
        name="project",
    )(pick, *pieces, weights, front, middle, had)


def produce(section, codes, tables, folded, back, had, spread, order, chunk, chunks):
    _, books, groups, width = codes.shape
    sections = 4
    group = tables.shape[1]
    slots, hidden = folded.shape
    token_total = spread.shape[0]
    steps = width // sections // chunks // LANES
    pair = 2

    def body(section_ref, codes_ref, tables_ref, folded_ref, back_ref, had_ref, spread_ref, out):
        outcome = None
        for p in range(groups // ROWS // pair):
            tiles = []
            for g in range(p * pair, (p + 1) * pair):
                tiles += decode_tile(
                    lambda c: codes_ref[0, c, g * ROWS : (g + 1) * ROWS, :],
                    lambda c, i, half: tables_ref[c, i, half],
                    group,
                )
            depth = pair * group * ROWS
            part = dot(folded_ref[:, p * depth : (p + 1) * depth], jnp.concatenate(tiles, 0))
            outcome = part if outcome is None else outcome + part
        high = outcome.astype(bf16)
        left = outcome - high.astype(f32)
        mid = left.astype(bf16)
        low = (left - mid.astype(f32)).astype(bf16)
        table = had_ref[...]
        turned = (dot(high, table) + (dot(mid, table) + dot(low, table))) * UNIT
        result = (back_ref[...] * turned).astype(bf16)
        out[...] = dot(spread_ref[...], result).astype(bf16)

    def column(j, s):
        return (jnp.bitwise_xor(s[0], order) * chunks + chunk) * steps + j

    whole = lambda shape: pl.BlockSpec(shape, lambda j, s: (0,) * len(shape))
    return pl.pallas_call(
        body,
        grid_spec=pltpu.PrefetchScalarGridSpec(
            num_scalar_prefetch=1,
            grid=(steps,),
            in_specs=[
                pl.BlockSpec((1, books, groups, LANES), lambda j, s: (0, 0, 0, column(j, s))),
                whole(tables.shape),
                whole(folded.shape),
                pl.BlockSpec((1, LANES), lambda j, s: (0, column(j, s))),
                whole(had.shape),
                whole(spread.shape),
            ],
            out_specs=pl.BlockSpec((token_total, LANES), lambda j, s: (0, j)),
        ),
        out_shape=jax.ShapeDtypeStruct((token_total, steps * LANES), bf16),
        compiler_params=pltpu.CompilerParams(vmem_limit_bytes=VMEM),
        name="produce",
    )(section, codes, tables, folded, back, had, spread)


def swap(values, axis, stride):
    size = lax.axis_size(axis)
    return lax.ppermute(values, axis, [(i, i ^ stride) for i in range(size)])


def per_device(
    tokens,
    routes,
    scores,
    gate_up_codes,
    down_codes,
    model_signs,
    hidden_signs,
    gate_up_books,
    down_books,
):
    sections = lax.axis_size("sec")
    devices = lax.axis_size("dev")
    section = lax.axis_index("sec")
    device = lax.axis_index("dev")
    token_count, quarter = tokens.shape
    width = quarter * sections
    token_total = token_count * devices
    slots = 4 * token_count
    group = gate_up_books.shape[-1]
    chunks = 2
    half = quarter // chunks
    strides = [1 << b for b in range(devices.bit_length() - 1)]
    section_word = section.astype(i32).reshape(1)

    relative = [0]
    for stride in reversed(strides):
        relative = relative + [b ^ stride for b in relative]
    places = [0, 2, 1, 3]

    gates = (ROUTED_SCALE * scores / jnp.sum(scores, axis=1, keepdims=True)).astype(bf16)
    facts = jnp.concatenate([routes.astype(f32), gates.astype(f32)], 1)
    facts = lax.all_gather(facts, "dev", axis=0)
    source = jnp.bitwise_xor(jnp.asarray(relative, i32), device.astype(i32))
    facts = jnp.take(facts, source, axis=0).reshape(token_total, -1)
    top = routes.shape[1]
    expert = ((section - 1) * devices + device).astype(f32)
    named = facts[:, :top] == expert
    hit = jnp.any(named, axis=1)
    gate = jnp.sum(jnp.where(named, facts[:, top:], 0.0), axis=1)
    earlier = (jnp.arange(token_total)[:, None] < jnp.arange(token_total)[None, :]).astype(f32)
    slot = jnp.sum(jnp.where(hit[:, None], earlier, 0.0), axis=0)
    slot = jnp.where(hit, slot, -1.0)
    shared = section == 0
    token_id = jnp.arange(token_total)
    own = token_id < token_count
    slot = jnp.where(shared, jnp.where(own, token_id.astype(f32), -1.0), slot)
    gate = jnp.where(shared, 1.0, gate)
    slot_id = jnp.arange(slots).astype(f32)
    pick = (slot_id[:, None] == slot[None, :]).astype(bf16)
    spread = jnp.where(slot[:, None] == slot_id[None, :], gate[:, None], 0.0).astype(bf16)

    tables_in = book_tables(gate_up_books)
    tables_down = book_tables(down_books)
    sylvester = hadamard_table(HAD)
    had_coded = jnp.asarray(sylvester[:, coded_order(group)], bf16)
    had = jnp.asarray(sylvester, bf16)
    front = (2 * model_signs[0, 0] - 1).astype(bf16).reshape(sections, chunks, 1, half)
    front = jnp.take(front, jnp.bitwise_xor(jnp.asarray(places, i32), section.astype(i32)), axis=0)
    front = front.reshape(sections * chunks, 1, half)
    back = (2 * model_signs[0, 1] - 1).astype(f32).reshape(1, width)
    middle = (2 * hidden_signs - 1).astype(bf16)

    def fence(*values):
        return lax.optimization_barrier(values)

    first, second = tokens[:, :half], tokens[:, half:]
    gathered = []
    for part in (first, second):
        gathered.append([part] + [swap(part, "dev", b) for b in relative[1 : devices // 2]])
    weights = decode_in(section_word, gate_up_codes, tables_in, None, places[0], 0)
    weights, gathered = fence(weights, gathered)
    first, second = [jnp.concatenate(g, 0) for g in gathered]
    first_near = swap(first, "dev", 1)
    second_cross = swap(second, "sec", 2)
    weights, first, second = fence(weights, first, second)
    weights = decode_in(section_word, gate_up_codes, tables_in, weights, places[1], 1)
    weights, first_near, second_cross = fence(weights, first_near, second_cross)
    first = jnp.concatenate([first, first_near], 0)
    first_cross = swap(first, "sec", 2)
    second_near = swap(second, "dev", 1)
    second_both = swap(second_cross, "dev", 1)
    weights = decode_in(section_word, gate_up_codes, tables_in, weights, places[2], 2)
    weights, first_cross, second_near, second_both = fence(
        weights, first_cross, second_near, second_both
    )
    second = jnp.concatenate([second, second_near], 0)
    second_cross = jnp.concatenate([second_cross, second_both], 0)
    pieces = [first, second, first_cross, second_cross]
    pieces = pieces + [swap(p, "sec", 1) for p in pieces]
    weights = decode_in(section_word, gate_up_codes, tables_in, weights, places[3], 3)

    folded = project(pick, pieces, weights, front, middle, had_coded)

    made = {}
    for order, chunk in ((3, 0), (2, 0), (3, 1), (2, 1), (1, 0), (0, 0), (1, 1), (0, 1)):
        made[order, chunk] = produce(
            section_word, down_codes, tables_down, folded, back, had, spread, order, chunk, chunks
        )
        folded, made[order, chunk] = fence(folded, made[order, chunk])
    outs = []
    for chunk in range(chunks):
        crossing = made[2, chunk].astype(f32) + swap(made[3, chunk], "sec", 1).astype(f32)
        crossed = swap(crossing.astype(bf16), "sec", 2).astype(f32)
        total = made[0, chunk].astype(f32) + swap(made[1, chunk], "sec", 1).astype(f32) + crossed
        for stride in strides:
            rows = total.shape[0] // 2
            sent = swap(total[rows:].astype(bf16), "dev", stride)
            total = total[:rows] + sent.astype(f32)
        outs.append(total.astype(bf16))
    return jnp.concatenate(outs, 1)


def solution(mesh):
    in_specs = (
        P("dev", "sec"),
        P("dev", None),
        P("dev", None),
        P(("sec", "dev"), None, None, None, None),
        P(("sec", "dev"), None, None, None),
        P(("sec", "dev"), None, None),
        P(("sec", "dev"), None),
        P(),
        P(),
    )
    out_specs = P("dev", "sec")
    return jax.shard_map(
        per_device, mesh=mesh, in_specs=in_specs, out_specs=out_specs, check_vma=False
    )
```

time: 1670 us -> 243 us (0.15)
  matrix products: 1450 us -> 0 us
  Pallas kernels: 0 us -> 147 us
  local copies, waits for them, and re-layouts: 132 us -> 6.75 us
    dot_general x51 -> x0, matrix products: 1450 us -> none  [the longest x28 923 us: decode_block(): jnp.einsum('mcghk,mckj->mgjh', onehot, codebooks, preferred_element_type=...]
    pallas_call x0 -> x13, Pallas kernels: none -> 147 us  [the longest x8 81.4 us: produce(): pl.pallas_call(body, grid_spec=pltpu.PrefetchScalarGridSpec(num_scalar_pr...]
    dynamic_slice x44 -> x0, local copies, waits for them, and re-layouts: 46.9 us -> none  [decode_block(): lax.dynamic_slice_in_dim(code_words, block_index * step_groups, step_grou...]
    unnamed x24 -> x27, local copies, waits for them, and re-layouts: 38.4 us -> 1.92 us
    all_to_all x2 -> x0, waiting for transfers between devices: 32 us -> none  [the longest x1 32 us: per_device(): lax.all_to_all(routed_part, 'dev', split_axis=0, concat_axis=0, tiled=True)]
    ppermute x0 -> x27, starting transfers between devices: none -> 25.7 us  [swap(): return lax.ppermute(values, axis, [(i, i ^ stride) for i in range(size)])]
    all_to_all x1 -> x0, blocking collectives: 25.3 us -> none  [per_device(): lax.all_to_all(results.reshape(slot_count, sections, quarter), 'sec', spl...]
    all_gather x1, blocking collectives: 8.46 us -> 30.5 us  [per_device(): facts = lax.all_gather(facts, 'dev', axis=0)]
  transfers between devices with their start and end apart: 2 -> 27, of which waited for: 1 -> 6; matrix products, arithmetic and copies ran while one was open for 92% -> 7% of each run, Pallas kernels for 0% -> 50%
where the time goes in v1:
time: 243 us; the launch traced here: 241 us
  Pallas kernels  147 us (60%)
  blocking collectives  30.5 us (13%)
  starting transfers between devices  25.7 us (11%)
  waiting for transfers between devices  16.5 us (7%)
  other arithmetic  14.8 us (6%)
  local copies, waits for them, and re-layouts  6.75 us (3%)
    pallas_call x8, Pallas kernels, produce(): pl.pallas_call(body, grid_spec=pltpu.PrefetchScalarGridSpec(num_scalar_pr...  81.4 us
    pallas_call x4, Pallas kernels, decode_in(): pl.pallas_call(body, grid_spec=pltpu.PrefetchScalarGridSpec(num_scalar_pr...  49 us
    all_gather x1, blocking collectives, per_device(): facts = lax.all_gather(facts, 'dev', axis=0)  30.5 us
    ppermute x27, starting transfers between devices, swap(): return lax.ppermute(values, axis, [(i, i ^ stride) for i in range(size)])  25.7 us
    ppermute x27, waiting for transfers between devices, swap(): return lax.ppermute(values, axis, [(i, i ^ stride) for i in range(size)])  16.5 us
    pallas_call x1, Pallas kernels, project(): pl.pallas_call(body, grid=(steps,), in_specs=[whole(pick.shape)] + [whole...  16.1 us
  transfers between devices with their start and end apart: 27, of which 6 were waited for; matrix products, arithmetic and copies ran while one was open for 7% of the time, Pallas kernels for 50%

profile of v1, /device:TPU:0, one launch (start us, length us, event | category | flops | bytes accessed | tf_op | source)
XLA Modules:
  0.0 241.2 jit_solution(9336083801486105188)
XLA Ops:
  0.9 4.1 %collective-permute-start = (bf16[32,896]{1,0:T(8,128)(2,1)S(1)}, bf16[32,896]{1,0:T(8,128)(2,1)S(1)}, u32[]{:S(2)}, u32[]{:S(2)}) collective-permute-start(bf16[32,896]{1,0:T(8,128)(2,1)S(1)} %get-tuple-element.40), channel_id=1, source_target_pairs={{0,4},{1,5},{2,6},{3,7},{4,0},{5,1},{6,2},{7,3},{8,12},{9,13},{10,... | collective-permute-start | bytes 172040 | tf_op jit(solution)/shard_map/ppermute | solution.py:237
  5.0 1.6 collective-permute-start.1
  6.5 1.9 collective-permute-start.3
  8.5 2.5 %collective-permute-start.4 = (bf16[32,896]{1,0:T(8,128)(2,1)S(1)}, bf16[32,896]{1,0:T(8,128)(2,1)S(1)}, u32[]{:S(2)}, u32[]{:S(2)}) collective-permute-start(bf16[32,896]{1,0:T(8,128)(2,1)S(1)} %get-tuple-element.44), channel_id=1, source_target_pairs={{0,2},{1,3},{2,0},{3,1},{4,6},{5,7},{6,4},{7,5},{8,10},{9,11},{10,... | collective-permute-start | bytes 172040 | tf_op jit(solution)/shard_map/ppermute | solution.py:237
  11.8 1.5 convert_bitcast_fusion.back_ref
  16.1 30.5 %all-gather.1 = f32[8,32,16]{1,2,0:T(8,128)S(1)} all-gather(f32[1,32,16]{1,2,0:T(8,128)S(1)} %maximum_bitcast_fusion), channel_id=2, replica_groups=mesh['sec'=4,'dev'=8] {'dev'}, dimensions={0}, use_global_device_ids=true | all-gather | bytes 18432 | tf_op jit(solution)/shard_map/all_gather | solution.py:272
  49.6 1.3 add_convert_fusion.2.refs_11_
  53.1 12.3 %decode_in.4.rest_0_ = bf16[2,7168,1024]{2,1,0:T(8,128)(2,1)} custom-call(s32[1]{0:T(128)} %bitcast.1.section_ref, s32[1,2,2,896,1024]{4,3,2,1,0:T(8,128)} %codes_ref.15, bf16[2,2,8,2,16,128]{5,4,3,2,1,0:T(8,128)(2,1)} %broadcast_in_dim.101.tables_ref), custom_call_target="tpu_custom_call" | custom-call | tf_op jit(solution)/shard_map/decode_in/pallas_call | solution.py:107
  65.5 1.6 collective-permute-start.7
  67.1 1.6 collective-permute-start.6
  68.7 12.2 %decode_in.5.rest_0_ = bf16[2,7168,1024]{2,1,0:T(8,128)(2,1)} custom-call(s32[1]{0:T(128)} %bitcast.1.section_ref, s32[1,2,2,896,1024]{4,3,2,1,0:T(8,128)} %codes_ref.15, bf16[2,2,8,2,16,128]{5,4,3,2,1,0:T(8,128)(2,1)} %broadcast_in_dim.101.tables_ref, bf16[2,7168,1024]{2,1,0:T(8,128)(2,1)} %decode_in.4.rest_0_), custom_call_target="tpu_custom_call", output_to_operand_aliasing={{}: (3, {})} | custom-call | tf_op jit(solution)/shard_map/decode_in/pallas_call | solution.py:107
  82.1 1.5 collective-permute-start.10
  83.8 12.3 %decode_in.6.rest_0_ = bf16[2,7168,1024]{2,1,0:T(8,128)(2,1)} custom-call(s32[1]{0:T(128)} %bitcast.1.section_ref, s32[1,2,2,896,1024]{4,3,2,1,0:T(8,128)} %codes_ref.15, bf16[2,2,8,2,16,128]{5,4,3,2,1,0:T(8,128)(2,1)} %broadcast_in_dim.101.tables_ref, bf16[2,7168,1024]{2,1,0:T(8,128)(2,1)} %decode_in.5.rest_0_), custom_call_target="tpu_custom_call", output_to_operand_aliasing={{}: (3, {})} | custom-call | tf_op jit(solution)/shard_map/decode_in/pallas_call | solution.py:107
  98.8 12.2 %decode_in.7.refs_9_ = bf16[2,7168,1024]{2,1,0:T(8,128)(2,1)} custom-call(s32[1]{0:T(128)} %bitcast.1.section_ref, s32[1,2,2,896,1024]{4,3,2,1,0:T(8,128)} %codes_ref.15, bf16[2,2,8,2,16,128]{5,4,3,2,1,0:T(8,128)(2,1)} %broadcast_in_dim.101.tables_ref, bf16[2,7168,1024]{2,1,0:T(8,128)(2,1)} %decode_in.6.rest_0_), custom_call_target="tpu_custom_call", output_to_operand_aliasing={{}: (3, {})} | custom-call | tf_op jit(solution)/shard_map/decode_in/pallas_call | solution.py:107
  112.9 16.1 %project.1.folded_ref = bf16[128,1024]{1,0:T(8,128)(2,1)} custom-call(bf16[128,256]{1,0:T(8,128)(2,1)} %compare_convert_fusion.refs_0_, bf16[256,896]{1,0:T(8,128)(2,1)} %copy-done.2, bf16[256,896]{1,0:T(8,128)(2,1)} %copy-done, bf16[256,896]{1,0:T(8,128)(2,1)} %copy-done.3, bf16[256,896]{1,0:T(8,128)(2,1)} %copy-done.1, bf16[256,896]{1,0:T(8,128)(2,1)} %copy-done.4, ...), custom_call_target="tpu_custom_call" | custom-call | tf_op jit(solution)/shard_map/project/pallas_call | solution.py:157
  129.7 10.1 %produce.8 = bf16[256,896]{1,0:T(8,128)(2,1)} custom-call(s32[1]{0:T(128)} %bitcast.1.section_ref, s32[1,2,128,7168]{3,2,1,0:T(8,128)} %codes_ref.23, bf16[2,8,2,16,128]{4,3,2,1,0:T(8,128)(2,1)} %broadcast_in_dim.108.tables_ref, bf16[128,1024]{1,0:T(8,128)(2,1)} %project.1.folded_ref, f32[1,7168]{1,0:T(1,128)} %convert_bitcast_fusion.back_ref, ...), custom_call_target="tpu_custom_call" | custom-call | tf_op jit(solution)/shard_map/produce/pallas_call | solution.py:214
  139.9 10.1 %produce.9 = bf16[256,896]{1,0:T(8,128)(2,1)} custom-call(s32[1]{0:T(128)} %bitcast.1.section_ref, s32[1,2,128,7168]{3,2,1,0:T(8,128)} %codes_ref.23, bf16[2,8,2,16,128]{4,3,2,1,0:T(8,128)(2,1)} %broadcast_in_dim.108.tables_ref, bf16[128,1024]{1,0:T(8,128)(2,1)} %project.1.folded_ref, f32[1,7168]{1,0:T(1,128)} %convert_bitcast_fusion.back_ref, ...), custom_call_target="tpu_custom_call" | custom-call | tf_op jit(solution)/shard_map/produce/pallas_call | solution.py:214
  150.0 10.2 %produce.10 = bf16[256,896]{1,0:T(8,128)(2,1)} custom-call(s32[1]{0:T(128)} %bitcast.1.section_ref, s32[1,2,128,7168]{3,2,1,0:T(8,128)} %codes_ref.23, bf16[2,8,2,16,128]{4,3,2,1,0:T(8,128)(2,1)} %broadcast_in_dim.108.tables_ref, bf16[128,1024]{1,0:T(8,128)(2,1)} %project.1.folded_ref, f32[1,7168]{1,0:T(1,128)} %convert_bitcast_fusion.back_ref, ...), custom_call_target="tpu_custom_call" | custom-call | tf_op jit(solution)/shard_map/produce/pallas_call | solution.py:214
  160.7 10.2 %produce.11 = bf16[256,896]{1,0:T(8,128)(2,1)} custom-call(s32[1]{0:T(128)} %bitcast.1.section_ref, s32[1,2,128,7168]{3,2,1,0:T(8,128)} %codes_ref.23, bf16[2,8,2,16,128]{4,3,2,1,0:T(8,128)(2,1)} %broadcast_in_dim.108.tables_ref, bf16[128,1024]{1,0:T(8,128)(2,1)} %project.1.folded_ref, f32[1,7168]{1,0:T(1,128)} %convert_bitcast_fusion.back_ref, ...), custom_call_target="tpu_custom_call" | custom-call | tf_op jit(solution)/shard_map/produce/pallas_call | solution.py:214
  170.9 10.2 %produce.12 = bf16[256,896]{1,0:T(8,128)(2,1)} custom-call(s32[1]{0:T(128)} %bitcast.1.section_ref, s32[1,2,128,7168]{3,2,1,0:T(8,128)} %codes_ref.23, bf16[2,8,2,16,128]{4,3,2,1,0:T(8,128)(2,1)} %broadcast_in_dim.108.tables_ref, bf16[128,1024]{1,0:T(8,128)(2,1)} %project.1.folded_ref, f32[1,7168]{1,0:T(1,128)} %convert_bitcast_fusion.back_ref, ...), custom_call_target="tpu_custom_call" | custom-call | tf_op jit(solution)/shard_map/produce/pallas_call | solution.py:214
  182.3 1.5 collective-permute-start.17
  183.8 10.1 %produce.13 = bf16[256,896]{1,0:T(8,128)(2,1)} custom-call(s32[1]{0:T(128)} %bitcast.1.section_ref, s32[1,2,128,7168]{3,2,1,0:T(8,128)} %codes_ref.23, bf16[2,8,2,16,128]{4,3,2,1,0:T(8,128)(2,1)} %broadcast_in_dim.108.tables_ref, bf16[128,1024]{1,0:T(8,128)(2,1)} %project.1.folded_ref, f32[1,7168]{1,0:T(1,128)} %convert_bitcast_fusion.back_ref, ...), custom_call_target="tpu_custom_call" | custom-call | tf_op jit(solution)/shard_map/produce/pallas_call | solution.py:214
  194.0 10.2 %produce.14 = bf16[256,896]{1,0:T(8,128)(2,1)} custom-call(s32[1]{0:T(128)} %bitcast.1.section_ref, s32[1,2,128,7168]{3,2,1,0:T(8,128)} %codes_ref.23, bf16[2,8,2,16,128]{4,3,2,1,0:T(8,128)(2,1)} %broadcast_in_dim.108.tables_ref, bf16[128,1024]{1,0:T(8,128)(2,1)} %project.1.folded_ref, f32[1,7168]{1,0:T(1,128)} %convert_bitcast_fusion.back_ref, ...), custom_call_target="tpu_custom_call" | custom-call | tf_op jit(solution)/shard_map/produce/pallas_call | solution.py:214
  206.1 10.2 %produce.15 = bf16[256,896]{1,0:T(8,128)(2,1)} custom-call(s32[1]{0:T(128)} %bitcast.1.section_ref, s32[1,2,128,7168]{3,2,1,0:T(8,128)} %codes_ref.23, bf16[2,8,2,16,128]{4,3,2,1,0:T(8,128)(2,1)} %broadcast_in_dim.108.tables_ref, bf16[128,1024]{1,0:T(8,128)(2,1)} %project.1.folded_ref, f32[1,7168]{1,0:T(1,128)} %convert_bitcast_fusion.back_ref, ...), custom_call_target="tpu_custom_call" | custom-call | tf_op jit(solution)/shard_map/produce/pallas_call | solution.py:214
  216.3 1.2 convert_add_fusion.1
  219.5 1.4 collective-permute-start.24
  220.9 5.2 %collective-permute-done.18 = bf16[128,896]{1,0:T(8,128)(2,1)S(1)} collective-permute-done((bf16[128,896]{1,0:T(8,128)(2,1)S(1)}, bf16[128,896]{1,0:T(8,128)(2,1)S(1)}, u32[]{:S(2)}, u32[]{:S(2)}) %collective-permute-start.18) | collective-permute-done | bytes 229408 | tf_op jit(solution)/shard_map/ppermute | solution.py:237
  226.2 3.9 %collective-permute-done.24 = bf16[128,896]{1,0:T(8,128)(2,1)S(1)} collective-permute-done((bf16[128,896]{1,0:T(8,128)(2,1)S(1)}, bf16[128,896]{1,0:T(8,128)(2,1)S(1)}, u32[]{:S(2)}, u32[]{:S(2)}) %collective-permute-start.24) | collective-permute-done | bytes 229408 | tf_op jit(solution)/shard_map/ppermute | solution.py:237
  231.0 1.9 collective-permute-start.20
  232.9 2.2 collective-permute-done.25
  235.1 1.2 collective-permute-start.26
  236.3 4.2 %collective-permute-done.26 = bf16[32,896]{1,0:T(8,128)(2,1)S(1)} collective-permute-done((bf16[32,896]{1,0:T(8,128)(2,1)S(1)}, bf16[32,896]{1,0:T(8,128)(2,1)S(1)}, u32[]{:S(2)}, u32[]{:S(2)}) %collective-permute-start.26) | collective-permute-done | bytes 57376 | tf_op jit(solution)/shard_map/ppermute | solution.py:237
  (121 shorter events, 23.7 us)
Async XLA Ops:
  0.9 50.1 %collective-permute-start = (bf16[32,896]{1,0:T(8,128)(2,1)S(1)}, bf16[32,896]{1,0:T(8,128)(2,1)S(1)}, u32[]{:S(2)}, u32[]{:S(2)}) collective-permute-start(bf16[32,896]{1,0:T(8,128)(2,1)S(1)} %get-tuple-element.40), channel_id=1, source_target_pairs={{0,4},{1,5},{2,6},{3,7},{4,0},{5,1},{6,2},{7,3},{8,12},{9,13},{10,... | collective-permute-start | bytes 172040 | tf_op jit(solution)/shard_map/ppermute | solution.py:237
  5.0 60.4 %collective-permute-start.1 = (bf16[32,896]{1,0:T(8,128)(2,1)S(1)}, bf16[32,896]{1,0:T(8,128)(2,1)S(1)}, u32[]{:S(2)}, u32[]{:S(2)}) collective-permute-start(bf16[32,896]{1,0:T(8,128)(2,1)S(1)} %get-tuple-element.40), channel_id=1, source_target_pairs={{0,2},{1,3},{2,0},{3,1},{4,6},{5,7},{6,4},{7,5},{8,10},{9,11},{10,... | collective-permute-start | bytes 172040 | tf_op jit(solution)/shard_map/ppermute | solution.py:237
  6.5 58.9 %collective-permute-start.2 = (bf16[32,896]{1,0:T(8,128)(2,1)S(1)}, bf16[32,896]{1,0:T(8,128)(2,1)S(1)}, u32[]{:S(2)}, u32[]{:S(2)}) collective-permute-start(bf16[32,896]{1,0:T(8,128)(2,1)S(1)} %get-tuple-element.40), channel_id=1, source_target_pairs={{0,6},{1,7},{2,4},{3,5},{4,2},{5,3},{6,0},{7,1},{8,14},{9,15},{10,... | collective-permute-start | bytes 172040 | tf_op jit(solution)/shard_map/ppermute | solution.py:237
  6.5 58.9 %collective-permute-start.3 = (bf16[32,896]{1,0:T(8,128)(2,1)S(1)}, bf16[32,896]{1,0:T(8,128)(2,1)S(1)}, u32[]{:S(2)}, u32[]{:S(2)}) collective-permute-start(bf16[32,896]{1,0:T(8,128)(2,1)S(1)} %get-tuple-element.44), channel_id=1, source_target_pairs={{0,4},{1,5},{2,6},{3,7},{4,0},{5,1},{6,2},{7,3},{8,12},{9,13},{10,... | collective-permute-start | bytes 172040 | tf_op jit(solution)/shard_map/ppermute | solution.py:237
  8.5 57.0 %collective-permute-start.4 = (bf16[32,896]{1,0:T(8,128)(2,1)S(1)}, bf16[32,896]{1,0:T(8,128)(2,1)S(1)}, u32[]{:S(2)}, u32[]{:S(2)}) collective-permute-start(bf16[32,896]{1,0:T(8,128)(2,1)S(1)} %get-tuple-element.44), channel_id=1, source_target_pairs={{0,2},{1,3},{2,0},{3,1},{4,6},{5,7},{6,4},{7,5},{8,10},{9,11},{10,... | collective-permute-start | bytes 172040 | tf_op jit(solution)/shard_map/ppermute | solution.py:237
  50.9 14.5 %collective-permute-start.5 = (bf16[32,896]{1,0:T(8,128)(2,1)S(1)}, bf16[32,896]{1,0:T(8,128)(2,1)S(1)}, u32[]{:S(2)}, u32[]{:S(2)}) collective-permute-start(bf16[32,896]{1,0:T(8,128)(2,1)S(1)} %get-tuple-element.44), channel_id=1, source_target_pairs={{0,6},{1,7},{2,4},{3,5},{4,2},{5,3},{6,0},{7,1},{8,14},{9,15},{10,... | collective-permute-start | bytes 172040 | tf_op jit(solution)/shard_map/ppermute | solution.py:237
  65.5 15.4 %collective-permute-start.7 = (bf16[128,896]{1,0:T(8,128)(2,1)S(1)}, bf16[128,896]{1,0:T(8,128)(2,1)S(1)}, u32[]{:S(2)}, u32[]{:S(2)}) collective-permute-start(bf16[128,896]{1,0:T(8,128)(2,1)S(1)} %constant_dynamic-update-slice_fusion.4), channel_id=1, source_target_pairs={{0,16},{8,24},{16,0},{24,8},{1,17},{9,25},{17,1},{25,9},{2,18},{10... | collective-permute-start | bytes 688136 | tf_op jit(solution)/shard_map/ppermute | solution.py:237
  67.1 13.9 %collective-permute-start.6 = (bf16[128,896]{1,0:T(8,128)(2,1)S(1)}, bf16[128,896]{1,0:T(8,128)(2,1)S(1)}, u32[]{:S(2)}, u32[]{:S(2)}) collective-permute-start(bf16[128,896]{1,0:T(8,128)(2,1)S(1)} %constant_dynamic-update-slice_fusion), channel_id=1, source_target_pairs={{0,1},{1,0},{2,3},{3,2},{4,5},{5,4},{6,7},{7,6},{8,9},{9,8},{10,11... | collective-permute-start | bytes 688136 | tf_op jit(solution)/shard_map/ppermute | solution.py:237
  81.0 15.0 %copy-start.2 = (bf16[256,896]{1,0:T(8,128)(2,1)}, bf16[256,896]{1,0:T(8,128)(2,1)S(1)}, u32[]{:S(2)}) copy-start(bf16[256,896]{1,0:T(8,128)(2,1)S(1)} %constant_dynamic-update-slice_fusion.8.refs_1_) | copy-start | bytes 1376260
  81.0 15.1 %collective-permute-start.8 = (bf16[256,896]{1,0:T(8,128)(2,1)S(1)}, bf16[256,896]{1,0:T(8,128)(2,1)S(1)}, u32[]{:S(2)}, u32[]{:S(2)}) collective-permute-start(bf16[256,896]{1,0:T(8,128)(2,1)S(1)} %constant_dynamic-update-slice_fusion.8.refs_1_), channel_id=1, source_target_pairs={{0,16},{8,24},{16,0},{24,8},{1,17},{9,25},{17,1},{25,9},{2,18},{10... | collective-permute-start | bytes 1376264 | tf_op jit(solution)/shard_map/ppermute | solution.py:237
  81.6 14.4 %collective-permute-start.9 = (bf16[128,896]{1,0:T(8,128)(2,1)S(1)}, bf16[128,896]{1,0:T(8,128)(2,1)S(1)}, u32[]{:S(2)}, u32[]{:S(2)}) collective-permute-start(bf16[128,896]{1,0:T(8,128)(2,1)S(1)} %constant_dynamic-update-slice_fusion.4), channel_id=1, source_target_pairs={{0,1},{1,0},{2,3},{3,2},{4,5},{5,4},{6,7},{7,6},{8,9},{9,8},{10,11... | collective-permute-start | bytes 688136 | tf_op jit(solution)/shard_map/ppermute | solution.py:237
  82.1 13.9 %collective-permute-start.10 = (bf16[128,896]{1,0:T(8,128)(2,1)S(1)}, bf16[128,896]{1,0:T(8,128)(2,1)S(1)}, u32[]{:S(2)}, u32[]{:S(2)}) collective-permute-start(bf16[128,896]{1,0:T(8,128)(2,1)S(1)} %collective-permute-done.7), channel_id=1, source_target_pairs={{0,1},{1,0},{2,3},{3,2},{4,5},{5,4},{6,7},{7,6},{8,9},{9,8},{10,11... | collective-permute-start | bytes 688136 | tf_op jit(solution)/shard_map/ppermute | solution.py:237
  83.7 13.6 %copy-start.8 = (bf16[2,256,8]{1,2,0:T(8,128)(2,1)S(1)}, bf16[2,256,8]{1,2,0:T(8,128)(2,1)}, u32[]{:S(2)}) copy-start(bf16[2,256,8]{1,2,0:T(8,128)(2,1)} %param.21) | copy-start | bytes 24580
  83.7 27.3 %collective-permute-start.11 = (bf16[256,896]{1,0:T(8,128)(2,1)S(1)}, bf16[256,896]{1,0:T(8,128)(2,1)S(1)}, u32[]{:S(2)}, u32[]{:S(2)}) collective-permute-start(bf16[256,896]{1,0:T(8,128)(2,1)S(1)} %constant_dynamic-update-slice_fusion.8.refs_1_), channel_id=1, source_target_pairs={{0,8},{8,0},{16,24},{24,16},{1,9},{9,1},{17,25},{25,17},{2,10},{10... | collective-permute-start | bytes 1376264 | tf_op jit(solution)/shard_map/ppermute | solution.py:237
  96.1 14.9 %copy-start.3 = (bf16[256,896]{1,0:T(8,128)(2,1)}, bf16[256,896]{1,0:T(8,128)(2,1)S(1)}, u32[]{:S(2)}) copy-start(bf16[256,896]{1,0:T(8,128)(2,1)S(1)} %collective-permute-done.8.refs_3_) | copy-start | bytes 1376260
  96.1 14.9 %copy-start.1 = (bf16[256,896]{1,0:T(8,128)(2,1)}, bf16[256,896]{1,0:T(8,128)(2,1)S(1)}, u32[]{:S(2)}) copy-start(bf16[256,896]{1,0:T(8,128)(2,1)S(1)} %constant_dynamic-update-slice_fusion.12.refs_4_) | copy-start | bytes 1376260
  96.2 14.9 %collective-permute-start.14 = (bf16[256,896]{1,0:T(8,128)(2,1)S(1)}, bf16[256,896]{1,0:T(8,128)(2,1)S(1)}, u32[]{:S(2)}, u32[]{:S(2)}) collective-permute-start(bf16[256,896]{1,0:T(8,128)(2,1)S(1)} %constant_dynamic-update-slice_fusion.12.refs_4_), channel_id=1, source_target_pairs={{0,8},{8,0},{16,24},{24,16},{1,9},{9,1},{17,25},{25,17},{2,10},{10... | collective-permute-start | bytes 1376264 | tf_op jit(solution)/shard_map/ppermute | solution.py:237
  96.7 14.3 %copy-start = (bf16[256,896]{1,0:T(8,128)(2,1)}, bf16[256,896]{1,0:T(8,128)(2,1)S(1)}, u32[]{:S(2)}) copy-start(bf16[256,896]{1,0:T(8,128)(2,1)S(1)} %constant_dynamic-update-slice_fusion.10.refs_2_) | copy-start | bytes 1376260
  96.7 14.3 %collective-permute-start.12 = (bf16[256,896]{1,0:T(8,128)(2,1)S(1)}, bf16[256,896]{1,0:T(8,128)(2,1)S(1)}, u32[]{:S(2)}, u32[]{:S(2)}) collective-permute-start(bf16[256,896]{1,0:T(8,128)(2,1)S(1)} %constant_dynamic-update-slice_fusion.10.refs_2_), channel_id=1, source_target_pairs={{0,8},{8,0},{16,24},{24,16},{1,9},{9,1},{17,25},{25,17},{2,10},{10... | collective-permute-start | bytes 1376264 | tf_op jit(solution)/shard_map/ppermute | solution.py:237
  96.8 14.3 %collective-permute-start.13 = (bf16[256,896]{1,0:T(8,128)(2,1)S(1)}, bf16[256,896]{1,0:T(8,128)(2,1)S(1)}, u32[]{:S(2)}, u32[]{:S(2)}) collective-permute-start(bf16[256,896]{1,0:T(8,128)(2,1)S(1)} %collective-permute-done.8.refs_3_), channel_id=1, source_target_pairs={{0,8},{8,0},{16,24},{24,16},{1,9},{9,1},{17,25},{25,17},{2,10},{10... | collective-permute-start | bytes 1376264 | tf_op jit(solution)/shard_map/ppermute | solution.py:237
  139.8 41.4 %collective-permute-start.16 = (bf16[256,896]{1,0:T(8,128)(2,1)}, bf16[256,896]{1,0:T(8,128)(2,1)S(1)}, u32[]{:S(2)}, u32[]{:S(2)}) collective-permute-start(bf16[256,896]{1,0:T(8,128)(2,1)} %produce.8), channel_id=1, source_target_pairs={{0,8},{8,0},{16,24},{24,16},{1,9},{9,1},{17,25},{25,17},{2,10},{10... | collective-permute-start | bytes 1376264 | tf_op jit(solution)/shard_map/ppermute | solution.py:237
  160.3 44.1 %collective-permute-start.22 = (bf16[256,896]{1,0:T(8,128)(2,1)}, bf16[256,896]{1,0:T(8,128)(2,1)S(1)}, u32[]{:S(2)}, u32[]{:S(2)}) collective-permute-start(bf16[256,896]{1,0:T(8,128)(2,1)} %produce.10), channel_id=1, source_target_pairs={{0,8},{8,0},{16,24},{24,16},{1,9},{9,1},{17,25},{25,17},{2,10},{10... | collective-permute-start | bytes 1376264 | tf_op jit(solution)/shard_map/ppermute | solution.py:237
  181.1 35.2 %collective-permute-start.15 = (bf16[256,896]{1,0:T(8,128)(2,1)}, bf16[256,896]{1,0:T(8,128)(2,1)S(1)}, u32[]{:S(2)}, u32[]{:S(2)}) collective-permute-start(bf16[256,896]{1,0:T(8,128)(2,1)} %produce.12), channel_id=1, source_target_pairs={{0,8},{8,0},{16,24},{24,16},{1,9},{9,1},{17,25},{25,17},{2,10},{10... | collective-permute-start | bytes 1376264 | tf_op jit(solution)/shard_map/ppermute | solution.py:237
  182.3 34.0 %collective-permute-start.17 = (bf16[256,896]{1,0:T(8,128)(2,1)S(1)}, bf16[256,896]{1,0:T(8,128)(2,1)S(1)}, u32[]{:S(2)}, u32[]{:S(2)}) collective-permute-start(bf16[256,896]{1,0:T(8,128)(2,1)S(1)} %add_convert_fusion.1), channel_id=1, source_target_pairs={{0,16},{8,24},{16,0},{24,8},{1,17},{9,25},{17,1},{25,9},{2,18},{10... | collective-permute-start | bytes 1376264 | tf_op jit(solution)/shard_map/ppermute | solution.py:237
  204.2 13.9 %collective-permute-start.21 = (bf16[256,896]{1,0:T(8,128)(2,1)}, bf16[256,896]{1,0:T(8,128)(2,1)S(1)}, u32[]{:S(2)}, u32[]{:S(2)}) collective-permute-start(bf16[256,896]{1,0:T(8,128)(2,1)} %produce.14), channel_id=1, source_target_pairs={{0,8},{8,0},{16,24},{24,16},{1,9},{9,1},{17,25},{25,17},{2,10},{10... | collective-permute-start | bytes 1376264 | tf_op jit(solution)/shard_map/ppermute | solution.py:237
  205.5 12.8 %collective-permute-start.23 = (bf16[256,896]{1,0:T(8,128)(2,1)S(1)}, bf16[256,896]{1,0:T(8,128)(2,1)S(1)}, u32[]{:S(2)}, u32[]{:S(2)}) collective-permute-start(bf16[256,896]{1,0:T(8,128)(2,1)S(1)} %add_convert_fusion), channel_id=1, source_target_pairs={{0,16},{8,24},{16,0},{24,8},{1,17},{9,25},{17,1},{25,9},{2,18},{10... | collective-permute-start | bytes 1376264 | tf_op jit(solution)/shard_map/ppermute | solution.py:237
  217.5 8.5 %collective-permute-start.18 = (bf16[128,896]{1,0:T(8,128)(2,1)S(1)}, bf16[128,896]{1,0:T(8,128)(2,1)S(1)}, u32[]{:S(2)}, u32[]{:S(2)}) collective-permute-start(bf16[128,896]{1,0:T(8,128)(2,1)S(1)} %slice.119), channel_id=1, source_target_pairs={{0,1},{1,0},{2,3},{3,2},{4,5},{5,4},{6,7},{7,6},{8,9},{9,8},{10,11... | collective-permute-start | bytes 688136 | tf_op jit(solution)/shard_map/ppermute | solution.py:237
  219.5 10.5 %collective-permute-start.24 = (bf16[128,896]{1,0:T(8,128)(2,1)S(1)}, bf16[128,896]{1,0:T(8,128)(2,1)S(1)}, u32[]{:S(2)}, u32[]{:S(2)}) collective-permute-start(bf16[128,896]{1,0:T(8,128)(2,1)S(1)} %slice.118), channel_id=1, source_target_pairs={{0,1},{1,0},{2,3},{3,2},{4,5},{5,4},{6,7},{7,6},{8,9},{9,8},{10,11... | collective-permute-start | bytes 688136 | tf_op jit(solution)/shard_map/ppermute | solution.py:237
  226.1 4.9 %collective-permute-start.19 = (bf16[64,896]{1,0:T(8,128)(2,1)S(1)}, bf16[64,896]{1,0:T(8,128)(2,1)S(1)}, u32[]{:S(2)}, u32[]{:S(2)}) collective-permute-start(bf16[64,896]{1,0:T(8,128)(2,1)S(1)} %slice.121), channel_id=1, source_target_pairs={{0,2},{1,3},{2,0},{3,1},{4,6},{5,7},{6,4},{7,5},{8,10},{9,11},{10,... | collective-permute-start | bytes 344072 | tf_op jit(solution)/shard_map/ppermute | solution.py:237
  230.1 5.0 %collective-permute-start.25 = (bf16[64,896]{1,0:T(8,128)(2,1)S(1)}, bf16[64,896]{1,0:T(8,128)(2,1)S(1)}, u32[]{:S(2)}, u32[]{:S(2)}) collective-permute-start(bf16[64,896]{1,0:T(8,128)(2,1)S(1)} %slice.120), channel_id=1, source_target_pairs={{0,2},{1,3},{2,0},{3,1},{4,6},{5,7},{6,4},{7,5},{8,10},{9,11},{10,... | collective-permute-start | bytes 344072 | tf_op jit(solution)/shard_map/ppermute | solution.py:237
  231.0 5.3 %collective-permute-start.20 = (bf16[32,896]{1,0:T(8,128)(2,1)S(1)}, bf16[32,896]{1,0:T(8,128)(2,1)S(1)}, u32[]{:S(2)}, u32[]{:S(2)}) collective-permute-start(bf16[32,896]{1,0:T(8,128)(2,1)S(1)} %slice.123), channel_id=1, source_target_pairs={{0,4},{1,5},{2,6},{3,7},{4,0},{5,1},{6,2},{7,3},{8,12},{9,13},{10,... | collective-permute-start | bytes 172040 | tf_op jit(solution)/shard_map/ppermute | solution.py:237
  235.1 5.4 %collective-permute-start.26 = (bf16[32,896]{1,0:T(8,128)(2,1)S(1)}, bf16[32,896]{1,0:T(8,128)(2,1)S(1)}, u32[]{:S(2)}, u32[]{:S(2)}) collective-permute-start(bf16[32,896]{1,0:T(8,128)(2,1)S(1)} %slice.122), channel_id=1, source_target_pairs={{0,4},{1,5},{2,6},{3,7},{4,0},{5,1},{6,2},{7,3},{8,12},{9,13},{10,... | collective-permute-start | bytes 172040 | tf_op jit(solution)/shard_map/ppermute | solution.py:237
  (4 other events, 3.5 us)

commit v2 on v1

--- a/solution.py
+++ b/solution.py
@@ -11,7 +11,6 @@
 HAD = 128
 LANES = 128
 ROWS = 16
-VMEM = 56 << 20
 ROUTED_SCALE = 2.5
 UNIT = 1.0 / math.sqrt(HAD)
 f32, bf16, i16, i32 = jnp.float32, jnp.bfloat16, jnp.int16, jnp.int32
@@ -76,7 +75,7 @@
     sections = 4
     group = tables.shape[2]
     share = groups // sections
-    cols = 256
+    cols = 512
 
     def body(section_ref, codes_ref, tables_ref, *rest):
         out = rest[-1]
@@ -114,7 +113,7 @@
         ),
         out_shape=jax.ShapeDtypeStruct((mats, groups * group, hidden), bf16),
         input_output_aliases=aliases,
-        compiler_params=pltpu.CompilerParams(vmem_limit_bytes=VMEM),
+        compiler_params=pltpu.CompilerParams(vmem_limit_bytes=56 << 20),
         name="decode_in",
     )(*operands)
 
@@ -171,63 +170,86 @@
             pltpu.VMEM((2, slots, hidden), f32),
             pltpu.VMEM((token_total, width), bf16),
         ],
-        compiler_params=pltpu.CompilerParams(vmem_limit_bytes=VMEM),
+        compiler_params=pltpu.CompilerParams(vmem_limit_bytes=32 << 20),
         name="project",
     )(pick, *pieces, weights, front, middle, had)
 
 
-def produce(section, codes, tables, folded, back, had, spread, order, chunk, chunks):
+def produce(section, codes, tables, folded, back, had, spread, order):
     _, books, groups, width = codes.shape
     sections = 4
     group = tables.shape[1]
     slots, hidden = folded.shape
     token_total = spread.shape[0]
-    steps = width // sections // chunks // LANES
+    cols = width // sections
+    tile = 2 * LANES
     pair = 2
 
     def body(section_ref, codes_ref, tables_ref, folded_ref, back_ref, had_ref, spread_ref, out):
-        outcome = None
-        for p in range(groups // ROWS // pair):
-            tiles = []
-            for g in range(p * pair, (p + 1) * pair):
-                tiles += decode_tile(
-                    lambda c: codes_ref[0, c, g * ROWS : (g + 1) * ROWS, :],
-                    lambda c, i, half: tables_ref[c, i, half],
-                    group,
-                )
-            depth = pair * group * ROWS
-            part = dot(folded_ref[:, p * depth : (p + 1) * depth], jnp.concatenate(tiles, 0))
-            outcome = part if outcome is None else outcome + part
-        high = outcome.astype(bf16)
-        left = outcome - high.astype(f32)
-        mid = left.astype(bf16)
-        low = (left - mid.astype(f32)).astype(bf16)
-        table = had_ref[...]
-        turned = (dot(high, table) + (dot(mid, table) + dot(low, table))) * UNIT
-        result = (back_ref[...] * turned).astype(bf16)
-        out[...] = dot(spread_ref[...], result).astype(bf16)
-
-    def column(j, s):
-        return (jnp.bitwise_xor(s[0], order) * chunks + chunk) * steps + j
+        def outcome_of(at, size):
+            outcome = None
+            for p in range(groups // ROWS // pair):
+                strips = []
+                for lane in range(at, at + size, LANES):
+                    tiles = []
+                    for g in range(p * pair, (p + 1) * pair):
+                        tiles += decode_tile(
+                            lambda c: codes_ref[0, c, g * ROWS : (g + 1) * ROWS, lane : lane + LANES],
+                            lambda c, i, half: tables_ref[c, i, half],
+                            group,
+                        )
+                    strips.append(jnp.concatenate(tiles, 0))
+                depth = pair * group * ROWS
+                part = dot(folded_ref[:, p * depth : (p + 1) * depth], jnp.concatenate(strips, 1))
+                outcome = part if outcome is None else outcome + part
+            return outcome
+
+        def finish(outcome, at, size):
+            high = outcome.astype(bf16)
+            left = outcome - high.astype(f32)
+            mid = left.astype(bf16)
+            low = (left - mid.astype(f32)).astype(bf16)
+            table = had_ref[...]
+            turned = []
+            for b in range(0, size, HAD):
+                s = slice(b, b + HAD)
+                turned.append(dot(high[:, s], table) + (dot(mid[:, s], table) + dot(low[:, s], table)))
+            turned = jnp.concatenate(turned, 1) * UNIT
+            result = (back_ref[:, at : at + size] * turned).astype(bf16)
+            out[:, at : at + size] = dot(spread_ref[...], result).astype(bf16)
+
+        pending = None
+        at = 0
+        while at < cols:
+            size = min(tile, cols - at)
+            outcome = outcome_of(at, size)
+            if pending is not None:
+                finish(*pending)
+            pending = (outcome, at, size)
+            at += size
+        finish(*pending)
+
+    def column(s):
+        return jnp.bitwise_xor(s[0], order)
 
     whole = lambda shape: pl.BlockSpec(shape, lambda j, s: (0,) * len(shape))
     return pl.pallas_call(
         body,
         grid_spec=pltpu.PrefetchScalarGridSpec(
             num_scalar_prefetch=1,
-            grid=(steps,),
+            grid=(1,),
             in_specs=[
-                pl.BlockSpec((1, books, groups, LANES), lambda j, s: (0, 0, 0, column(j, s))),
+                pl.BlockSpec((1, books, groups, cols), lambda j, s: (0, 0, 0, column(s))),
                 whole(tables.shape),
                 whole(folded.shape),
-                pl.BlockSpec((1, LANES), lambda j, s: (0, column(j, s))),
+                pl.BlockSpec((1, cols), lambda j, s: (0, column(s))),
                 whole(had.shape),
                 whole(spread.shape),
             ],
-            out_specs=pl.BlockSpec((token_total, LANES), lambda j, s: (0, j)),
+            out_specs=pl.BlockSpec((token_total, cols), lambda j, s: (0, j)),
         ),
-        out_shape=jax.ShapeDtypeStruct((token_total, steps * LANES), bf16),
-        compiler_params=pltpu.CompilerParams(vmem_limit_bytes=VMEM),
+        out_shape=jax.ShapeDtypeStruct((token_total, cols), bf16),
+        compiler_params=pltpu.CompilerParams(vmem_limit_bytes=20 << 20),
         name="produce",
     )(section, codes, tables, folded, back, had, spread)
 
@@ -268,27 +290,7 @@
     places = [0, 2, 1, 3]
 
     gates = (ROUTED_SCALE * scores / jnp.sum(scores, axis=1, keepdims=True)).astype(bf16)
-    facts = jnp.concatenate([routes.astype(f32), gates.astype(f32)], 1)
-    facts = lax.all_gather(facts, "dev", axis=0)
-    source = jnp.bitwise_xor(jnp.asarray(relative, i32), device.astype(i32))
-    facts = jnp.take(facts, source, axis=0).reshape(token_total, -1)
     top = routes.shape[1]
-    expert = ((section - 1) * devices + device).astype(f32)
-    named = facts[:, :top] == expert
-    hit = jnp.any(named, axis=1)
-    gate = jnp.sum(jnp.where(named, facts[:, top:], 0.0), axis=1)
-    earlier = (jnp.arange(token_total)[:, None] < jnp.arange(token_total)[None, :]).astype(f32)
-    slot = jnp.sum(jnp.where(hit[:, None], earlier, 0.0), axis=0)
-    slot = jnp.where(hit, slot, -1.0)
-    shared = section == 0
-    token_id = jnp.arange(token_total)
-    own = token_id < token_count
-    slot = jnp.where(shared, jnp.where(own, token_id.astype(f32), -1.0), slot)
-    gate = jnp.where(shared, 1.0, gate)
-    slot_id = jnp.arange(slots).astype(f32)
-    pick = (slot_id[:, None] == slot[None, :]).astype(bf16)
-    spread = jnp.where(slot[:, None] == slot_id[None, :], gate[:, None], 0.0).astype(bf16)
-
     tables_in = book_tables(gate_up_books)
     tables_down = book_tables(down_books)
     sylvester = hadamard_table(HAD)
@@ -303,19 +305,22 @@
     def fence(*values):
         return lax.optimization_barrier(values)
 
-    first, second = tokens[:, :half], tokens[:, half:]
-    gathered = []
-    for part in (first, second):
-        gathered.append([part] + [swap(part, "dev", b) for b in relative[1 : devices // 2]])
+    facts = jnp.concatenate([routes.astype(bf16), gates], 1)
+    facts = jnp.pad(facts, ((0, 0), (0, LANES - 2 * top)))
+    row = jnp.concatenate([tokens, facts], 1)
+    gathered = [row] + [swap(row, "dev", b) for b in relative[1 : devices // 2]]
     weights = decode_in(section_word, gate_up_codes, tables_in, None, places[0], 0)
     weights, gathered = fence(weights, gathered)
-    first, second = [jnp.concatenate(g, 0) for g in gathered]
+    gathered = jnp.concatenate(gathered, 0)
+    first = jnp.concatenate([gathered[:, :half], gathered[:, quarter:]], 1)
+    second = gathered[:, half:quarter]
     first_near = swap(first, "dev", 1)
     second_cross = swap(second, "sec", 2)
     weights, first, second = fence(weights, first, second)
     weights = decode_in(section_word, gate_up_codes, tables_in, weights, places[1], 1)
     weights, first_near, second_cross = fence(weights, first_near, second_cross)
     first = jnp.concatenate([first, first_near], 0)
+    first, facts = first[:, :half], first[:, half:].astype(f32)
     first_cross = swap(first, "sec", 2)
     second_near = swap(second, "dev", 1)
     second_both = swap(second_cross, "dev", 1)
@@ -329,19 +334,47 @@
     pieces = pieces + [swap(p, "sec", 1) for p in pieces]
     weights = decode_in(section_word, gate_up_codes, tables_in, weights, places[3], 3)
 
+    expert = ((section - 1) * devices + device).astype(f32)
+    named = facts[:, :top] == expert
+    hit = jnp.any(named, axis=1)
+    gate = jnp.sum(jnp.where(named, facts[:, top : 2 * top], 0.0), axis=1)
+    earlier = (jnp.arange(token_total)[:, None] < jnp.arange(token_total)[None, :]).astype(f32)
+    slot = jnp.sum(jnp.where(hit[:, None], earlier, 0.0), axis=0)
+    slot = jnp.where(hit, slot, -1.0)
+    shared = section == 0
+    token_id = jnp.arange(token_total)
+    own = token_id < token_count
+    slot = jnp.where(shared, jnp.where(own, token_id.astype(f32), -1.0), slot)
+    gate = jnp.where(shared, 1.0, gate)
+    slot_id = jnp.arange(slots).astype(f32)
+    pick = (slot_id[:, None] == slot[None, :]).astype(bf16)
+    spread = jnp.where(slot[:, None] == slot_id[None, :], gate[:, None], 0.0).astype(bf16)
+
+
     folded = project(pick, pieces, weights, front, middle, had_coded)
 
-    made = {}
-    for order, chunk in ((3, 0), (2, 0), (3, 1), (2, 1), (1, 0), (0, 0), (1, 1), (0, 1)):
-        made[order, chunk] = produce(
-            section_word, down_codes, tables_down, folded, back, had, spread, order, chunk, chunks
-        )
-        folded, made[order, chunk] = fence(folded, made[order, chunk])
+    def make(order):
+        return produce(section_word, down_codes, tables_down, folded, back, had, spread, order)
+
+    def cut(values):
+        return [values[:, c * half : (c + 1) * half] for c in range(chunks)]
+
+    given = make(3)
+    folded, given = fence(folded, given)
+    near = swap(given, "sec", 1)
+    kept = make(2)
+    folded, kept, near = fence(folded, kept, near)
+    crossing = cut((kept.astype(f32) + near.astype(f32)).astype(bf16))
+    folded, *crossing = fence(folded, *crossing)
+    crossed = [swap(c, "sec", 2) for c in crossing]
+    given = make(1)
+    folded, given, crossed[0] = fence(folded, given, crossed[0])
+    near = swap(given, "sec", 1)
+    kept = make(0)
+    kept, near = fence(kept, near)
     outs = []
-    for chunk in range(chunks):
-        crossing = made[2, chunk].astype(f32) + swap(made[3, chunk], "sec", 1).astype(f32)
-        crossed = swap(crossing.astype(bf16), "sec", 2).astype(f32)
-        total = made[0, chunk].astype(f32) + swap(made[1, chunk], "sec", 1).astype(f32) + crossed
+    for own, beside, across in zip(cut(kept), cut(near), crossed):
+        total = own.astype(f32) + beside.astype(f32) + across.astype(f32)
         for stride in strides:
             rows = total.shape[0] // 2
             sent = swap(total[rows:].astype(bf16), "dev", stride)

time: 243 us -> 155 us (0.64)
  Pallas kernels: 147 us -> 85.7 us
  blocking collectives: 30.5 us -> 0 us
  waiting for transfers between devices: 16.5 us -> 26 us
  other arithmetic: 14.8 us -> 9.52 us
    pallas_call x8 -> x4, Pallas kernels: 81.4 us -> 22.8 us  [produce(): pl.pallas_call(body, grid_spec=pltpu.PrefetchScalarGridSpec(num_scalar_pr...]
    all_gather x1 -> x0, blocking collectives: 30.5 us -> none  [per_device(): facts = lax.all_gather(facts, 'dev', axis=0)]
    ppermute x27 -> x22, waiting for transfers between devices: 16.5 us -> 26 us  [swap(): return lax.ppermute(values, axis, [(i, i ^ stride) for i in range(size)])]
    unnamed x27 -> x29, local copies, waits for them, and re-layouts: 1.92 us -> 4.61 us
    convert_element_type x4, other arithmetic: 3.64 us -> 1.03 us  [the longest x1 0.69 us: per_device(): facts = jnp.concatenate([routes.astype(bf16), gates], 1)]
    ppermute x27 -> x22, starting transfers between devices: 25.7 us -> 24.2 us  [swap(): return lax.ppermute(values, axis, [(i, i ^ stride) for i in range(size)])]
  transfers between devices with their start and end apart: 27 -> 22, of which waited for: 6 -> 8; matrix products, arithmetic and copies ran while one was open for 7% -> 7% of each run, Pallas kernels for 50% -> 42%
where the time goes in v2:
time: 155 us; the launch traced here: 154 us
  Pallas kernels  85.7 us (55%)
  waiting for transfers between devices  26 us (17%)
  starting transfers between devices  24.2 us (16%)
  other arithmetic  9.52 us (6%)
  local copies, waits for them, and re-layouts  8.61 us (6%)
    pallas_call x4, Pallas kernels, decode_in(): pl.pallas_call(body, grid_spec=pltpu.PrefetchScalarGridSpec(num_scalar_pr...  47.6 us
    ppermute x22, waiting for transfers between devices, swap(): return lax.ppermute(values, axis, [(i, i ^ stride) for i in range(size)])  26 us
    ppermute x22, starting transfers between devices, swap(): return lax.ppermute(values, axis, [(i, i ^ stride) for i in range(size)])  24.2 us
    pallas_call x4, Pallas kernels, produce(): pl.pallas_call(body, grid_spec=pltpu.PrefetchScalarGridSpec(num_scalar_pr...  22.8 us
    pallas_call x1, Pallas kernels, project(): pl.pallas_call(body, grid=(steps,), in_specs=[whole(pick.shape)] + [whole...  15.3 us
    unnamed x29, local copies, waits for them, and re-layouts  4.61 us
  transfers between devices with their start and end apart: 22, of which 8 were waited for; matrix products, arithmetic and copies ran while one was open for 7% of the time, Pallas kernels for 42%

profile of v2, /device:TPU:0, one launch (start us, length us, event | category | flops | bytes accessed | tf_op | source)
XLA Modules:
  0.0 154.5 jit_solution(15951155595011795641)
XLA Ops:
  0.0 0.8 copy.32
  2.4 0.9 pad_maximum_fusion.1
  3.3 4.1 %collective-permute-start = (bf16[32,1920]{1,0:T(8,128)(2,1)S(1)}, bf16[32,1920]{1,0:T(8,128)(2,1)S(1)}, u32[]{:S(2)}, u32[]{:S(2)}) collective-permute-start(bf16[32,1920]{1,0:T(8,128)(2,1)S(1)} %pad_maximum_fusion.1), channel_id=1, source_target_pairs={{0,4},{1,5},{2,6},{3,7},{4,0},{5,1},{6,2},{7,3},{8,12},{9,13},{10,... | collective-permute-start | bytes 368648 | tf_op jit(solution)/shard_map/ppermute | solution.py:259
  7.4 1.6 %collective-permute-start.1 = (bf16[32,1920]{1,0:T(8,128)(2,1)S(1)}, bf16[32,1920]{1,0:T(8,128)(2,1)S(1)}, u32[]{:S(2)}, u32[]{:S(2)}) collective-permute-start(bf16[32,1920]{1,0:T(8,128)(2,1)S(1)} %pad_maximum_fusion.1), channel_id=1, source_target_pairs={{0,2},{1,3},{2,0},{3,1},{4,6},{5,7},{6,4},{7,5},{8,10},{9,11},{10,... | collective-permute-start | bytes 368648 | tf_op jit(solution)/shard_map/ppermute | solution.py:259
  9.0 0.9 convert_reduce_fusion
  9.9 1.5 convert_bitcast_fusion.back_ref
  14.3 0.7 broadcast_in_dim.80.tables_ref
  15.0 11.9 %decode_in.4.rest_0_ = bf16[2,7168,1024]{2,1,0:T(8,128)(2,1)} custom-call(s32[1]{0:T(128)} %bitcast.section_ref, s32[1,2,2,896,1024]{4,3,2,1,0:T(8,128)} %codes_ref.11, bf16[2,2,8,2,16,128]{5,4,3,2,1,0:T(8,128)(2,1)} %broadcast_in_dim.80.tables_ref), custom_call_target="tpu_custom_call" | custom-call | tf_op jit(solution)/shard_map/decode_in/pallas_call | solution.py:106
  27.7 1.8 %collective-permute-start.3 = (bf16[128,1024]{1,0:T(8,128)(2,1)S(1)}, bf16[128,1024]{1,0:T(8,128)(2,1)S(1)}, u32[]{:S(2)}, u32[]{:S(2)}) collective-permute-start(bf16[128,1024]{1,0:T(8,128)(2,1)S(1)} %pad_maximum_fusion), channel_id=1, source_target_pairs={{0,1},{1,0},{2,3},{3,2},{4,5},{5,4},{6,7},{7,6},{8,9},{9,8},{10,11... | collective-permute-start | bytes 786440 | tf_op jit(solution)/shard_map/ppermute | solution.py:259
  30.1 1.5 collective-permute-start.4
  31.6 11.8 %decode_in.5.rest_0_ = bf16[2,7168,1024]{2,1,0:T(8,128)(2,1)} custom-call(s32[1]{0:T(128)} %bitcast.section_ref, s32[1,2,2,896,1024]{4,3,2,1,0:T(8,128)} %codes_ref.11, bf16[2,2,8,2,16,128]{5,4,3,2,1,0:T(8,128)(2,1)} %broadcast_in_dim.80.tables_ref, bf16[2,7168,1024]{2,1,0:T(8,128)(2,1)} %decode_in.4.rest_0_), custom_call_target="tpu_custom_call", output_to_operand_aliasing={{}: (3, {})} | custom-call | tf_op jit(solution)/shard_map/decode_in/pallas_call | solution.py:106
  44.5 1.8 %collective-permute-start.7 = (bf16[128,896]{1,0:T(8,128)(2,1)S(1)}, bf16[128,896]{1,0:T(8,128)(2,1)S(1)}, u32[]{:S(2)}, u32[]{:S(2)}) collective-permute-start(bf16[128,896]{1,0:T(8,128)(2,1)S(1)} %collective-permute-done.4), channel_id=1, source_target_pairs={{0,1},{1,0},{2,3},{3,2},{4,5},{5,4},{6,7},{7,6},{8,9},{9,8},{10,11... | collective-permute-start | bytes 688136 | tf_op jit(solution)/shard_map/ppermute | solution.py:259
  47.5 11.8 %decode_in.6.rest_0_ = bf16[2,7168,1024]{2,1,0:T(8,128)(2,1)} custom-call(s32[1]{0:T(128)} %bitcast.section_ref, s32[1,2,2,896,1024]{4,3,2,1,0:T(8,128)} %codes_ref.11, bf16[2,2,8,2,16,128]{5,4,3,2,1,0:T(8,128)(2,1)} %broadcast_in_dim.80.tables_ref, bf16[2,7168,1024]{2,1,0:T(8,128)(2,1)} %decode_in.5.rest_0_), custom_call_target="tpu_custom_call", output_to_operand_aliasing={{}: (3, {})} | custom-call | tf_op jit(solution)/shard_map/decode_in/pallas_call | solution.py:106
  61.8 12.0 %decode_in.7.refs_9_ = bf16[2,7168,1024]{2,1,0:T(8,128)(2,1)} custom-call(s32[1]{0:T(128)} %bitcast.section_ref, s32[1,2,2,896,1024]{4,3,2,1,0:T(8,128)} %codes_ref.11, bf16[2,2,8,2,16,128]{5,4,3,2,1,0:T(8,128)(2,1)} %broadcast_in_dim.80.tables_ref, bf16[2,7168,1024]{2,1,0:T(8,128)(2,1)} %decode_in.6.rest_0_), custom_call_target="tpu_custom_call", output_to_operand_aliasing={{}: (3, {})} | custom-call | tf_op jit(solution)/shard_map/decode_in/pallas_call | solution.py:106
  73.8 0.8 copy-done.2
  75.4 0.8 copy-done.4
  76.8 15.3 %project.1.folded_ref = bf16[128,1024]{1,0:T(8,128)(2,1)S(1)} custom-call(bf16[128,256]{1,0:T(8,128)(2,1)S(1)} %copy-done.2, bf16[256,896]{1,0:T(8,128)(2,1)S(1)} %slice.121.refs_1_, bf16[256,896]{1,0:T(8,128)(2,1)S(1)} %constant_dynamic-update-slice_fusion.6.refs_2_, bf16[256,896]{1,0:T(8,128)(2,1)} %collective-permute-done.5.refs_3_, ...), custom_call_target="tpu_custom_call" | custom-call | tf_op jit(solution)/shard_map/project/pallas_call | solution.py:156
  92.2 5.7 %produce.4 = bf16[256,1792]{1,0:T(8,128)(2,1)S(1)} custom-call(s32[1]{0:T(128)} %bitcast.section_ref, s32[1,2,128,7168]{3,2,1,0:T(8,128)S(1)} %bitcast.10, bf16[2,8,2,16,128]{4,3,2,1,0:T(8,128)(2,1)S(1)} %broadcast_in_dim.77.tables_ref, bf16[128,1024]{1,0:T(8,128)(2,1)S(1)} %project.1.folded_ref, f32[1,7168]{1,0:T(1,128)S(1)} %copy-done, ...), custom_call_target="tpu_custom_call" | custom-call | tf_op jit(solution)/shard_map/produce/pallas_call | solution.py:236
  98.2 5.7 %produce.5 = bf16[256,1792]{1,0:T(8,128)(2,1)S(1)} custom-call(s32[1]{0:T(128)} %bitcast.section_ref, s32[1,2,128,7168]{3,2,1,0:T(8,128)S(1)} %bitcast.10, bf16[2,8,2,16,128]{4,3,2,1,0:T(8,128)(2,1)S(1)} %broadcast_in_dim.77.tables_ref, bf16[128,1024]{1,0:T(8,128)(2,1)S(1)} %project.1.folded_ref, f32[1,7168]{1,0:T(1,128)S(1)} %copy-done, ...), custom_call_target="tpu_custom_call" | custom-call | tf_op jit(solution)/shard_map/produce/pallas_call | solution.py:236
  104.2 1.6 %collective-permute-start.13 = (bf16[256,896]{1,0:T(8,128)(2,1)S(1)}, bf16[256,896]{1,0:T(8,128)(2,1)S(1)}, u32[]{:S(2)}, u32[]{:S(2)}) collective-permute-start(bf16[256,896]{1,0:T(8,128)(2,1)S(1)} %get-tuple-element.54), channel_id=1, source_target_pairs={{0,16},{8,24},{16,0},{24,8},{1,17},{9,25},{17,1},{25,9},{2,18},{10... | collective-permute-start | bytes 1376264 | tf_op jit(solution)/shard_map/ppermute | solution.py:259
  105.8 5.9 %produce.6 = bf16[256,1792]{1,0:T(8,128)(2,1)S(1)} custom-call(s32[1]{0:T(128)} %bitcast.section_ref, s32[1,2,128,7168]{3,2,1,0:T(8,128)S(1)} %bitcast.10, bf16[2,8,2,16,128]{4,3,2,1,0:T(8,128)(2,1)S(1)} %broadcast_in_dim.77.tables_ref, bf16[128,1024]{1,0:T(8,128)(2,1)S(1)} %project.1.folded_ref, f32[1,7168]{1,0:T(1,128)S(1)} %copy-done, ...), custom_call_target="tpu_custom_call" | custom-call | tf_op jit(solution)/shard_map/produce/pallas_call | solution.py:236
  111.7 5.3 %collective-permute-done.13 = bf16[256,896]{1,0:T(8,128)(2,1)S(1)} collective-permute-done((bf16[256,896]{1,0:T(8,128)(2,1)S(1)}, bf16[256,896]{1,0:T(8,128)(2,1)S(1)}, u32[]{:S(2)}, u32[]{:S(2)}) %collective-permute-start.13) | collective-permute-done | bytes 458784 | tf_op jit(solution)/shard_map/ppermute | solution.py:259
  117.0 1.5 collective-permute-start.18
  118.5 5.6 %produce.7 = bf16[256,1792]{1,0:T(8,128)(2,1)S(1)} custom-call(s32[1]{0:T(128)} %bitcast.section_ref, s32[1,2,128,7168]{3,2,1,0:T(8,128)S(1)} %bitcast.10, bf16[2,8,2,16,128]{4,3,2,1,0:T(8,128)(2,1)S(1)} %broadcast_in_dim.77.tables_ref, bf16[128,1024]{1,0:T(8,128)(2,1)S(1)} %project.1.folded_ref, f32[1,7168]{1,0:T(1,128)S(1)} %copy-done, ...), custom_call_target="tpu_custom_call" | custom-call | tf_op jit(solution)/shard_map/produce/pallas_call | solution.py:236
  124.1 5.8 %collective-permute-done.18 = bf16[256,896]{1,0:T(8,128)(2,1)S(1)} collective-permute-done((bf16[256,896]{1,0:T(8,128)(2,1)S(1)}, bf16[256,896]{1,0:T(8,128)(2,1)S(1)}, u32[]{:S(2)}, u32[]{:S(2)}) %collective-permute-start.18) | collective-permute-done | bytes 458784 | tf_op jit(solution)/shard_map/ppermute | solution.py:259
  130.7 1.8 %collective-permute-start.19 = (bf16[128,896]{1,0:T(8,128)(2,1)S(1)}, bf16[128,896]{1,0:T(8,128)(2,1)S(1)}, u32[]{:S(2)}, u32[]{:S(2)}) collective-permute-start(bf16[128,896]{1,0:T(8,128)(2,1)S(1)} %slice.164), channel_id=1, source_target_pairs={{0,1},{1,0},{2,3},{3,2},{4,5},{5,4},{6,7},{7,6},{8,9},{9,8},{10,11... | collective-permute-start | bytes 688136 | tf_op jit(solution)/shard_map/ppermute | solution.py:259
  132.4 6.4 %collective-permute-done.15 = bf16[128,896]{1,0:T(8,128)(2,1)S(1)} collective-permute-done((bf16[128,896]{1,0:T(8,128)(2,1)S(1)}, bf16[128,896]{1,0:T(8,128)(2,1)S(1)}, u32[]{:S(2)}, u32[]{:S(2)}) %collective-permute-start.15) | collective-permute-done | bytes 229408 | tf_op jit(solution)/shard_map/ppermute | solution.py:259
  139.6 2.8 %collective-permute-done.19 = bf16[128,896]{1,0:T(8,128)(2,1)S(1)} collective-permute-done((bf16[128,896]{1,0:T(8,128)(2,1)S(1)}, bf16[128,896]{1,0:T(8,128)(2,1)S(1)}, u32[]{:S(2)}, u32[]{:S(2)}) %collective-permute-start.19) | collective-permute-done | bytes 229408 | tf_op jit(solution)/shard_map/ppermute | solution.py:259
  143.8 3.1 %collective-permute-start.17 = (bf16[32,896]{1,0:T(8,128)(2,1)S(1)}, bf16[32,896]{1,0:T(8,128)(2,1)S(1)}, u32[]{:S(2)}, u32[]{:S(2)}) collective-permute-start(bf16[32,896]{1,0:T(8,128)(2,1)S(1)} %slice.169), channel_id=1, source_target_pairs={{0,4},{1,5},{2,6},{3,7},{4,0},{5,1},{6,2},{7,3},{8,12},{9,13},{10,... | collective-permute-start | bytes 172040 | tf_op jit(solution)/shard_map/ppermute | solution.py:259
  146.9 1.1 collective-permute-done.20
  148.1 1.6 %collective-permute-start.21 = (bf16[32,896]{1,0:T(8,128)(2,1)S(1)}, bf16[32,896]{1,0:T(8,128)(2,1)S(1)}, u32[]{:S(2)}, u32[]{:S(2)}) collective-permute-start(bf16[32,896]{1,0:T(8,128)(2,1)S(1)} %slice.168), channel_id=1, source_target_pairs={{0,4},{1,5},{2,6},{3,7},{4,0},{5,1},{6,2},{7,3},{8,12},{9,13},{10,... | collective-permute-start | bytes 172040 | tf_op jit(solution)/shard_map/ppermute | solution.py:259
  150.0 3.9 %collective-permute-done.21 = bf16[32,896]{1,0:T(8,128)(2,1)S(1)} collective-permute-done((bf16[32,896]{1,0:T(8,128)(2,1)S(1)}, bf16[32,896]{1,0:T(8,128)(2,1)S(1)}, u32[]{:S(2)}, u32[]{:S(2)}) %collective-permute-start.21) | collective-permute-done | bytes 57376 | tf_op jit(solution)/shard_map/ppermute | solution.py:259
  (105 shorter events, 16.4 us)
Async XLA Ops:
  3.3 24.2 %collective-permute-start = (bf16[32,1920]{1,0:T(8,128)(2,1)S(1)}, bf16[32,1920]{1,0:T(8,128)(2,1)S(1)}, u32[]{:S(2)}, u32[]{:S(2)}) collective-permute-start(bf16[32,1920]{1,0:T(8,128)(2,1)S(1)} %pad_maximum_fusion.1), channel_id=1, source_target_pairs={{0,4},{1,5},{2,6},{3,7},{4,0},{5,1},{6,2},{7,3},{8,12},{9,13},{10,... | collective-permute-start | bytes 368648 | tf_op jit(solution)/shard_map/ppermute | solution.py:259
  7.4 20.1 %collective-permute-start.1 = (bf16[32,1920]{1,0:T(8,128)(2,1)S(1)}, bf16[32,1920]{1,0:T(8,128)(2,1)S(1)}, u32[]{:S(2)}, u32[]{:S(2)}) collective-permute-start(bf16[32,1920]{1,0:T(8,128)(2,1)S(1)} %pad_maximum_fusion.1), channel_id=1, source_target_pairs={{0,2},{1,3},{2,0},{3,1},{4,6},{5,7},{6,4},{7,5},{8,10},{9,11},{10,... | collective-permute-start | bytes 368648 | tf_op jit(solution)/shard_map/ppermute | solution.py:259
  9.0 18.6 %collective-permute-start.2 = (bf16[32,1920]{1,0:T(8,128)(2,1)S(1)}, bf16[32,1920]{1,0:T(8,128)(2,1)S(1)}, u32[]{:S(2)}, u32[]{:S(2)}) collective-permute-start(bf16[32,1920]{1,0:T(8,128)(2,1)S(1)} %pad_maximum_fusion.1), channel_id=1, source_target_pairs={{0,6},{1,7},{2,4},{3,5},{4,2},{5,3},{6,0},{7,1},{8,14},{9,15},{10,... | collective-permute-start | bytes 368648 | tf_op jit(solution)/shard_map/ppermute | solution.py:259
  15.0 11.9 %copy-start.8 = (s32[1,1024]{1,0:T(1,128)S(1)}, s32[1,1024]{1,0:T(1,128)}, u32[]{:S(2)}) copy-start(s32[1,1024]{1,0:T(1,128)} %param.18) | copy-start | bytes 12292
  15.0 14.5 %copy-start.7 = (bf16[2,256,8]{1,2,0:T(8,128)(2,1)S(1)}, bf16[2,256,8]{1,2,0:T(8,128)(2,1)}, u32[]{:S(2)}) copy-start(bf16[2,256,8]{1,2,0:T(8,128)(2,1)} %param.20) | copy-start | bytes 24580
  27.7 16.3 %collective-permute-start.3 = (bf16[128,1024]{1,0:T(8,128)(2,1)S(1)}, bf16[128,1024]{1,0:T(8,128)(2,1)S(1)}, u32[]{:S(2)}, u32[]{:S(2)}) collective-permute-start(bf16[128,1024]{1,0:T(8,128)(2,1)S(1)} %pad_maximum_fusion), channel_id=1, source_target_pairs={{0,1},{1,0},{2,3},{3,2},{4,5},{5,4},{6,7},{7,6},{8,9},{9,8},{10,11... | collective-permute-start | bytes 786440 | tf_op jit(solution)/shard_map/ppermute | solution.py:259
  30.1 13.9 %collective-permute-start.4 = (bf16[128,896]{1,0:T(8,128)(2,1)S(1)}, bf16[128,896]{1,0:T(8,128)(2,1)S(1)}, u32[]{:S(2)}, u32[]{:S(2)}) collective-permute-start(bf16[128,896]{1,0:T(8,128)(2,1)S(1)} %get-tuple-element.41), channel_id=1, source_target_pairs={{0,16},{8,24},{16,0},{24,8},{1,17},{9,25},{17,1},{25,9},{2,18},{10... | collective-permute-start | bytes 688136 | tf_op jit(solution)/shard_map/ppermute | solution.py:259
  43.5 15.8 %collective-permute-start.6 = (bf16[128,896]{1,0:T(8,128)(2,1)S(1)}, bf16[128,896]{1,0:T(8,128)(2,1)S(1)}, u32[]{:S(2)}, u32[]{:S(2)}) collective-permute-start(bf16[128,896]{1,0:T(8,128)(2,1)S(1)} %get-tuple-element.41), channel_id=1, source_target_pairs={{0,1},{1,0},{2,3},{3,2},{4,5},{5,4},{6,7},{7,6},{8,9},{9,8},{10,11... | collective-permute-start | bytes 688136 | tf_op jit(solution)/shard_map/ppermute | solution.py:259
  44.1 15.2 %collective-permute-start.5 = (bf16[256,896]{1,0:T(8,128)(2,1)S(1)}, bf16[256,896]{1,0:T(8,128)(2,1)}, u32[]{:S(2)}, u32[]{:S(2)}) collective-permute-start(bf16[256,896]{1,0:T(8,128)(2,1)S(1)} %slice.121.refs_1_), channel_id=1, source_target_pairs={{0,16},{8,24},{16,0},{24,8},{1,17},{9,25},{17,1},{25,9},{2,18},{10... | collective-permute-start | bytes 1376264 | tf_op jit(solution)/shard_map/ppermute | solution.py:259
  44.5 29.2 %collective-permute-start.8 = (bf16[256,896]{1,0:T(8,128)(2,1)S(1)}, bf16[256,896]{1,0:T(8,128)(2,1)}, u32[]{:S(2)}, u32[]{:S(2)}) collective-permute-start(bf16[256,896]{1,0:T(8,128)(2,1)S(1)} %slice.121.refs_1_), channel_id=1, source_target_pairs={{0,8},{8,0},{16,24},{24,16},{1,9},{9,1},{17,25},{25,17},{2,10},{10... | collective-permute-start | bytes 1376264 | tf_op jit(solution)/shard_map/ppermute | solution.py:259
  44.5 14.8 %collective-permute-start.7 = (bf16[128,896]{1,0:T(8,128)(2,1)S(1)}, bf16[128,896]{1,0:T(8,128)(2,1)S(1)}, u32[]{:S(2)}, u32[]{:S(2)}) collective-permute-start(bf16[128,896]{1,0:T(8,128)(2,1)S(1)} %collective-permute-done.4), channel_id=1, source_target_pairs={{0,1},{1,0},{2,3},{3,2},{4,5},{5,4},{6,7},{7,6},{8,9},{9,8},{10,11... | collective-permute-start | bytes 688136 | tf_op jit(solution)/shard_map/ppermute | solution.py:259
  60.0 13.7 %collective-permute-start.11 = (bf16[256,896]{1,0:T(8,128)(2,1)}, bf16[256,896]{1,0:T(8,128)(2,1)}, u32[]{:S(2)}, u32[]{:S(2)}) collective-permute-start(bf16[256,896]{1,0:T(8,128)(2,1)} %constant_dynamic-update-slice_fusion.8.refs_4_), channel_id=1, source_target_pairs={{0,8},{8,0},{16,24},{24,16},{1,9},{9,1},{17,25},{25,17},{2,10},{10... | collective-permute-start | bytes 1376264 | tf_op jit(solution)/shard_map/ppermute | solution.py:259
  60.3 13.5 %collective-permute-start.9 = (bf16[256,896]{1,0:T(8,128)(2,1)S(1)}, bf16[256,896]{1,0:T(8,128)(2,1)}, u32[]{:S(2)}, u32[]{:S(2)}) collective-permute-start(bf16[256,896]{1,0:T(8,128)(2,1)S(1)} %constant_dynamic-update-slice_fusion.6.refs_2_), channel_id=1, source_target_pairs={{0,8},{8,0},{16,24},{24,16},{1,9},{9,1},{17,25},{25,17},{2,10},{10... | collective-permute-start | bytes 1376264 | tf_op jit(solution)/shard_map/ppermute | solution.py:259
  60.7 13.1 %collective-permute-start.10 = (bf16[256,896]{1,0:T(8,128)(2,1)}, bf16[256,896]{1,0:T(8,128)(2,1)}, u32[]{:S(2)}, u32[]{:S(2)}) collective-permute-start(bf16[256,896]{1,0:T(8,128)(2,1)} %collective-permute-done.5.refs_3_), channel_id=1, source_target_pairs={{0,8},{8,0},{16,24},{24,16},{1,9},{9,1},{17,25},{25,17},{2,10},{10... | collective-permute-start | bytes 1376264 | tf_op jit(solution)/shard_map/ppermute | solution.py:259
  61.6 30.6 %slice-start = ((s8[7340032]{0:T(1024)(128)(4,1)}), s8[4194304]{0:T(1024)(128)(4,1)S(1)}, s32[]{:S(2)}) async-start(s8[7340032]{0:T(1024)(128)(4,1)} %bitcast.9), calls=%async_computation | async-start | bytes 8388608
  61.7 30.4 %slice-start.1 = ((s8[7340032]{0:T(1024)(128)(4,1)}), s8[3145728]{0:T(1024)(128)(4,1)S(1)}, s32[]{:S(2)}) async-start(s8[7340032]{0:T(1024)(128)(4,1)} %bitcast.9), calls=%async_computation.1 | async-start | bytes 6291456
  73.7 18.5 %copy-start = (f32[1,7168]{1,0:T(1,128)S(1)}, f32[1,7168]{1,0:T(1,128)}, u32[]{:S(2)}) copy-start(f32[1,7168]{1,0:T(1,128)} %convert_bitcast_fusion.back_ref) | copy-start | bytes 86020
  73.7 18.5 %copy-start.1 = (bf16[128,128]{1,0:T(8,128)(2,1)S(1)}, bf16[128,128]{1,0:T(8,128)(2,1)}, u32[]{:S(2)}) copy-start(bf16[128,128]{1,0:T(8,128)(2,1)} %constant.59.clone.had_ref) | copy-start | bytes 98308
  73.8 0.8 copy-start.2
  74.6 0.7 copy-start.3
  75.4 0.8 copy-start.4
  76.8 15.3 %copy-start.6 = (bf16[2,8,2,128]{3,2,1,0:T(2,128)(2,1)S(1)}, bf16[2,8,2,128]{3,2,1,0:T(2,128)(2,1)}, u32[]{:S(2)}) copy-start(bf16[2,8,2,128]{3,2,1,0:T(2,128)(2,1)} %copy.30) | copy-start | bytes 24580
  97.9 6.0 %collective-permute-start.12 = (bf16[256,1792]{1,0:T(8,128)(2,1)S(1)}, bf16[256,1792]{1,0:T(8,128)(2,1)S(1)}, u32[]{:S(2)}, u32[]{:S(2)}) collective-permute-start(bf16[256,1792]{1,0:T(8,128)(2,1)S(1)} %produce.4), channel_id=1, source_target_pairs={{0,8},{8,0},{16,24},{24,16},{1,9},{9,1},{17,25},{25,17},{2,10},{10... | collective-permute-start | bytes 2752520 | tf_op jit(solution)/shard_map/ppermute | solution.py:259
  104.2 12.7 %collective-permute-start.13 = (bf16[256,896]{1,0:T(8,128)(2,1)S(1)}, bf16[256,896]{1,0:T(8,128)(2,1)S(1)}, u32[]{:S(2)}, u32[]{:S(2)}) collective-permute-start(bf16[256,896]{1,0:T(8,128)(2,1)S(1)} %get-tuple-element.54), channel_id=1, source_target_pairs={{0,16},{8,24},{16,0},{24,8},{1,17},{9,25},{17,1},{25,9},{2,18},{10... | collective-permute-start | bytes 1376264 | tf_op jit(solution)/shard_map/ppermute | solution.py:259
  117.0 7.2 %collective-permute-start.14 = (bf16[256,1792]{1,0:T(8,128)(2,1)S(1)}, bf16[256,1792]{1,0:T(8,128)(2,1)S(1)}, u32[]{:S(2)}, u32[]{:S(2)}) collective-permute-start(bf16[256,1792]{1,0:T(8,128)(2,1)S(1)} %produce.6), channel_id=1, source_target_pairs={{0,8},{8,0},{16,24},{24,16},{1,9},{9,1},{17,25},{25,17},{2,10},{10... | collective-permute-start | bytes 2752520 | tf_op jit(solution)/shard_map/ppermute | solution.py:259
  117.0 12.9 %collective-permute-start.18 = (bf16[256,896]{1,0:T(8,128)(2,1)S(1)}, bf16[256,896]{1,0:T(8,128)(2,1)S(1)}, u32[]{:S(2)}, u32[]{:S(2)}) collective-permute-start(bf16[256,896]{1,0:T(8,128)(2,1)S(1)} %get-tuple-element.60), channel_id=1, source_target_pairs={{0,16},{8,24},{16,0},{24,8},{1,17},{9,25},{17,1},{25,9},{2,18},{10... | collective-permute-start | bytes 1376264 | tf_op jit(solution)/shard_map/ppermute | solution.py:259
  130.3 8.6 %collective-permute-start.15 = (bf16[128,896]{1,0:T(8,128)(2,1)S(1)}, bf16[128,896]{1,0:T(8,128)(2,1)S(1)}, u32[]{:S(2)}, u32[]{:S(2)}) collective-permute-start(bf16[128,896]{1,0:T(8,128)(2,1)S(1)} %slice.165), channel_id=1, source_target_pairs={{0,1},{1,0},{2,3},{3,2},{4,5},{5,4},{6,7},{7,6},{8,9},{9,8},{10,11... | collective-permute-start | bytes 688136 | tf_op jit(solution)/shard_map/ppermute | solution.py:259
  130.7 11.8 %collective-permute-start.19 = (bf16[128,896]{1,0:T(8,128)(2,1)S(1)}, bf16[128,896]{1,0:T(8,128)(2,1)S(1)}, u32[]{:S(2)}, u32[]{:S(2)}) collective-permute-start(bf16[128,896]{1,0:T(8,128)(2,1)S(1)} %slice.164), channel_id=1, source_target_pairs={{0,1},{1,0},{2,3},{3,2},{4,5},{5,4},{6,7},{7,6},{8,9},{9,8},{10,11... | collective-permute-start | bytes 688136 | tf_op jit(solution)/shard_map/ppermute | solution.py:259
  138.9 4.9 %collective-permute-start.16 = (bf16[64,896]{1,0:T(8,128)(2,1)S(1)}, bf16[64,896]{1,0:T(8,128)(2,1)S(1)}, u32[]{:S(2)}, u32[]{:S(2)}) collective-permute-start(bf16[64,896]{1,0:T(8,128)(2,1)S(1)} %slice.167), channel_id=1, source_target_pairs={{0,2},{1,3},{2,0},{3,1},{4,6},{5,7},{6,4},{7,5},{8,10},{9,11},{10,... | collective-permute-start | bytes 344072 | tf_op jit(solution)/shard_map/ppermute | solution.py:259
  142.6 5.5 %collective-permute-start.20 = (bf16[64,896]{1,0:T(8,128)(2,1)S(1)}, bf16[64,896]{1,0:T(8,128)(2,1)S(1)}, u32[]{:S(2)}, u32[]{:S(2)}) collective-permute-start(bf16[64,896]{1,0:T(8,128)(2,1)S(1)} %slice.166), channel_id=1, source_target_pairs={{0,2},{1,3},{2,0},{3,1},{4,6},{5,7},{6,4},{7,5},{8,10},{9,11},{10,... | collective-permute-start | bytes 344072 | tf_op jit(solution)/shard_map/ppermute | solution.py:259
  143.8 6.1 %collective-permute-start.17 = (bf16[32,896]{1,0:T(8,128)(2,1)S(1)}, bf16[32,896]{1,0:T(8,128)(2,1)S(1)}, u32[]{:S(2)}, u32[]{:S(2)}) collective-permute-start(bf16[32,896]{1,0:T(8,128)(2,1)S(1)} %slice.169), channel_id=1, source_target_pairs={{0,4},{1,5},{2,6},{3,7},{4,0},{5,1},{6,2},{7,3},{8,12},{9,13},{10,... | collective-permute-start | bytes 172040 | tf_op jit(solution)/shard_map/ppermute | solution.py:259
  148.1 5.8 %collective-permute-start.21 = (bf16[32,896]{1,0:T(8,128)(2,1)S(1)}, bf16[32,896]{1,0:T(8,128)(2,1)S(1)}, u32[]{:S(2)}, u32[]{:S(2)}) collective-permute-start(bf16[32,896]{1,0:T(8,128)(2,1)S(1)} %slice.168), channel_id=1, source_target_pairs={{0,4},{1,5},{2,6},{3,7},{4,0},{5,1},{6,2},{7,3},{8,12},{9,13},{10,... | collective-permute-start | bytes 172040 | tf_op jit(solution)/shard_map/ppermute | solution.py:259
  (1 other events, 0.7 us)

commit v3 on v2

--- a/solution.py
+++ b/solution.py
@@ -111,9 +111,9 @@
             in_specs=in_specs,
             out_specs=pl.BlockSpec((1, share * group, cols), lambda m, h, s: (m, place, h)),
         ),
-        out_shape=jax.ShapeDtypeStruct((mats, groups * group, hidden), bf16),
+        out_shape=jax.ShapeDtypeStruct((mats, (sections - 1) * share * group, hidden), bf16),
         input_output_aliases=aliases,
-        compiler_params=pltpu.CompilerParams(vmem_limit_bytes=56 << 20),
+        compiler_params=pltpu.CompilerParams(vmem_limit_bytes=50 << 20),
         name="decode_in",
     )(*operands)
 
@@ -125,57 +125,91 @@
     return jnp.concatenate(parts, 1)
 
 
-def project(pick, pieces, weights, front, middle, had):
+def project(section, codes, tables, weights, pick, pieces, signs, middle, had, order, places):
+    _, mats, books, groups, hidden = codes.shape
+    sections = len(places)
+    group = tables.shape[2]
+    share = groups // sections
     slots, token_total = pick.shape
-    steps = len(pieces)
     width = pieces[0].shape[1]
-    hidden = weights.shape[2]
+    chunks = len(pieces) // sections
+    stored = weights.shape[1]
+    cols = 512
+    per_mat = hidden // cols
+    pair = 2
 
     def body(*refs):
-        pick_ref, *piece_refs = refs[: 1 + steps]
-        weights_ref, front_ref, middle_ref, had_ref, out, total, picked = refs[1 + steps :]
-        step = pl.program_id(0)
-        for at in range(steps):
-
-            @pl.when(step == at)
-            def _():
-                picked[...] = piece_refs[at][...]
-
-        rows = dot(pick_ref[...], picked[...]).astype(bf16) * front_ref[0]
-        turned = rotate(rows, had_ref[...])
-        for m in range(2):
-            part = dot(turned, weights_ref[m])
-            total[m] = jnp.where(step == 0, part, total[m] + part)
-
-        @pl.when(step == steps - 1)
+        section_ref, codes_ref, tables_ref, weights_ref, pick_ref = refs[:5]
+        piece_refs = refs[5 : 5 + len(pieces)]
+        signs_ref, middle_ref, had_ref, out, turned, total = refs[5 + len(pieces) :]
+        step = pl.program_id(0) * per_mat + pl.program_id(1)
+
+        @pl.when(step == 0)
         def _():
-            acted = (jax.nn.silu(total[0]) * total[1]).astype(bf16)
-            out[...] = rotate(acted * middle_ref[...], had_ref[...])
-
-    whole = lambda shape: pl.BlockSpec(shape, lambda s: (0,) * len(shape))
+            for at, piece in enumerate(piece_refs):
+                quarter = jnp.bitwise_xor(section_ref[0], places[at // chunks])
+                start = pl.multiple_of((quarter * chunks + at % chunks) * width, LANES)
+                front = (2 * signs_ref[0, 0:1, pl.ds(start, width)] - 1).astype(bf16)
+                rows = dot(pick_ref[...], piece[...]).astype(bf16) * front
+                turned[:, at * width : (at + 1) * width] = rotate(rows, had_ref[...])
+
+        part = dot(turned[:, :stored], weights_ref[0])
+        depth = pair * group * ROWS
+        for p in range(share // ROWS // pair):
+            strips = []
+            for lane in range(0, cols, LANES):
+                tiles = []
+                for g in range(p * pair, (p + 1) * pair):
+                    tiles += decode_tile(
+                        lambda c: codes_ref[
+                            0, 0, c, g * ROWS : (g + 1) * ROWS, lane : lane + LANES
+                        ],
+                        lambda c, i, half: tables_ref[0, c, i, half],
+                        group,
+                    )
+                strips.append(jnp.concatenate(tiles, 0))
+            at = stored + p * depth
+            part = part + dot(turned[:, at : at + depth], jnp.concatenate(strips, 1))
+        total[step] = part
+
+        @pl.when(step == mats * per_mat - 1)
+        def _():
+            for h in range(per_mat):
+                lanes = slice(h * cols, (h + 1) * cols)
+                acted = (jax.nn.silu(total[h]) * total[per_mat + h]).astype(bf16)
+                flips = (2 * middle_ref[:, lanes] - 1).astype(bf16)
+                out[:, lanes] = rotate(acted * flips, had_ref[...])
+
+    whole = lambda shape: pl.BlockSpec(shape, lambda m, h, s: (0,) * len(shape))
     return pl.pallas_call(
         body,
-        grid=(steps,),
-        in_specs=[whole(pick.shape)]
-        + [whole(p.shape) for p in pieces]
-        + [
-            pl.BlockSpec((2, width, hidden), lambda s: (0, s, 0)),
-            pl.BlockSpec((1, 1, width), lambda s: (s, 0, 0)),
-            whole(middle.shape),
-            whole(had.shape),
-        ],
-        out_specs=whole((slots, hidden)),
+        grid_spec=pltpu.PrefetchScalarGridSpec(
+            num_scalar_prefetch=1,
+            grid=(mats, per_mat),
+            in_specs=[
+                pl.BlockSpec(
+                    (1, 1, books, share, cols),
+                    lambda m, h, s: (0, m, 0, jnp.bitwise_xor(s[0], order), h),
+                ),
+                pl.BlockSpec((1,) + tables.shape[1:], lambda m, h, s: (m, 0, 0, 0, 0, 0)),
+                pl.BlockSpec((1, stored, cols), lambda m, h, s: (m, 0, h)),
+                whole(pick.shape),
+            ]
+            + [whole(p.shape) for p in pieces]
+            + [whole(signs.shape), whole(middle.shape), whole(had.shape)],
+            out_specs=whole((slots, hidden)),
+            scratch_shapes=[
+                pltpu.VMEM((slots, groups * group), bf16),
+                pltpu.VMEM((mats * per_mat, slots, cols), f32),
+            ],
+        ),
         out_shape=jax.ShapeDtypeStruct((slots, hidden), bf16),
-        scratch_shapes=[
-            pltpu.VMEM((2, slots, hidden), f32),
-            pltpu.VMEM((token_total, width), bf16),
-        ],
-        compiler_params=pltpu.CompilerParams(vmem_limit_bytes=32 << 20),
+        compiler_params=pltpu.CompilerParams(vmem_limit_bytes=50 << 20),
         name="project",
-    )(pick, *pieces, weights, front, middle, had)
-
-
-def produce(section, codes, tables, folded, back, had, spread, order):
+    )(section, codes, tables, weights, pick, *pieces, signs, middle, had)
+
+
+def produce(section, codes, tables, folded, signs, had, spread, order, added, dtype):
     _, books, groups, width = codes.shape
     sections = 4
     group = tables.shape[1]
@@ -185,7 +219,12 @@
     tile = 2 * LANES
     pair = 2
 
-    def body(section_ref, codes_ref, tables_ref, folded_ref, back_ref, had_ref, spread_ref, out):
+    extra = [] if added is None else [added]
+
+    def body(section_ref, codes_ref, tables_ref, folded_ref, signs_ref, had_ref, spread_ref, *rest):
+        outs = rest[-2:]
+        back = (2 * signs_ref[0, 1:2, :] - 1).astype(f32)
+
         def outcome_of(at, size):
             outcome = None
             for p in range(groups // ROWS // pair):
@@ -215,8 +254,17 @@
                 s = slice(b, b + HAD)
                 turned.append(dot(high[:, s], table) + (dot(mid[:, s], table) + dot(low[:, s], table)))
             turned = jnp.concatenate(turned, 1) * UNIT
-            result = (back_ref[:, at : at + size] * turned).astype(bf16)
-            out[:, at : at + size] = dot(spread_ref[...], result).astype(bf16)
+            result = (back[:, at : at + size] * turned).astype(bf16)
+            weighted = dot(spread_ref[...], result)
+            if extra:
+                weighted = weighted + rest[0][:, at : at + size].astype(f32)
+            for side in range(2):
+                low, high = max(at, side * cols // 2), min(at + size, (side + 1) * cols // 2)
+                if low < high:
+                    shift = side * cols // 2
+                    outs[side][:, low - shift : high - shift] = weighted[
+                        :, low - at : high - at
+                    ].astype(dtype)
 
         pending = None
         at = 0
@@ -242,16 +290,17 @@
                 pl.BlockSpec((1, books, groups, cols), lambda j, s: (0, 0, 0, column(s))),
                 whole(tables.shape),
                 whole(folded.shape),
-                pl.BlockSpec((1, cols), lambda j, s: (0, column(s))),
+                pl.BlockSpec((1, 2, cols), lambda j, s: (0, 0, column(s))),
                 whole(had.shape),
                 whole(spread.shape),
-            ],
-            out_specs=pl.BlockSpec((token_total, cols), lambda j, s: (0, j)),
+            ]
+            + [whole(e.shape) for e in extra],
+            out_specs=[whole((token_total, cols // 2))] * 2,
         ),
-        out_shape=jax.ShapeDtypeStruct((token_total, cols), bf16),
+        out_shape=[jax.ShapeDtypeStruct((token_total, cols // 2), dtype)] * 2,
         compiler_params=pltpu.CompilerParams(vmem_limit_bytes=20 << 20),
         name="produce",
-    )(section, codes, tables, folded, back, had, spread)
+    )(section, codes, tables, folded, signs, had, spread, *extra)
 
 
 def swap(values, axis, stride):
@@ -296,11 +345,6 @@
     sylvester = hadamard_table(HAD)
     had_coded = jnp.asarray(sylvester[:, coded_order(group)], bf16)
     had = jnp.asarray(sylvester, bf16)
-    front = (2 * model_signs[0, 0] - 1).astype(bf16).reshape(sections, chunks, 1, half)
-    front = jnp.take(front, jnp.bitwise_xor(jnp.asarray(places, i32), section.astype(i32)), axis=0)
-    front = front.reshape(sections * chunks, 1, half)
-    back = (2 * model_signs[0, 1] - 1).astype(f32).reshape(1, width)
-    middle = (2 * hidden_signs - 1).astype(bf16)
 
     def fence(*values):
         return lax.optimization_barrier(values)
@@ -309,22 +353,20 @@
     facts = jnp.pad(facts, ((0, 0), (0, LANES - 2 * top)))
     row = jnp.concatenate([tokens, facts], 1)
     gathered = [row] + [swap(row, "dev", b) for b in relative[1 : devices // 2]]
-    weights = decode_in(section_word, gate_up_codes, tables_in, None, places[0], 0)
-    weights, gathered = fence(weights, gathered)
     gathered = jnp.concatenate(gathered, 0)
     first = jnp.concatenate([gathered[:, :half], gathered[:, quarter:]], 1)
     second = gathered[:, half:quarter]
+    section_word, first, second = fence(section_word, first, second)
     first_near = swap(first, "dev", 1)
     second_cross = swap(second, "sec", 2)
-    weights, first, second = fence(weights, first, second)
-    weights = decode_in(section_word, gate_up_codes, tables_in, weights, places[1], 1)
+    weights = decode_in(section_word, gate_up_codes, tables_in, None, places[0], 0)
     weights, first_near, second_cross = fence(weights, first_near, second_cross)
     first = jnp.concatenate([first, first_near], 0)
     first, facts = first[:, :half], first[:, half:].astype(f32)
     first_cross = swap(first, "sec", 2)
     second_near = swap(second, "dev", 1)
     second_both = swap(second_cross, "dev", 1)
-    weights = decode_in(section_word, gate_up_codes, tables_in, weights, places[2], 2)
+    weights = decode_in(section_word, gate_up_codes, tables_in, weights, places[1], 1)
     weights, first_cross, second_near, second_both = fence(
         weights, first_cross, second_near, second_both
     )
@@ -332,7 +374,7 @@
     second_cross = jnp.concatenate([second_cross, second_both], 0)
     pieces = [first, second, first_cross, second_cross]
     pieces = pieces + [swap(p, "sec", 1) for p in pieces]
-    weights = decode_in(section_word, gate_up_codes, tables_in, weights, places[3], 3)
+    weights = decode_in(section_word, gate_up_codes, tables_in, weights, places[2], 2)
 
     expert = ((section - 1) * devices + device).astype(f32)
     named = facts[:, :top] == expert
@@ -351,31 +393,57 @@
     spread = jnp.where(slot[:, None] == slot_id[None, :], gate[:, None], 0.0).astype(bf16)
 
 
-    folded = project(pick, pieces, weights, front, middle, had_coded)
-
-    def make(order):
-        return produce(section_word, down_codes, tables_down, folded, back, had, spread, order)
-
-    def cut(values):
-        return [values[:, c * half : (c + 1) * half] for c in range(chunks)]
-
-    given = make(3)
-    folded, given = fence(folded, given)
-    near = swap(given, "sec", 1)
-    kept = make(2)
-    folded, kept, near = fence(folded, kept, near)
-    crossing = cut((kept.astype(f32) + near.astype(f32)).astype(bf16))
-    folded, *crossing = fence(folded, *crossing)
-    crossed = [swap(c, "sec", 2) for c in crossing]
-    given = make(1)
-    folded, given, crossed[0] = fence(folded, given, crossed[0])
-    near = swap(given, "sec", 1)
-    kept = make(0)
-    kept, near = fence(kept, near)
+    folded = project(
+        section_word,
+        gate_up_codes,
+        tables_in,
+        weights,
+        pick,
+        pieces,
+        model_signs,
+        hidden_signs,
+        had_coded,
+        places[3],
+        places,
+    )
+
+    def make(order, added=None, dtype=bf16):
+        return produce(
+            section_word,
+            down_codes,
+            tables_down,
+            folded,
+            model_signs,
+            had,
+            spread,
+            order,
+            added,
+            dtype,
+        )
+
+    rows = token_total // 2
+    far_made = jnp.concatenate(make(3), 1)
+    folded, far_made = fence(folded, far_made)
+    far_near = swap(far_made, "sec", 1)
+    beside = jnp.concatenate(make(1), 1)
+    folded, beside, far_near = fence(folded, beside, far_near)
+    beside = swap(beside, "sec", 1)
+    across = make(2, far_near)
+    folded, beside, *across = fence(folded, beside, *across)
+    first_across = swap(across[0], "sec", 2)
+    second_met = swap(across[1][rows:], "dev", 1)
+    first, second = make(0, beside, f32)
+    first, second, second_met = fence(first, second, second_met)
+    second_across = (across[1][:rows].astype(f32) + second_met.astype(f32)).astype(bf16)
+    second_across = swap(second_across, "sec", 2)
+    second_near = swap(second[rows:].astype(bf16), "dev", 1)
+    first = first + first_across.astype(f32)
+    first_near = swap(first[rows:].astype(bf16), "dev", 1)
+    first = first[:rows] + first_near.astype(f32)
+    second = second[:rows] + second_near.astype(f32) + second_across.astype(f32)
     outs = []
-    for own, beside, across in zip(cut(kept), cut(near), crossed):
-        total = own.astype(f32) + beside.astype(f32) + across.astype(f32)
-        for stride in strides:
+    for total in (first, second):
+        for stride in strides[1:]:
             rows = total.shape[0] // 2
             sent = swap(total[rows:].astype(bf16), "dev", stride)
             total = total[:rows] + sent.astype(f32)

time: 155 us -> 132 us (0.85)
  Pallas kernels: 85.7 us -> 75.2 us
  local copies, waits for them, and re-layouts: 8.61 us -> 2.08 us
  waiting for transfers between devices: 26 us -> 19.9 us
  starting transfers between devices: 24.2 us -> 28.5 us
  other arithmetic: 9.52 us -> 5.25 us
    pallas_call x4 -> x3, Pallas kernels: 47.6 us -> 35.9 us  [decode_in(): pl.pallas_call(body, grid_spec=pltpu.PrefetchScalarGridSpec(num_scalar_pr...]
    ppermute x22 -> x23, waiting for transfers between devices: 26 us -> 19.9 us  [swap(): return lax.ppermute(values, axis, [(i, i ^ stride) for i in range(size)])]
    ppermute x22 -> x23, starting transfers between devices: 24.2 us -> 28.5 us  [swap(): return lax.ppermute(values, axis, [(i, i ^ stride) for i in range(size)])]
    convert_element_type x4 -> x1, other arithmetic: 3.23 us -> 0.06 us  [per_device(): (across[1][:rows].astype(f32) + second_met.astype(f32)).astype(bf16)]
    unnamed x29 -> x24, local copies, waits for them, and re-layouts: 4.61 us -> 1.65 us
    broadcast_in_dim x4, local copies, waits for them, and re-layouts: 2.09 us -> 0.08 us  [book_tables(): return jnp.broadcast_to(turned, lead + (group, halves, ROWS, LANES))]
  transfers between devices with their start and end apart: 22 -> 23, of which waited for: 8 -> 8; matrix products, arithmetic and copies ran while one was open for 7% -> 1% of each run, Pallas kernels for 42% -> 40%
where the time goes in v3:
time: 132 us; the launch traced here: 131 us
  Pallas kernels  75.2 us (57%)
  starting transfers between devices  28.5 us (22%)
  waiting for transfers between devices  19.9 us (15%)
  other arithmetic  5.25 us (4%)
  local copies, waits for them, and re-layouts  2.08 us (2%)
    pallas_call x3, Pallas kernels, decode_in(): pl.pallas_call(body, grid_spec=pltpu.PrefetchScalarGridSpec(num_scalar_pr...  35.9 us
    ppermute x23, starting transfers between devices, swap(): return lax.ppermute(values, axis, [(i, i ^ stride) for i in range(size)])  28.5 us
    pallas_call x4, Pallas kernels, produce(): pl.pallas_call(body, grid_spec=pltpu.PrefetchScalarGridSpec(num_scalar_pr...  22.9 us
    ppermute x23, waiting for transfers between devices, swap(): return lax.ppermute(values, axis, [(i, i ^ stride) for i in range(size)])  19.9 us
    pallas_call x1, Pallas kernels, project(): pl.pallas_call(body, grid_spec=pltpu.PrefetchScalarGridSpec(num_scalar_pr...  16.4 us
  transfers between devices with their start and end apart: 23, of which 8 were waited for; matrix products, arithmetic and copies ran while one was open for 1% of the time, Pallas kernels for 40%

profile of v3, /device:TPU:0, one launch (start us, length us, event | category | flops | bytes accessed | tf_op | source)
XLA Modules:
  0.0 131.4 jit_solution(14422292621089026642)
XLA Ops:
  0.0 0.8 copy.22
  0.8 0.7 reduce_sum.27
  2.4 0.9 pad_maximum_fusion.4
  3.4 4.1 %collective-permute-start = (bf16[32,1920]{1,0:T(8,128)(2,1)S(1)}, bf16[32,1920]{1,0:T(8,128)(2,1)S(1)}, u32[]{:S(2)}, u32[]{:S(2)}) collective-permute-start(bf16[32,1920]{1,0:T(8,128)(2,1)S(1)} %pad_maximum_fusion.4), channel_id=1, source_target_pairs={{0,4},{1,5},{2,6},{3,7},{4,0},{5,1},{6,2},{7,3},{8,12},{9,13},{10,... | collective-permute-start | bytes 368648 | tf_op jit(solution)/shard_map/ppermute | solution.py:308
  7.5 1.6 %collective-permute-start.1 = (bf16[32,1920]{1,0:T(8,128)(2,1)S(1)}, bf16[32,1920]{1,0:T(8,128)(2,1)S(1)}, u32[]{:S(2)}, u32[]{:S(2)}) collective-permute-start(bf16[32,1920]{1,0:T(8,128)(2,1)S(1)} %pad_maximum_fusion.4), channel_id=1, source_target_pairs={{0,2},{1,3},{2,0},{3,1},{4,6},{5,7},{6,4},{7,5},{8,10},{9,11},{10,... | collective-permute-start | bytes 368648 | tf_op jit(solution)/shard_map/ppermute | solution.py:308
  9.1 6.0 %collective-permute-done = bf16[32,1920]{1,0:T(8,128)(2,1)S(1)} collective-permute-done((bf16[32,1920]{1,0:T(8,128)(2,1)S(1)}, bf16[32,1920]{1,0:T(8,128)(2,1)S(1)}, u32[]{:S(2)}, u32[]{:S(2)}) %collective-permute-start) | collective-permute-done | bytes 122912 | tf_op jit(solution)/shard_map/ppermute | solution.py:308
  15.1 2.1 %collective-permute-done.2 = bf16[32,1920]{1,0:T(8,128)(2,1)S(1)} collective-permute-done((bf16[32,1920]{1,0:T(8,128)(2,1)S(1)}, bf16[32,1920]{1,0:T(8,128)(2,1)S(1)}, u32[]{:S(2)}, u32[]{:S(2)}) %collective-permute-start.2) | collective-permute-done | bytes 122912 | tf_op jit(solution)/shard_map/ppermute | solution.py:308
  17.2 0.9 pad_maximum_fusion.2
  18.3 1.6 %collective-permute-start.3 = (bf16[128,1024]{1,0:T(8,128)(2,1)S(1)}, bf16[128,1024]{1,0:T(8,128)(2,1)S(1)}, u32[]{:S(2)}, u32[]{:S(2)}) collective-permute-start(bf16[128,1024]{1,0:T(8,128)(2,1)S(1)} %fusion.8), channel_id=1, source_target_pairs={{0,1},{1,0},{2,3},{3,2},{4,5},{5,4},{6,7},{7,6},{8,9},{9,8},{10,11... | collective-permute-start | bytes 786440 | tf_op jit(solution)/shard_map/ppermute | solution.py:308
  19.9 1.6 %collective-permute-start.4 = (bf16[128,896]{1,0:T(8,128)(2,1)S(1)}, bf16[128,896]{1,0:T(8,128)(2,1)S(1)}, u32[]{:S(2)}, u32[]{:S(2)}) collective-permute-start(bf16[128,896]{1,0:T(8,128)(2,1)S(1)} %pad_maximum_fusion.3), channel_id=1, source_target_pairs={{0,16},{8,24},{16,0},{24,8},{1,17},{9,25},{17,1},{25,9},{2,18},{10... | collective-permute-start | bytes 688136 | tf_op jit(solution)/shard_map/ppermute | solution.py:308
  22.0 11.8 %decode_in.3.rest_0_ = bf16[2,5376,1024]{2,1,0:T(8,128)(2,1)} custom-call(s32[1]{0:T(128)} %bitcast.section_ref.refs_0_, s32[1,2,2,896,1024]{4,3,2,1,0:T(8,128)} %refs_1_.1, bf16[2,2,8,2,16,128]{5,4,3,2,1,0:T(8,128)(2,1)S(1)} %broadcast_in_dim.63.tables_ref.refs_2_), custom_call_target="tpu_custom_call" | custom-call | tf_op jit(solution)/shard_map/decode_in/pallas_call | solution.py:106
  34.6 1.5 %collective-permute-start.7 = (bf16[128,896]{1,0:T(8,128)(2,1)S(1)}, bf16[128,896]{1,0:T(8,128)(2,1)S(1)}, u32[]{:S(2)}, u32[]{:S(2)}) collective-permute-start(bf16[128,896]{1,0:T(8,128)(2,1)S(1)} %collective-permute-done.4), channel_id=1, source_target_pairs={{0,1},{1,0},{2,3},{3,2},{4,5},{5,4},{6,7},{7,6},{8,9},{9,8},{10,11... | collective-permute-start | bytes 688136 | tf_op jit(solution)/shard_map/ppermute | solution.py:308
  36.6 12.0 %decode_in.4.rest_0_ = bf16[2,5376,1024]{2,1,0:T(8,128)(2,1)} custom-call(s32[1]{0:T(128)} %bitcast.section_ref.refs_0_, s32[1,2,2,896,1024]{4,3,2,1,0:T(8,128)} %refs_1_.1, bf16[2,2,8,2,16,128]{5,4,3,2,1,0:T(8,128)(2,1)S(1)} %broadcast_in_dim.63.tables_ref.refs_2_, bf16[2,5376,1024]{2,1,0:T(8,128)(2,1)} %decode_in.3.rest_0_), custom_call_target="tpu_custom_call", output_to_operand_aliasing={{}: (3, {})} | custom-call | tf_op jit(solution)/shard_map/decode_in/pallas_call | solution.py:106
  49.9 12.0 %decode_in.5.refs_3_ = bf16[2,5376,1024]{2,1,0:T(8,128)(2,1)} custom-call(s32[1]{0:T(128)} %bitcast.section_ref.refs_0_, s32[1,2,2,896,1024]{4,3,2,1,0:T(8,128)} %refs_1_.1, bf16[2,2,8,2,16,128]{5,4,3,2,1,0:T(8,128)(2,1)S(1)} %broadcast_in_dim.63.tables_ref.refs_2_, bf16[2,5376,1024]{2,1,0:T(8,128)(2,1)} %decode_in.4.rest_0_), custom_call_target="tpu_custom_call", output_to_operand_aliasing={{}: (3, {})} | custom-call | tf_op jit(solution)/shard_map/decode_in/pallas_call | solution.py:106
  61.9 0.7 copy-done.5
  62.7 16.4 %project.1.folded_ref = bf16[128,1024]{1,0:T(8,128)(2,1)S(1)} custom-call(s32[1]{0:T(128)} %bitcast.section_ref.refs_0_, s32[1,2,2,896,1024]{4,3,2,1,0:T(8,128)} %refs_1_.1, bf16[2,2,8,2,16,128]{5,4,3,2,1,0:T(8,128)(2,1)S(1)} %broadcast_in_dim.63.tables_ref.refs_2_, bf16[2,5376,1024]{2,1,0:T(8,128)(2,1)} %decode_in.5.refs_3_, ...), custom_call_target="tpu_custom_call" | custom-call | tf_op jit(solution)/shard_map/project/pallas_call | solution.py:184
  79.2 5.7 %produce.4 = (bf16[256,896]{1,0:T(8,128)(2,1)S(1)}, bf16[256,896]{1,0:T(8,128)(2,1)S(1)}) custom-call(s32[1]{0:T(128)} %bitcast.section_ref.refs_0_, s32[1,2,128,7168]{3,2,1,0:T(8,128)S(1)} %bitcast.8, bf16[2,8,2,16,128]{4,3,2,1,0:T(8,128)(2,1)S(1)} %broadcast_in_dim.61.tables_ref, bf16[128,1024]{1,0:T(8,128)(2,1)S(1)} %project.1.folded_ref, ...), custom_call_target="tpu_custom_call" | custom-call | tf_op jit(solution)/shard_map/produce/pallas_call | solution.py:284
  85.2 5.7 %produce.5 = (bf16[256,896]{1,0:T(8,128)(2,1)S(1)}, bf16[256,896]{1,0:T(8,128)(2,1)S(1)}) custom-call(s32[1]{0:T(128)} %bitcast.section_ref.refs_0_, s32[1,2,128,7168]{3,2,1,0:T(8,128)S(1)} %bitcast.8, bf16[2,8,2,16,128]{4,3,2,1,0:T(8,128)(2,1)S(1)} %broadcast_in_dim.61.tables_ref, bf16[128,1024]{1,0:T(8,128)(2,1)S(1)} %project.1.folded_ref, ...), custom_call_target="tpu_custom_call" | custom-call | tf_op jit(solution)/shard_map/produce/pallas_call | solution.py:284
  91.4 5.9 %produce.6 = (bf16[256,896]{1,0:T(8,128)(2,1)S(1)}, bf16[256,896]{1,0:T(8,128)(2,1)S(1)}) custom-call(s32[1]{0:T(128)} %bitcast.section_ref.refs_0_, s32[1,2,128,7168]{3,2,1,0:T(8,128)S(1)} %bitcast.8, bf16[2,8,2,16,128]{4,3,2,1,0:T(8,128)(2,1)S(1)} %broadcast_in_dim.61.tables_ref, bf16[128,1024]{1,0:T(8,128)(2,1)S(1)} %project.1.folded_ref, ...), custom_call_target="tpu_custom_call" | custom-call | tf_op jit(solution)/shard_map/produce/pallas_call | solution.py:284
  97.9 1.5 %collective-permute-start.15 = (bf16[256,896]{1,0:T(8,128)(2,1)S(1)}, bf16[256,896]{1,0:T(8,128)(2,1)S(1)}, u32[]{:S(2)}, u32[]{:S(2)}) collective-permute-start(bf16[256,896]{1,0:T(8,128)(2,1)S(1)} %get-tuple-element.62), channel_id=1, source_target_pairs={{0,16},{8,24},{16,0},{24,8},{1,17},{9,25},{17,1},{25,9},{2,18},{10... | collective-permute-start | bytes 1376264 | tf_op jit(solution)/shard_map/ppermute | solution.py:308
  99.4 5.7 %produce.7 = (f32[256,896]{1,0:T(8,128)S(1)}, f32[256,896]{1,0:T(8,128)S(1)}) custom-call(s32[1]{0:T(128)} %bitcast.section_ref.refs_0_, s32[1,2,128,7168]{3,2,1,0:T(8,128)S(1)} %bitcast.8, bf16[2,8,2,16,128]{4,3,2,1,0:T(8,128)(2,1)S(1)} %broadcast_in_dim.61.tables_ref, bf16[128,1024]{1,0:T(8,128)(2,1)S(1)} %project.1.folded_ref, s32[1,2,7168]{2,1,0:T(2,128)S(1)} %copy-done, ...), custom_call_target="tpu_custom_call" | custom-call | tf_op jit(solution)/shard_map/produce/pallas_call | solution.py:284
  105.2 1.5 %collective-permute-start.19 = (bf16[128,896]{1,0:T(8,128)(2,1)S(1)}, bf16[128,896]{1,0:T(8,128)(2,1)S(1)}, u32[]{:S(2)}, u32[]{:S(2)}) collective-permute-start(bf16[128,896]{1,0:T(8,128)(2,1)S(1)} %slice.128), channel_id=1, source_target_pairs={{0,1},{1,0},{2,3},{3,2},{4,5},{5,4},{6,7},{7,6},{8,9},{9,8},{10,11... | collective-permute-start | bytes 688136 | tf_op jit(solution)/shard_map/ppermute | solution.py:308
  107.4 3.9 %collective-permute-done.15 = bf16[256,896]{1,0:T(8,128)(2,1)S(1)} collective-permute-done((bf16[256,896]{1,0:T(8,128)(2,1)S(1)}, bf16[256,896]{1,0:T(8,128)(2,1)S(1)}, u32[]{:S(2)}, u32[]{:S(2)}) %collective-permute-start.15) | collective-permute-done | bytes 458784 | tf_op jit(solution)/shard_map/ppermute | solution.py:308
  111.4 1.6 %collective-permute-start.16 = (bf16[128,896]{1,0:T(8,128)(2,1)S(1)}, bf16[128,896]{1,0:T(8,128)(2,1)S(1)}, u32[]{:S(2)}, u32[]{:S(2)}) collective-permute-start(bf16[128,896]{1,0:T(8,128)(2,1)S(1)} %slice.129), channel_id=1, source_target_pairs={{0,1},{1,0},{2,3},{3,2},{4,5},{5,4},{6,7},{7,6},{8,9},{9,8},{10,11... | collective-permute-start | bytes 688136 | tf_op jit(solution)/shard_map/ppermute | solution.py:308
  113.0 2.2 %collective-permute-done.20 = bf16[128,896]{1,0:T(8,128)(2,1)S(1)} collective-permute-done((bf16[128,896]{1,0:T(8,128)(2,1)S(1)}, bf16[128,896]{1,0:T(8,128)(2,1)S(1)}, u32[]{:S(2)}, u32[]{:S(2)}) %collective-permute-start.20) | collective-permute-done | bytes 229408 | tf_op jit(solution)/shard_map/ppermute | solution.py:308
  115.3 2.3 %collective-permute-start.21 = (bf16[64,896]{1,0:T(8,128)(2,1)S(1)}, bf16[64,896]{1,0:T(8,128)(2,1)S(1)}, u32[]{:S(2)}, u32[]{:S(2)}) collective-permute-start(bf16[64,896]{1,0:T(8,128)(2,1)S(1)} %slice.130), channel_id=1, source_target_pairs={{0,2},{1,3},{2,0},{3,1},{4,6},{5,7},{6,4},{7,5},{8,10},{9,11},{10,... | collective-permute-start | bytes 344072 | tf_op jit(solution)/shard_map/ppermute | solution.py:308
  117.6 2.2 %collective-permute-start.17 = (bf16[64,896]{1,0:T(8,128)(2,1)S(1)}, bf16[64,896]{1,0:T(8,128)(2,1)S(1)}, u32[]{:S(2)}, u32[]{:S(2)}) collective-permute-start(bf16[64,896]{1,0:T(8,128)(2,1)S(1)} %slice.131), channel_id=1, source_target_pairs={{0,2},{1,3},{2,0},{3,1},{4,6},{5,7},{6,4},{7,5},{8,10},{9,11},{10,... | collective-permute-start | bytes 344072 | tf_op jit(solution)/shard_map/ppermute | solution.py:308
  119.8 1.7 %collective-permute-done.21 = bf16[64,896]{1,0:T(8,128)(2,1)S(1)} collective-permute-done((bf16[64,896]{1,0:T(8,128)(2,1)S(1)}, bf16[64,896]{1,0:T(8,128)(2,1)S(1)}, u32[]{:S(2)}, u32[]{:S(2)}) %collective-permute-start.21) | collective-permute-done | bytes 114720 | tf_op jit(solution)/shard_map/ppermute | solution.py:308
  121.5 4.1 %collective-permute-start.22 = (bf16[32,896]{1,0:T(8,128)(2,1)S(1)}, bf16[32,896]{1,0:T(8,128)(2,1)S(1)}, u32[]{:S(2)}, u32[]{:S(2)}) collective-permute-start(bf16[32,896]{1,0:T(8,128)(2,1)S(1)} %slice.132), channel_id=1, source_target_pairs={{0,4},{1,5},{2,6},{3,7},{4,0},{5,1},{6,2},{7,3},{8,12},{9,13},{10,... | collective-permute-start | bytes 172040 | tf_op jit(solution)/shard_map/ppermute | solution.py:308
  125.6 1.2 collective-permute-start.18
  126.8 1.3 %collective-permute-done.22 = bf16[32,896]{1,0:T(8,128)(2,1)S(1)} collective-permute-done((bf16[32,896]{1,0:T(8,128)(2,1)S(1)}, bf16[32,896]{1,0:T(8,128)(2,1)S(1)}, u32[]{:S(2)}, u32[]{:S(2)}) %collective-permute-start.22) | collective-permute-done | bytes 57376 | tf_op jit(solution)/shard_map/ppermute | solution.py:308
  128.2 2.6 %collective-permute-done.18 = bf16[32,896]{1,0:T(8,128)(2,1)S(1)} collective-permute-done((bf16[32,896]{1,0:T(8,128)(2,1)S(1)}, bf16[32,896]{1,0:T(8,128)(2,1)S(1)}, u32[]{:S(2)}, u32[]{:S(2)}) %collective-permute-start.18) | collective-permute-done | bytes 57376 | tf_op jit(solution)/shard_map/ppermute | solution.py:308
  (92 shorter events, 7.1 us)
Async XLA Ops:
  0.0 18.2 %copy-start.4 = (bf16[32,1792]{1,0:T(8,128)(2,1)S(1)}, bf16[32,1792]{1,0:T(8,128)(2,1)}, u32[]{:S(2)}) copy-start(bf16[32,1792]{1,0:T(8,128)(2,1)} %param.11) | copy-start | bytes 344068
  0.0 19.9 %copy-start.6 = (bf16[2,2,256,8]{2,3,1,0:T(8,128)(2,1)S(1)}, bf16[2,2,256,8]{2,3,1,0:T(8,128)(2,1)}, u32[]{:S(2)}) copy-start(bf16[2,2,256,8]{2,3,1,0:T(8,128)(2,1)} %param.18) | copy-start | bytes 49156
  0.0 19.9 %copy-start.7 = (bf16[2,256,8]{1,2,0:T(8,128)(2,1)S(1)}, bf16[2,256,8]{1,2,0:T(8,128)(2,1)}, u32[]{:S(2)}) copy-start(bf16[2,256,8]{1,2,0:T(8,128)(2,1)} %param.19) | copy-start | bytes 24580
  3.4 11.7 %collective-permute-start = (bf16[32,1920]{1,0:T(8,128)(2,1)S(1)}, bf16[32,1920]{1,0:T(8,128)(2,1)S(1)}, u32[]{:S(2)}, u32[]{:S(2)}) collective-permute-start(bf16[32,1920]{1,0:T(8,128)(2,1)S(1)} %pad_maximum_fusion.4), channel_id=1, source_target_pairs={{0,4},{1,5},{2,6},{3,7},{4,0},{5,1},{6,2},{7,3},{8,12},{9,13},{10,... | collective-permute-start | bytes 368648 | tf_op jit(solution)/shard_map/ppermute | solution.py:308
  7.5 7.6 %collective-permute-start.1 = (bf16[32,1920]{1,0:T(8,128)(2,1)S(1)}, bf16[32,1920]{1,0:T(8,128)(2,1)S(1)}, u32[]{:S(2)}, u32[]{:S(2)}) collective-permute-start(bf16[32,1920]{1,0:T(8,128)(2,1)S(1)} %pad_maximum_fusion.4), channel_id=1, source_target_pairs={{0,2},{1,3},{2,0},{3,1},{4,6},{5,7},{6,4},{7,5},{8,10},{9,11},{10,... | collective-permute-start | bytes 368648 | tf_op jit(solution)/shard_map/ppermute | solution.py:308
  9.1 8.2 %collective-permute-start.2 = (bf16[32,1920]{1,0:T(8,128)(2,1)S(1)}, bf16[32,1920]{1,0:T(8,128)(2,1)S(1)}, u32[]{:S(2)}, u32[]{:S(2)}) collective-permute-start(bf16[32,1920]{1,0:T(8,128)(2,1)S(1)} %pad_maximum_fusion.4), channel_id=1, source_target_pairs={{0,6},{1,7},{2,4},{3,5},{4,2},{5,3},{6,0},{7,1},{8,14},{9,15},{10,... | collective-permute-start | bytes 368648 | tf_op jit(solution)/shard_map/ppermute | solution.py:308
  18.3 15.7 %collective-permute-start.3 = (bf16[128,1024]{1,0:T(8,128)(2,1)S(1)}, bf16[128,1024]{1,0:T(8,128)(2,1)S(1)}, u32[]{:S(2)}, u32[]{:S(2)}) collective-permute-start(bf16[128,1024]{1,0:T(8,128)(2,1)S(1)} %fusion.8), channel_id=1, source_target_pairs={{0,1},{1,0},{2,3},{3,2},{4,5},{5,4},{6,7},{7,6},{8,9},{9,8},{10,11... | collective-permute-start | bytes 786440 | tf_op jit(solution)/shard_map/ppermute | solution.py:308
  19.9 14.0 %collective-permute-start.4 = (bf16[128,896]{1,0:T(8,128)(2,1)S(1)}, bf16[128,896]{1,0:T(8,128)(2,1)S(1)}, u32[]{:S(2)}, u32[]{:S(2)}) collective-permute-start(bf16[128,896]{1,0:T(8,128)(2,1)S(1)} %pad_maximum_fusion.3), channel_id=1, source_target_pairs={{0,16},{8,24},{16,0},{24,8},{1,17},{9,25},{17,1},{25,9},{2,18},{10... | collective-permute-start | bytes 688136 | tf_op jit(solution)/shard_map/ppermute | solution.py:308
  21.5 27.2 %collective-permute-start.6 = (bf16[128,896]{1,0:T(8,128)(2,1)S(1)}, bf16[128,896]{1,0:T(8,128)(2,1)S(1)}, u32[]{:S(2)}, u32[]{:S(2)}) collective-permute-start(bf16[128,896]{1,0:T(8,128)(2,1)S(1)} %pad_maximum_fusion.3), channel_id=1, source_target_pairs={{0,1},{1,0},{2,3},{3,2},{4,5},{5,4},{6,7},{7,6},{8,9},{9,8},{10,11... | collective-permute-start | bytes 688136 | tf_op jit(solution)/shard_map/ppermute | solution.py:308
  34.0 14.6 %collective-permute-start.5 = (bf16[256,896]{1,0:T(8,128)(2,1)S(1)}, bf16[256,896]{1,0:T(8,128)(2,1)S(1)}, u32[]{:S(2)}, u32[]{:S(2)}) collective-permute-start(bf16[256,896]{1,0:T(8,128)(2,1)S(1)} %slice.91.refs_5_), channel_id=1, source_target_pairs={{0,16},{8,24},{16,0},{24,8},{1,17},{9,25},{17,1},{25,9},{2,18},{10... | collective-permute-start | bytes 1376264 | tf_op jit(solution)/shard_map/ppermute | solution.py:308
  34.6 27.3 %collective-permute-start.8 = (bf16[256,896]{1,0:T(8,128)(2,1)S(1)}, bf16[256,896]{1,0:T(8,128)(2,1)S(1)}, u32[]{:S(2)}, u32[]{:S(2)}) collective-permute-start(bf16[256,896]{1,0:T(8,128)(2,1)S(1)} %slice.91.refs_5_), channel_id=1, source_target_pairs={{0,8},{8,0},{16,24},{24,16},{1,9},{9,1},{17,25},{25,17},{2,10},{10... | collective-permute-start | bytes 1376264 | tf_op jit(solution)/shard_map/ppermute | solution.py:308
  34.6 14.0 %collective-permute-start.7 = (bf16[128,896]{1,0:T(8,128)(2,1)S(1)}, bf16[128,896]{1,0:T(8,128)(2,1)S(1)}, u32[]{:S(2)}, u32[]{:S(2)}) collective-permute-start(bf16[128,896]{1,0:T(8,128)(2,1)S(1)} %collective-permute-done.4), channel_id=1, source_target_pairs={{0,1},{1,0},{2,3},{3,2},{4,5},{5,4},{6,7},{7,6},{8,9},{9,8},{10,11... | collective-permute-start | bytes 688136 | tf_op jit(solution)/shard_map/ppermute | solution.py:308
  36.6 42.5 %slice-start = ((s8[7340032]{0:T(1024)(128)(4,1)}), s8[4194304]{0:T(1024)(128)(4,1)S(1)}, s32[]{:S(2)}) async-start(s8[7340032]{0:T(1024)(128)(4,1)} %bitcast.7), calls=%async_computation | async-start | bytes 8388608
  48.7 13.2 %collective-permute-start.11 = (bf16[256,896]{1,0:T(8,128)(2,1)S(1)}, bf16[256,896]{1,0:T(8,128)(2,1)S(1)}, u32[]{:S(2)}, u32[]{:S(2)}) collective-permute-start(bf16[256,896]{1,0:T(8,128)(2,1)S(1)} %constant_dynamic-update-slice_fusion.4.refs_8_), channel_id=1, source_target_pairs={{0,8},{8,0},{16,24},{24,16},{1,9},{9,1},{17,25},{25,17},{2,10},{10... | collective-permute-start | bytes 1376264 | tf_op jit(solution)/shard_map/ppermute | solution.py:308
  49.0 12.9 %collective-permute-start.9 = (bf16[256,896]{1,0:T(8,128)(2,1)S(1)}, bf16[256,896]{1,0:T(8,128)(2,1)S(1)}, u32[]{:S(2)}, u32[]{:S(2)}) collective-permute-start(bf16[256,896]{1,0:T(8,128)(2,1)S(1)} %constant_dynamic-update-slice_fusion.2.refs_6_), channel_id=1, source_target_pairs={{0,8},{8,0},{16,24},{24,16},{1,9},{9,1},{17,25},{25,17},{2,10},{10... | collective-permute-start | bytes 1376264 | tf_op jit(solution)/shard_map/ppermute | solution.py:308
  49.4 12.5 %collective-permute-start.10 = (bf16[256,896]{1,0:T(8,128)(2,1)S(1)}, bf16[256,896]{1,0:T(8,128)(2,1)S(1)}, u32[]{:S(2)}, u32[]{:S(2)}) collective-permute-start(bf16[256,896]{1,0:T(8,128)(2,1)S(1)} %collective-permute-done.5.refs_7_), channel_id=1, source_target_pairs={{0,8},{8,0},{16,24},{24,16},{1,9},{9,1},{17,25},{25,17},{2,10},{10... | collective-permute-start | bytes 1376264 | tf_op jit(solution)/shard_map/ppermute | solution.py:308
  49.8 12.8 %copy-start = (s32[1,2,7168]{2,1,0:T(2,128)S(1)}, s32[1,2,7168]{2,1,0:T(2,128)}, u32[]{:S(2)}) copy-start(s32[1,2,7168]{2,1,0:T(2,128)} %signs_ref.7) | copy-start | bytes 172036
  49.8 12.8 %copy-start.2 = (bf16[128,128]{1,0:T(8,128)(2,1)S(1)}, bf16[128,128]{1,0:T(8,128)(2,1)}, u32[]{:S(2)}) copy-start(bf16[128,128]{1,0:T(8,128)(2,1)} %constant.33.clone.refs_15_) | copy-start | bytes 98308
  49.9 12.8 %copy-start.3 = (s32[1,1024]{1,0:T(1,128)S(1)}, s32[1,1024]{1,0:T(1,128)}, u32[]{:S(2)}) copy-start(s32[1,1024]{1,0:T(1,128)} %refs_14_.1) | copy-start | bytes 12292
  49.9 29.3 %slice-start.1 = ((s8[7340032]{0:T(1024)(128)(4,1)}), s8[3145728]{0:T(1024)(128)(4,1)S(1)}, s32[]{:S(2)}) async-start(s8[7340032]{0:T(1024)(128)(4,1)} %bitcast.7), calls=%async_computation.1 | async-start | bytes 6291456
  61.9 17.3 %copy-start.1 = (bf16[128,128]{1,0:T(8,128)(2,1)S(1)}, bf16[128,128]{1,0:T(8,128)(2,1)}, u32[]{:S(2)}) copy-start(bf16[128,128]{1,0:T(8,128)(2,1)} %constant.34.clone.had_ref) | copy-start | bytes 98308
  85.0 6.1 %collective-permute-start.12 = (bf16[256,1792]{1,0:T(8,128)(2,1)S(1)}, bf16[256,1792]{1,0:T(8,128)(2,1)S(1)}, u32[]{:S(2)}, u32[]{:S(2)}) collective-permute-start(bf16[256,1792]{1,0:T(8,128)(2,1)S(1)} %pad_maximum_fusion), channel_id=1, source_target_pairs={{0,8},{8,0},{16,24},{24,16},{1,9},{9,1},{17,25},{25,17},{2,10},{10... | collective-permute-start | bytes 2752520 | tf_op jit(solution)/shard_map/ppermute | solution.py:308
  91.0 6.2 %collective-permute-start.13 = (bf16[256,1792]{1,0:T(8,128)(2,1)S(1)}, bf16[256,1792]{1,0:T(8,128)(2,1)S(1)}, u32[]{:S(2)}, u32[]{:S(2)}) collective-permute-start(bf16[256,1792]{1,0:T(8,128)(2,1)S(1)} %pad_maximum_fusion.1), channel_id=1, source_target_pairs={{0,8},{8,0},{16,24},{24,16},{1,9},{9,1},{17,25},{25,17},{2,10},{10... | collective-permute-start | bytes 2752520 | tf_op jit(solution)/shard_map/ppermute | solution.py:308
  97.3 7.8 %collective-permute-start.14 = (bf16[128,896]{1,0:T(8,128)(2,1)S(1)}, bf16[128,896]{1,0:T(8,128)(2,1)S(1)}, u32[]{:S(2)}, u32[]{:S(2)}) collective-permute-start(bf16[128,896]{1,0:T(8,128)(2,1)S(1)} %slice.76), channel_id=1, source_target_pairs={{0,1},{1,0},{2,3},{3,2},{4,5},{5,4},{6,7},{7,6},{8,9},{9,8},{10,11... | collective-permute-start | bytes 688136 | tf_op jit(solution)/shard_map/ppermute | solution.py:308
  97.9 13.4 %collective-permute-start.15 = (bf16[256,896]{1,0:T(8,128)(2,1)S(1)}, bf16[256,896]{1,0:T(8,128)(2,1)S(1)}, u32[]{:S(2)}, u32[]{:S(2)}) collective-permute-start(bf16[256,896]{1,0:T(8,128)(2,1)S(1)} %get-tuple-element.62), channel_id=1, source_target_pairs={{0,16},{8,24},{16,0},{24,8},{1,17},{9,25},{17,1},{25,9},{2,18},{10... | collective-permute-start | bytes 1376264 | tf_op jit(solution)/shard_map/ppermute | solution.py:308
  105.2 7.8 %collective-permute-start.19 = (bf16[128,896]{1,0:T(8,128)(2,1)S(1)}, bf16[128,896]{1,0:T(8,128)(2,1)S(1)}, u32[]{:S(2)}, u32[]{:S(2)}) collective-permute-start(bf16[128,896]{1,0:T(8,128)(2,1)S(1)} %slice.128), channel_id=1, source_target_pairs={{0,1},{1,0},{2,3},{3,2},{4,5},{5,4},{6,7},{7,6},{8,9},{9,8},{10,11... | collective-permute-start | bytes 688136 | tf_op jit(solution)/shard_map/ppermute | solution.py:308
  106.7 8.4 %collective-permute-start.20 = (bf16[128,896]{1,0:T(8,128)(2,1)S(1)}, bf16[128,896]{1,0:T(8,128)(2,1)S(1)}, u32[]{:S(2)}, u32[]{:S(2)}) collective-permute-start(bf16[128,896]{1,0:T(8,128)(2,1)S(1)} %add_convert_fusion), channel_id=1, source_target_pairs={{0,16},{8,24},{16,0},{24,8},{1,17},{9,25},{17,1},{25,9},{2,18},{10... | collective-permute-start | bytes 688136 | tf_op jit(solution)/shard_map/ppermute | solution.py:308
  111.4 6.1 %collective-permute-start.16 = (bf16[128,896]{1,0:T(8,128)(2,1)S(1)}, bf16[128,896]{1,0:T(8,128)(2,1)S(1)}, u32[]{:S(2)}, u32[]{:S(2)}) collective-permute-start(bf16[128,896]{1,0:T(8,128)(2,1)S(1)} %slice.129), channel_id=1, source_target_pairs={{0,1},{1,0},{2,3},{3,2},{4,5},{5,4},{6,7},{7,6},{8,9},{9,8},{10,11... | collective-permute-start | bytes 688136 | tf_op jit(solution)/shard_map/ppermute | solution.py:308
  115.3 6.2 %collective-permute-start.21 = (bf16[64,896]{1,0:T(8,128)(2,1)S(1)}, bf16[64,896]{1,0:T(8,128)(2,1)S(1)}, u32[]{:S(2)}, u32[]{:S(2)}) collective-permute-start(bf16[64,896]{1,0:T(8,128)(2,1)S(1)} %slice.130), channel_id=1, source_target_pairs={{0,2},{1,3},{2,0},{3,1},{4,6},{5,7},{6,4},{7,5},{8,10},{9,11},{10,... | collective-permute-start | bytes 344072 | tf_op jit(solution)/shard_map/ppermute | solution.py:308
  117.6 8.0 %collective-permute-start.17 = (bf16[64,896]{1,0:T(8,128)(2,1)S(1)}, bf16[64,896]{1,0:T(8,128)(2,1)S(1)}, u32[]{:S(2)}, u32[]{:S(2)}) collective-permute-start(bf16[64,896]{1,0:T(8,128)(2,1)S(1)} %slice.131), channel_id=1, source_target_pairs={{0,2},{1,3},{2,0},{3,1},{4,6},{5,7},{6,4},{7,5},{8,10},{9,11},{10,... | collective-permute-start | bytes 344072 | tf_op jit(solution)/shard_map/ppermute | solution.py:308
  121.5 6.6 %collective-permute-start.22 = (bf16[32,896]{1,0:T(8,128)(2,1)S(1)}, bf16[32,896]{1,0:T(8,128)(2,1)S(1)}, u32[]{:S(2)}, u32[]{:S(2)}) collective-permute-start(bf16[32,896]{1,0:T(8,128)(2,1)S(1)} %slice.132), channel_id=1, source_target_pairs={{0,4},{1,5},{2,6},{3,7},{4,0},{5,1},{6,2},{7,3},{8,12},{9,13},{10,... | collective-permute-start | bytes 172040 | tf_op jit(solution)/shard_map/ppermute | solution.py:308
  125.6 5.1 %collective-permute-start.18 = (bf16[32,896]{1,0:T(8,128)(2,1)S(1)}, bf16[32,896]{1,0:T(8,128)(2,1)S(1)}, u32[]{:S(2)}, u32[]{:S(2)}) collective-permute-start(bf16[32,896]{1,0:T(8,128)(2,1)S(1)} %slice.133), channel_id=1, source_target_pairs={{0,4},{1,5},{2,6},{3,7},{4,0},{5,1},{6,2},{7,3},{8,12},{9,13},{10,... | collective-permute-start | bytes 172040 | tf_op jit(solution)/shard_map/ppermute | solution.py:308
  (1 other events, 0.8 us)

commit v4 on v3

--- a/solution.py
+++ b/solution.py
@@ -70,12 +70,13 @@
     return sums
 
 
-def decode_in(section, codes, tables, weights, order, place):
+def decode_in(section, codes, tables, weights, piece, cols, stored):
     _, mats, books, groups, hidden = codes.shape
-    sections = 4
+    sections = stored + 1
     group = tables.shape[2]
     share = groups // sections
-    cols = 512
+    per_mat = hidden // cols
+    mat, block = piece // per_mat, piece % per_mat
 
     def body(section_ref, codes_ref, tables_ref, *rest):
         out = rest[-1]
@@ -91,11 +92,12 @@
                     at = (g * group + i) * ROWS
                     out[0, at : at + ROWS, lanes] = tiles[i]
 
+    def source(j, s):
+        return (0, mat, 0, jnp.bitwise_xor(s[0], (j % 2) * 2 + j // 2), block)
+
     in_specs = [
-        pl.BlockSpec(
-            (1, 1, books, share, cols), lambda m, h, s: (0, m, 0, jnp.bitwise_xor(s[0], order), h)
-        ),
-        pl.BlockSpec((1,) + tables.shape[1:], lambda m, h, s: (m, 0, 0, 0, 0, 0)),
+        pl.BlockSpec((1, 1, books, share, cols), source),
+        pl.BlockSpec((1,) + tables.shape[1:], lambda j, s: (mat, 0, 0, 0, 0, 0)),
     ]
     operands = [section, codes, tables]
     aliases = {}
@@ -107,11 +109,11 @@
         body,
         grid_spec=pltpu.PrefetchScalarGridSpec(
             num_scalar_prefetch=1,
-            grid=(mats, hidden // cols),
+            grid=(stored,),
             in_specs=in_specs,
-            out_specs=pl.BlockSpec((1, share * group, cols), lambda m, h, s: (m, place, h)),
+            out_specs=pl.BlockSpec((1, share * group, cols), lambda j, s: (mat, j, block)),
         ),
-        out_shape=jax.ShapeDtypeStruct((mats, (sections - 1) * share * group, hidden), bf16),
+        out_shape=jax.ShapeDtypeStruct((mats, stored * share * group, hidden), bf16),
         input_output_aliases=aliases,
         compiler_params=pltpu.CompilerParams(vmem_limit_bytes=50 << 20),
         name="decode_in",
@@ -209,20 +211,17 @@
     )(section, codes, tables, weights, pick, *pieces, signs, middle, had)
 
 
-def produce(section, codes, tables, folded, signs, had, spread, order, added, dtype):
+def produce(section, codes, tables, folded, signs, had, spread, order, cols, at_col, dtype):
     _, books, groups, width = codes.shape
     sections = 4
     group = tables.shape[1]
     slots, hidden = folded.shape
     token_total = spread.shape[0]
-    cols = width // sections
+    per_quarter = width // sections // cols
     tile = 2 * LANES
     pair = 2
 
-    extra = [] if added is None else [added]
-
-    def body(section_ref, codes_ref, tables_ref, folded_ref, signs_ref, had_ref, spread_ref, *rest):
-        outs = rest[-2:]
+    def body(section_ref, codes_ref, tables_ref, folded_ref, signs_ref, had_ref, spread_ref, out):
         back = (2 * signs_ref[0, 1:2, :] - 1).astype(f32)
 
         def outcome_of(at, size):
@@ -255,16 +254,7 @@
                 turned.append(dot(high[:, s], table) + (dot(mid[:, s], table) + dot(low[:, s], table)))
             turned = jnp.concatenate(turned, 1) * UNIT
             result = (back[:, at : at + size] * turned).astype(bf16)
-            weighted = dot(spread_ref[...], result)
-            if extra:
-                weighted = weighted + rest[0][:, at : at + size].astype(f32)
-            for side in range(2):
-                low, high = max(at, side * cols // 2), min(at + size, (side + 1) * cols // 2)
-                if low < high:
-                    shift = side * cols // 2
-                    outs[side][:, low - shift : high - shift] = weighted[
-                        :, low - at : high - at
-                    ].astype(dtype)
+            out[:, at : at + size] = dot(spread_ref[...], result).astype(dtype)
 
         pending = None
         at = 0
@@ -278,7 +268,7 @@
         finish(*pending)
 
     def column(s):
-        return jnp.bitwise_xor(s[0], order)
+        return jnp.bitwise_xor(s[0], order) * per_quarter + at_col
 
     whole = lambda shape: pl.BlockSpec(shape, lambda j, s: (0,) * len(shape))
     return pl.pallas_call(
@@ -293,14 +283,13 @@
                 pl.BlockSpec((1, 2, cols), lambda j, s: (0, 0, column(s))),
                 whole(had.shape),
                 whole(spread.shape),
-            ]
-            + [whole(e.shape) for e in extra],
-            out_specs=[whole((token_total, cols // 2))] * 2,
+            ],
+            out_specs=whole((token_total, cols)),
         ),
-        out_shape=[jax.ShapeDtypeStruct((token_total, cols // 2), dtype)] * 2,
+        out_shape=jax.ShapeDtypeStruct((token_total, cols), dtype),
         compiler_params=pltpu.CompilerParams(vmem_limit_bytes=20 << 20),
         name="produce",
-    )(section, codes, tables, folded, signs, had, spread, *extra)
+    )(section, codes, tables, folded, signs, had, spread)
 
 
 def swap(values, axis, stride):
@@ -353,20 +342,29 @@
     facts = jnp.pad(facts, ((0, 0), (0, LANES - 2 * top)))
     row = jnp.concatenate([tokens, facts], 1)
     gathered = [row] + [swap(row, "dev", b) for b in relative[1 : devices // 2]]
+
+    def piece_of(stack, piece):
+        return decode_in(
+            section_word, gate_up_codes, tables_in, stack, piece, hidden // 2, sections - 1
+        )
+
+    hidden = gate_up_codes.shape[-1]
+    weights = piece_of(None, 0)
+    weights, gathered = fence(weights, gathered)
     gathered = jnp.concatenate(gathered, 0)
     first = jnp.concatenate([gathered[:, :half], gathered[:, quarter:]], 1)
     second = gathered[:, half:quarter]
-    section_word, first, second = fence(section_word, first, second)
+    weights, first, second = fence(weights, first, second)
     first_near = swap(first, "dev", 1)
     second_cross = swap(second, "sec", 2)
-    weights = decode_in(section_word, gate_up_codes, tables_in, None, places[0], 0)
+    weights = piece_of(weights, 1)
     weights, first_near, second_cross = fence(weights, first_near, second_cross)
     first = jnp.concatenate([first, first_near], 0)
     first, facts = first[:, :half], first[:, half:].astype(f32)
     first_cross = swap(first, "sec", 2)
     second_near = swap(second, "dev", 1)
     second_both = swap(second_cross, "dev", 1)
-    weights = decode_in(section_word, gate_up_codes, tables_in, weights, places[1], 1)
+    weights = piece_of(weights, 2)
     weights, first_cross, second_near, second_both = fence(
         weights, first_cross, second_near, second_both
     )
@@ -374,7 +372,7 @@
     second_cross = jnp.concatenate([second_cross, second_both], 0)
     pieces = [first, second, first_cross, second_cross]
     pieces = pieces + [swap(p, "sec", 1) for p in pieces]
-    weights = decode_in(section_word, gate_up_codes, tables_in, weights, places[2], 2)
+    weights = piece_of(weights, 3)
 
     expert = ((section - 1) * devices + device).astype(f32)
     named = facts[:, :top] == expert
@@ -407,7 +405,7 @@
         places,
     )
 
-    def make(order, added=None, dtype=bf16):
+    def make(order, cols=quarter, at_col=0, dtype=bf16):
         return produce(
             section_word,
             down_codes,
@@ -417,30 +415,45 @@
             had,
             spread,
             order,
-            added,
+            cols,
+            at_col,
             dtype,
         )
 
     rows = token_total // 2
-    far_made = jnp.concatenate(make(3), 1)
-    folded, far_made = fence(folded, far_made)
-    far_near = swap(far_made, "sec", 1)
-    beside = jnp.concatenate(make(1), 1)
-    folded, beside, far_near = fence(folded, beside, far_near)
+    given = make(3)
+    folded, given = fence(folded, given)
+    given = swap(given, "sec", 1)
+    across = make(2)
+    folded, across, given = fence(folded, across, given)
+    across = across.astype(f32) + given.astype(f32)
+    early = half // LANES // 2 * LANES
+    first_across = [across[:, :early].astype(bf16), across[:, early:half].astype(bf16)]
+    second_met = across[rows:, half:].astype(bf16)
+    second_kept = across[:rows, half:].astype(bf16)
+    folded, *first_across, second_met, second_kept = fence(
+        folded, *first_across, second_met, second_kept
+    )
+    first_across = [swap(f, "sec", 2) for f in first_across]
+    second_met = swap(second_met, "dev", 1)
+    beside = make(1)
+    folded, beside, second_met, first_across[0] = fence(
+        folded, beside, second_met, first_across[0]
+    )
     beside = swap(beside, "sec", 1)
-    across = make(2, far_near)
-    folded, beside, *across = fence(folded, beside, *across)
-    first_across = swap(across[0], "sec", 2)
-    second_met = swap(across[1][rows:], "dev", 1)
-    first, second = make(0, beside, f32)
-    first, second, second_met = fence(first, second, second_met)
-    second_across = (across[1][:rows].astype(f32) + second_met.astype(f32)).astype(bf16)
+    second_across = (second_kept.astype(f32) + second_met.astype(f32)).astype(bf16)
     second_across = swap(second_across, "sec", 2)
+    second = make(0, half, 1, f32)
+    folded, second, beside = fence(folded, second, beside)
+    second = second + beside[:, half:].astype(f32)
     second_near = swap(second[rows:].astype(bf16), "dev", 1)
-    first = first + first_across.astype(f32)
+    first = make(0, half, 0, f32)
+    first, second_near = fence(first, second_near)
+    first_across = jnp.concatenate(first_across, 1)
+    first = first + beside[:, :half].astype(f32) + first_across.astype(f32)
     first_near = swap(first[rows:].astype(bf16), "dev", 1)
+    second = second[:rows] + second_near.astype(f32) + second_across.astype(f32)
     first = first[:rows] + first_near.astype(f32)
-    second = second[:rows] + second_near.astype(f32) + second_across.astype(f32)
     outs = []
     for total in (first, second):
         for stride in strides[1:]:

time: 132 us -> 125 us (0.947)
  waiting for transfers between devices: 19.9 us -> 11.3 us
  Pallas kernels: 75.2 us -> 78.4 us
  starting transfers between devices: 28.5 us -> 26.7 us
    ppermute x23 -> x24, waiting for transfers between devices: 19.9 us -> 11.3 us  [swap(): return lax.ppermute(values, axis, [(i, i ^ stride) for i in range(size)])]
    pallas_call x3 -> x4, Pallas kernels: 35.9 us -> 38.2 us  [decode_in(): pl.pallas_call(body, grid_spec=pltpu.PrefetchScalarGridSpec(num_scalar_pr...]
    ppermute x23 -> x24, starting transfers between devices: 28.5 us -> 26.7 us  [swap(): return lax.ppermute(values, axis, [(i, i ^ stride) for i in range(size)])]
    pallas_call x4 -> x5, Pallas kernels: 22.9 us -> 23.7 us  [produce(): pl.pallas_call(body, grid_spec=pltpu.PrefetchScalarGridSpec(num_scalar_pr...]
  transfers between devices with their start and end apart: 23 -> 24, of which waited for: 8 -> 5; matrix products, arithmetic and copies ran while one was open for 1% -> 2% of each run, Pallas kernels for 40% -> 45%
where the time goes in v4:
time: 125 us; the launch traced here: 124 us
  Pallas kernels  78.4 us (63%)
  starting transfers between devices  26.7 us (21%)
  waiting for transfers between devices  11.3 us (9%)
  other arithmetic  4.47 us (4%)
  local copies, waits for them, and re-layouts  2.93 us (2%)
    pallas_call x4, Pallas kernels, decode_in(): pl.pallas_call(body, grid_spec=pltpu.PrefetchScalarGridSpec(num_scalar_pr...  38.2 us
    ppermute x24, starting transfers between devices, swap(): return lax.ppermute(values, axis, [(i, i ^ stride) for i in range(size)])  26.7 us
    pallas_call x5, Pallas kernels, produce(): pl.pallas_call(body, grid_spec=pltpu.PrefetchScalarGridSpec(num_scalar_pr...  23.7 us
    pallas_call x1, Pallas kernels, project(): pl.pallas_call(body, grid_spec=pltpu.PrefetchScalarGridSpec(num_scalar_pr...  16.4 us
    ppermute x24, waiting for transfers between devices, swap(): return lax.ppermute(values, axis, [(i, i ^ stride) for i in range(size)])  11.3 us
  transfers between devices with their start and end apart: 24, of which 5 were waited for; matrix products, arithmetic and copies ran while one was open for 2% of the time, Pallas kernels for 45%

profile of v4, /device:TPU:0, one launch (start us, length us, event | category | flops | bytes accessed | tf_op | source)
XLA Modules:
  0.0 124.3 jit_solution(6256859543899986056)
XLA Ops:
  0.0 0.8 copy.25
  2.4 0.9 pad_maximum_fusion.1
  3.3 4.1 %collective-permute-start = (bf16[32,1920]{1,0:T(8,128)(2,1)S(1)}, bf16[32,1920]{1,0:T(8,128)(2,1)S(1)}, u32[]{:S(2)}, u32[]{:S(2)}) collective-permute-start(bf16[32,1920]{1,0:T(8,128)(2,1)S(1)} %pad_maximum_fusion.1), channel_id=1, source_target_pairs={{0,4},{1,5},{2,6},{3,7},{4,0},{5,1},{6,2},{7,3},{8,12},{9,13},{10,... | collective-permute-start | bytes 368648 | tf_op jit(solution)/shard_map/ppermute | solution.py:297
  7.4 1.6 %collective-permute-start.1 = (bf16[32,1920]{1,0:T(8,128)(2,1)S(1)}, bf16[32,1920]{1,0:T(8,128)(2,1)S(1)}, u32[]{:S(2)}, u32[]{:S(2)}) collective-permute-start(bf16[32,1920]{1,0:T(8,128)(2,1)S(1)} %pad_maximum_fusion.1), channel_id=1, source_target_pairs={{0,2},{1,3},{2,0},{3,1},{4,6},{5,7},{6,4},{7,5},{8,10},{9,11},{10,... | collective-permute-start | bytes 368648 | tf_op jit(solution)/shard_map/ppermute | solution.py:297
  9.8 9.5 %decode_in.4.rest_0_ = bf16[2,5376,1024]{2,1,0:T(8,128)(2,1)} custom-call(s32[1]{0:T(128)} %bitcast.section_ref.refs_0_, s32[1,2,2,896,1024]{4,3,2,1,0:T(8,128)} %refs_1_.1, bf16[2,2,8,2,16,128]{5,4,3,2,1,0:T(8,128)(2,1)S(1)} %broadcast_in_dim.63.tables_ref.refs_2_), custom_call_target="tpu_custom_call" | custom-call | tf_op jit(solution)/shard_map/decode_in/pallas_call | solution.py:108
  19.5 1.8 %collective-permute-start.3 = (bf16[128,1024]{1,0:T(8,128)(2,1)S(1)}, bf16[128,1024]{1,0:T(8,128)(2,1)S(1)}, u32[]{:S(2)}, u32[]{:S(2)}) collective-permute-start(bf16[128,1024]{1,0:T(8,128)(2,1)S(1)} %pad_maximum_fusion), channel_id=1, source_target_pairs={{0,1},{1,0},{2,3},{3,2},{4,5},{5,4},{6,7},{7,6},{8,9},{9,8},{10,11... | collective-permute-start | bytes 786440 | tf_op jit(solution)/shard_map/ppermute | solution.py:297
  21.3 1.6 %collective-permute-start.4 = (bf16[128,896]{1,0:T(8,128)(2,1)S(1)}, bf16[128,896]{1,0:T(8,128)(2,1)S(1)}, u32[]{:S(2)}, u32[]{:S(2)}) collective-permute-start(bf16[128,896]{1,0:T(8,128)(2,1)S(1)} %get-tuple-element.46), channel_id=1, source_target_pairs={{0,16},{8,24},{16,0},{24,8},{1,17},{9,25},{17,1},{25,9},{2,18},{10... | collective-permute-start | bytes 688136 | tf_op jit(solution)/shard_map/ppermute | solution.py:297
  23.4 9.5 %decode_in.5.rest_0_ = bf16[2,5376,1024]{2,1,0:T(8,128)(2,1)} custom-call(s32[1]{0:T(128)} %bitcast.section_ref.refs_0_, s32[1,2,2,896,1024]{4,3,2,1,0:T(8,128)} %refs_1_.1, bf16[2,2,8,2,16,128]{5,4,3,2,1,0:T(8,128)(2,1)S(1)} %broadcast_in_dim.63.tables_ref.refs_2_, bf16[2,5376,1024]{2,1,0:T(8,128)(2,1)} %decode_in.4.rest_0_), custom_call_target="tpu_custom_call", output_to_operand_aliasing={{}: (3, {})} | custom-call | tf_op jit(solution)/shard_map/decode_in/pallas_call | solution.py:108
  33.5 1.7 %collective-permute-start.7 = (bf16[128,896]{1,0:T(8,128)(2,1)S(1)}, bf16[128,896]{1,0:T(8,128)(2,1)S(1)}, u32[]{:S(2)}, u32[]{:S(2)}) collective-permute-start(bf16[128,896]{1,0:T(8,128)(2,1)S(1)} %collective-permute-done.4), channel_id=1, source_target_pairs={{0,1},{1,0},{2,3},{3,2},{4,5},{5,4},{6,7},{7,6},{8,9},{9,8},{10,11... | collective-permute-start | bytes 688136 | tf_op jit(solution)/shard_map/ppermute | solution.py:297
  35.7 9.5 %decode_in.6.rest_0_ = bf16[2,5376,1024]{2,1,0:T(8,128)(2,1)} custom-call(s32[1]{0:T(128)} %bitcast.section_ref.refs_0_, s32[1,2,2,896,1024]{4,3,2,1,0:T(8,128)} %refs_1_.1, bf16[2,2,8,2,16,128]{5,4,3,2,1,0:T(8,128)(2,1)S(1)} %broadcast_in_dim.63.tables_ref.refs_2_, bf16[2,5376,1024]{2,1,0:T(8,128)(2,1)} %decode_in.5.rest_0_), custom_call_target="tpu_custom_call", output_to_operand_aliasing={{}: (3, {})} | custom-call | tf_op jit(solution)/shard_map/decode_in/pallas_call | solution.py:108
  46.4 9.7 %decode_in.7.refs_3_ = bf16[2,5376,1024]{2,1,0:T(8,128)(2,1)} custom-call(s32[1]{0:T(128)} %bitcast.section_ref.refs_0_, s32[1,2,2,896,1024]{4,3,2,1,0:T(8,128)} %refs_1_.1, bf16[2,2,8,2,16,128]{5,4,3,2,1,0:T(8,128)(2,1)S(1)} %broadcast_in_dim.63.tables_ref.refs_2_, bf16[2,5376,1024]{2,1,0:T(8,128)(2,1)} %decode_in.6.rest_0_), custom_call_target="tpu_custom_call", output_to_operand_aliasing={{}: (3, {})} | custom-call | tf_op jit(solution)/shard_map/decode_in/pallas_call | solution.py:108
  56.2 0.8 copy-done.4
  56.9 16.4 %project.1.folded_ref = bf16[128,1024]{1,0:T(8,128)(2,1)S(1)} custom-call(s32[1]{0:T(128)} %bitcast.section_ref.refs_0_, s32[1,2,2,896,1024]{4,3,2,1,0:T(8,128)} %refs_1_.1, bf16[2,2,8,2,16,128]{5,4,3,2,1,0:T(8,128)(2,1)S(1)} %broadcast_in_dim.63.tables_ref.refs_2_, bf16[2,5376,1024]{2,1,0:T(8,128)(2,1)} %decode_in.7.refs_3_, ...), custom_call_target="tpu_custom_call" | custom-call | tf_op jit(solution)/shard_map/project/pallas_call | solution.py:186
  73.4 5.7 %produce.5 = bf16[256,1792]{1,0:T(8,128)(2,1)S(1)} custom-call(s32[1]{0:T(128)} %bitcast.section_ref.refs_0_, s32[1,2,128,7168]{3,2,1,0:T(8,128)S(1)} %bitcast.8, bf16[2,8,2,16,128]{4,3,2,1,0:T(8,128)(2,1)S(1)} %broadcast_in_dim.61.tables_ref, bf16[128,1024]{1,0:T(8,128)(2,1)S(1)} %project.1.folded_ref, s32[1,2,7168]{2,1,0:T(2,128)S(1)} %copy-done, ...), custom_call_target="tpu_custom_call" | custom-call | tf_op jit(solution)/shard_map/produce/pallas_call | solution.py:274
  79.4 5.7 %produce.6 = bf16[256,1792]{1,0:T(8,128)(2,1)S(1)} custom-call(s32[1]{0:T(128)} %bitcast.section_ref.refs_0_, s32[1,2,128,7168]{3,2,1,0:T(8,128)S(1)} %bitcast.8, bf16[2,8,2,16,128]{4,3,2,1,0:T(8,128)(2,1)S(1)} %broadcast_in_dim.61.tables_ref, bf16[128,1024]{1,0:T(8,128)(2,1)S(1)} %project.1.folded_ref, s32[1,2,7168]{2,1,0:T(2,128)S(1)} %copy-done, ...), custom_call_target="tpu_custom_call" | custom-call | tf_op jit(solution)/shard_map/produce/pallas_call | solution.py:274
  85.8 1.7 %collective-permute-start.14 = (bf16[256,384]{1,0:T(8,128)(2,1)S(1)}, bf16[256,384]{1,0:T(8,128)(2,1)S(1)}, u32[]{:S(2)}, u32[]{:S(2)}) collective-permute-start(bf16[256,384]{1,0:T(8,128)(2,1)S(1)} %slice.117), channel_id=1, source_target_pairs={{0,16},{8,24},{16,0},{24,8},{1,17},{9,25},{17,1},{25,9},{2,18},{10... | collective-permute-start | bytes 589832 | tf_op jit(solution)/shard_map/ppermute | solution.py:297
  87.5 5.9 %produce.7 = bf16[256,1792]{1,0:T(8,128)(2,1)S(1)} custom-call(s32[1]{0:T(128)} %bitcast.section_ref.refs_0_, s32[1,2,128,7168]{3,2,1,0:T(8,128)S(1)} %bitcast.8, bf16[2,8,2,16,128]{4,3,2,1,0:T(8,128)(2,1)S(1)} %broadcast_in_dim.61.tables_ref, bf16[128,1024]{1,0:T(8,128)(2,1)S(1)} %project.1.folded_ref, s32[1,2,7168]{2,1,0:T(2,128)S(1)} %copy-done, ...), custom_call_target="tpu_custom_call" | custom-call | tf_op jit(solution)/shard_map/produce/pallas_call | solution.py:274
  93.5 1.3 %collective-permute-start.17 = (bf16[256,512]{1,0:T(8,128)(2,1)S(1)}, bf16[256,512]{1,0:T(8,128)(2,1)S(1)}, u32[]{:S(2)}, u32[]{:S(2)}) collective-permute-start(bf16[256,512]{1,0:T(8,128)(2,1)S(1)} %slice.118), channel_id=1, source_target_pairs={{0,16},{8,24},{16,0},{24,8},{1,17},{9,25},{17,1},{25,9},{2,18},{10... | collective-permute-start | bytes 786440 | tf_op jit(solution)/shard_map/ppermute | solution.py:297
  94.8 3.2 %produce.8 = f32[256,896]{1,0:T(8,128)S(1)} custom-call(s32[1]{0:T(128)} %bitcast.section_ref.refs_0_, s32[1,2,128,7168]{3,2,1,0:T(8,128)S(1)} %bitcast.8, bf16[2,8,2,16,128]{4,3,2,1,0:T(8,128)(2,1)S(1)} %broadcast_in_dim.61.tables_ref, bf16[128,1024]{1,0:T(8,128)(2,1)S(1)} %project.1.folded_ref, s32[1,2,7168]{2,1,0:T(2,128)S(1)} %copy-done, ...), custom_call_target="tpu_custom_call" | custom-call | tf_op jit(solution)/shard_map/produce/pallas_call | solution.py:274
  98.2 1.1 collective-permute-start.16
  99.3 1.3 %collective-permute-start.21 = (bf16[128,896]{1,0:T(8,128)(2,1)S(1)}, bf16[128,896]{1,0:T(8,128)(2,1)S(1)}, u32[]{:S(2)}, u32[]{:S(2)}) collective-permute-start(bf16[128,896]{1,0:T(8,128)(2,1)S(1)} %add_convert_fusion.1), channel_id=1, source_target_pairs={{0,16},{8,24},{16,0},{24,8},{1,17},{9,25},{17,1},{25,9},{2,18},{10... | collective-permute-start | bytes 688136 | tf_op jit(solution)/shard_map/ppermute | solution.py:297
  100.7 3.2 %produce.9 = f32[256,896]{1,0:T(8,128)S(1)} custom-call(s32[1]{0:T(128)} %bitcast.section_ref.refs_0_, s32[1,2,128,7168]{3,2,1,0:T(8,128)S(1)} %bitcast.8, bf16[2,8,2,16,128]{4,3,2,1,0:T(8,128)(2,1)S(1)} %broadcast_in_dim.61.tables_ref, bf16[128,1024]{1,0:T(8,128)(2,1)S(1)} %project.1.folded_ref, s32[1,2,7168]{2,1,0:T(2,128)S(1)} %copy-done, ...), custom_call_target="tpu_custom_call" | custom-call | tf_op jit(solution)/shard_map/produce/pallas_call | solution.py:274
  103.9 2.1 %collective-permute-done.16 = bf16[128,896]{1,0:T(8,128)(2,1)S(1)} collective-permute-done((bf16[128,896]{1,0:T(8,128)(2,1)S(1)}, bf16[128,896]{1,0:T(8,128)(2,1)S(1)}, u32[]{:S(2)}, u32[]{:S(2)}) %collective-permute-start.16) | collective-permute-done | bytes 229408 | tf_op jit(solution)/shard_map/ppermute | solution.py:297
  106.2 1.1 collective-permute-start.18
  107.4 0.7 collective-permute-start.22
  108.1 5.0 %collective-permute-done.18 = bf16[128,896]{1,0:T(8,128)(2,1)S(1)} collective-permute-done((bf16[128,896]{1,0:T(8,128)(2,1)S(1)}, bf16[128,896]{1,0:T(8,128)(2,1)S(1)}, u32[]{:S(2)}, u32[]{:S(2)}) %collective-permute-start.18) | collective-permute-done | bytes 229408 | tf_op jit(solution)/shard_map/ppermute | solution.py:297
  113.2 0.7 collective-permute-start.19
  114.0 3.6 %collective-permute-start.23 = (bf16[32,896]{1,0:T(8,128)(2,1)S(1)}, bf16[32,896]{1,0:T(8,128)(2,1)S(1)}, u32[]{:S(2)}, u32[]{:S(2)}) collective-permute-start(bf16[32,896]{1,0:T(8,128)(2,1)S(1)} %slice.162), channel_id=1, source_target_pairs={{0,4},{1,5},{2,6},{3,7},{4,0},{5,1},{6,2},{7,3},{8,12},{9,13},{10,... | collective-permute-start | bytes 172040 | tf_op jit(solution)/shard_map/ppermute | solution.py:297
  117.6 0.9 collective-permute-done.19
  118.5 1.8 %collective-permute-start.20 = (bf16[32,896]{1,0:T(8,128)(2,1)S(1)}, bf16[32,896]{1,0:T(8,128)(2,1)S(1)}, u32[]{:S(2)}, u32[]{:S(2)}) collective-permute-start(bf16[32,896]{1,0:T(8,128)(2,1)S(1)} %slice.163), channel_id=1, source_target_pairs={{0,4},{1,5},{2,6},{3,7},{4,0},{5,1},{6,2},{7,3},{8,12},{9,13},{10,... | collective-permute-start | bytes 172040 | tf_op jit(solution)/shard_map/ppermute | solution.py:297
  120.3 1.2 collective-permute-done.23
  121.6 2.1 %collective-permute-done.20 = bf16[32,896]{1,0:T(8,128)(2,1)S(1)} collective-permute-done((bf16[32,896]{1,0:T(8,128)(2,1)S(1)}, bf16[32,896]{1,0:T(8,128)(2,1)S(1)}, u32[]{:S(2)}, u32[]{:S(2)}) %collective-permute-start.20) | collective-permute-done | bytes 57376 | tf_op jit(solution)/shard_map/ppermute | solution.py:297
  (97 shorter events, 7.5 us)
Async XLA Ops:
  3.3 16.0 %collective-permute-start = (bf16[32,1920]{1,0:T(8,128)(2,1)S(1)}, bf16[32,1920]{1,0:T(8,128)(2,1)S(1)}, u32[]{:S(2)}, u32[]{:S(2)}) collective-permute-start(bf16[32,1920]{1,0:T(8,128)(2,1)S(1)} %pad_maximum_fusion.1), channel_id=1, source_target_pairs={{0,4},{1,5},{2,6},{3,7},{4,0},{5,1},{6,2},{7,3},{8,12},{9,13},{10,... | collective-permute-start | bytes 368648 | tf_op jit(solution)/shard_map/ppermute | solution.py:297
  7.4 11.9 %collective-permute-start.1 = (bf16[32,1920]{1,0:T(8,128)(2,1)S(1)}, bf16[32,1920]{1,0:T(8,128)(2,1)S(1)}, u32[]{:S(2)}, u32[]{:S(2)}) collective-permute-start(bf16[32,1920]{1,0:T(8,128)(2,1)S(1)} %pad_maximum_fusion.1), channel_id=1, source_target_pairs={{0,2},{1,3},{2,0},{3,1},{4,6},{5,7},{6,4},{7,5},{8,10},{9,11},{10,... | collective-permute-start | bytes 368648 | tf_op jit(solution)/shard_map/ppermute | solution.py:297
  9.0 10.3 %collective-permute-start.2 = (bf16[32,1920]{1,0:T(8,128)(2,1)S(1)}, bf16[32,1920]{1,0:T(8,128)(2,1)S(1)}, u32[]{:S(2)}, u32[]{:S(2)}) collective-permute-start(bf16[32,1920]{1,0:T(8,128)(2,1)S(1)} %pad_maximum_fusion.1), channel_id=1, source_target_pairs={{0,6},{1,7},{2,4},{3,5},{4,2},{5,3},{6,0},{7,1},{8,14},{9,15},{10,... | collective-permute-start | bytes 368648 | tf_op jit(solution)/shard_map/ppermute | solution.py:297
  9.8 11.6 %copy-start.5 = (bf16[2,256,8]{1,2,0:T(8,128)(2,1)S(1)}, bf16[2,256,8]{1,2,0:T(8,128)(2,1)}, u32[]{:S(2)}) copy-start(bf16[2,256,8]{1,2,0:T(8,128)(2,1)} %param.19) | copy-start | bytes 24580
  19.5 13.5 %collective-permute-start.3 = (bf16[128,1024]{1,0:T(8,128)(2,1)S(1)}, bf16[128,1024]{1,0:T(8,128)(2,1)S(1)}, u32[]{:S(2)}, u32[]{:S(2)}) collective-permute-start(bf16[128,1024]{1,0:T(8,128)(2,1)S(1)} %pad_maximum_fusion), channel_id=1, source_target_pairs={{0,1},{1,0},{2,3},{3,2},{4,5},{5,4},{6,7},{7,6},{8,9},{9,8},{10,11... | collective-permute-start | bytes 786440 | tf_op jit(solution)/shard_map/ppermute | solution.py:297
  21.3 11.6 %collective-permute-start.4 = (bf16[128,896]{1,0:T(8,128)(2,1)S(1)}, bf16[128,896]{1,0:T(8,128)(2,1)S(1)}, u32[]{:S(2)}, u32[]{:S(2)}) collective-permute-start(bf16[128,896]{1,0:T(8,128)(2,1)S(1)} %get-tuple-element.46), channel_id=1, source_target_pairs={{0,16},{8,24},{16,0},{24,8},{1,17},{9,25},{17,1},{25,9},{2,18},{10... | collective-permute-start | bytes 688136 | tf_op jit(solution)/shard_map/ppermute | solution.py:297
  22.9 22.3 %collective-permute-start.6 = (bf16[128,896]{1,0:T(8,128)(2,1)S(1)}, bf16[128,896]{1,0:T(8,128)(2,1)S(1)}, u32[]{:S(2)}, u32[]{:S(2)}) collective-permute-start(bf16[128,896]{1,0:T(8,128)(2,1)S(1)} %get-tuple-element.46), channel_id=1, source_target_pairs={{0,1},{1,0},{2,3},{3,2},{4,5},{5,4},{6,7},{7,6},{8,9},{9,8},{10,11... | collective-permute-start | bytes 688136 | tf_op jit(solution)/shard_map/ppermute | solution.py:297
  33.1 12.1 %collective-permute-start.5 = (bf16[256,896]{1,0:T(8,128)(2,1)S(1)}, bf16[256,896]{1,0:T(8,128)(2,1)S(1)}, u32[]{:S(2)}, u32[]{:S(2)}) collective-permute-start(bf16[256,896]{1,0:T(8,128)(2,1)S(1)} %slice.113.refs_5_), channel_id=1, source_target_pairs={{0,16},{8,24},{16,0},{24,8},{1,17},{9,25},{17,1},{25,9},{2,18},{10... | collective-permute-start | bytes 1376264 | tf_op jit(solution)/shard_map/ppermute | solution.py:297
  33.5 22.6 %collective-permute-start.8 = (bf16[256,896]{1,0:T(8,128)(2,1)S(1)}, bf16[256,896]{1,0:T(8,128)(2,1)S(1)}, u32[]{:S(2)}, u32[]{:S(2)}) collective-permute-start(bf16[256,896]{1,0:T(8,128)(2,1)S(1)} %slice.113.refs_5_), channel_id=1, source_target_pairs={{0,8},{8,0},{16,24},{24,16},{1,9},{9,1},{17,25},{25,17},{2,10},{10... | collective-permute-start | bytes 1376264 | tf_op jit(solution)/shard_map/ppermute | solution.py:297
  33.5 11.7 %collective-permute-start.7 = (bf16[128,896]{1,0:T(8,128)(2,1)S(1)}, bf16[128,896]{1,0:T(8,128)(2,1)S(1)}, u32[]{:S(2)}, u32[]{:S(2)}) collective-permute-start(bf16[128,896]{1,0:T(8,128)(2,1)S(1)} %collective-permute-done.4), channel_id=1, source_target_pairs={{0,1},{1,0},{2,3},{3,2},{4,5},{5,4},{6,7},{7,6},{8,9},{9,8},{10,11... | collective-permute-start | bytes 688136 | tf_op jit(solution)/shard_map/ppermute | solution.py:297
  45.2 10.9 %collective-permute-start.9 = (bf16[256,896]{1,0:T(8,128)(2,1)S(1)}, bf16[256,896]{1,0:T(8,128)(2,1)S(1)}, u32[]{:S(2)}, u32[]{:S(2)}) collective-permute-start(bf16[256,896]{1,0:T(8,128)(2,1)S(1)} %constant_dynamic-update-slice_fusion.6.refs_6_), channel_id=1, source_target_pairs={{0,8},{8,0},{16,24},{24,16},{1,9},{9,1},{17,25},{25,17},{2,10},{10... | collective-permute-start | bytes 1376264 | tf_op jit(solution)/shard_map/ppermute | solution.py:297
  45.5 10.6 %collective-permute-start.10 = (bf16[256,896]{1,0:T(8,128)(2,1)S(1)}, bf16[256,896]{1,0:T(8,128)(2,1)S(1)}, u32[]{:S(2)}, u32[]{:S(2)}) collective-permute-start(bf16[256,896]{1,0:T(8,128)(2,1)S(1)} %collective-permute-done.5.refs_7_), channel_id=1, source_target_pairs={{0,8},{8,0},{16,24},{24,16},{1,9},{9,1},{17,25},{25,17},{2,10},{10... | collective-permute-start | bytes 1376264 | tf_op jit(solution)/shard_map/ppermute | solution.py:297
  45.8 10.3 %collective-permute-start.11 = (bf16[256,896]{1,0:T(8,128)(2,1)S(1)}, bf16[256,896]{1,0:T(8,128)(2,1)S(1)}, u32[]{:S(2)}, u32[]{:S(2)}) collective-permute-start(bf16[256,896]{1,0:T(8,128)(2,1)S(1)} %constant_dynamic-update-slice_fusion.8.refs_8_), channel_id=1, source_target_pairs={{0,8},{8,0},{16,24},{24,16},{1,9},{9,1},{17,25},{25,17},{2,10},{10... | collective-permute-start | bytes 1376264 | tf_op jit(solution)/shard_map/ppermute | solution.py:297
  46.2 27.2 %slice-start = ((s8[7340032]{0:T(1024)(128)(4,1)}), s8[4194304]{0:T(1024)(128)(4,1)S(1)}, s32[]{:S(2)}) async-start(s8[7340032]{0:T(1024)(128)(4,1)} %bitcast.7), calls=%async_computation | async-start | bytes 8388608
  46.4 10.5 %copy-start = (s32[1,2,7168]{2,1,0:T(2,128)S(1)}, s32[1,2,7168]{2,1,0:T(2,128)}, u32[]{:S(2)}) copy-start(s32[1,2,7168]{2,1,0:T(2,128)} %signs_ref.9) | copy-start | bytes 172036
  46.4 10.5 %copy-start.2 = (bf16[128,128]{1,0:T(8,128)(2,1)S(1)}, bf16[128,128]{1,0:T(8,128)(2,1)}, u32[]{:S(2)}) copy-start(bf16[128,128]{1,0:T(8,128)(2,1)} %constant.33.clone.refs_15_) | copy-start | bytes 98308
  46.4 10.5 %copy-start.3 = (s32[1,1024]{1,0:T(1,128)S(1)}, s32[1,1024]{1,0:T(1,128)}, u32[]{:S(2)}) copy-start(s32[1,1024]{1,0:T(1,128)} %refs_14_.1) | copy-start | bytes 12292
  46.4 27.0 %slice-start.1 = ((s8[7340032]{0:T(1024)(128)(4,1)}), s8[3145728]{0:T(1024)(128)(4,1)S(1)}, s32[]{:S(2)}) async-start(s8[7340032]{0:T(1024)(128)(4,1)} %bitcast.7), calls=%async_computation.1 | async-start | bytes 6291456
  56.1 17.3 %copy-start.1 = (bf16[128,128]{1,0:T(8,128)(2,1)S(1)}, bf16[128,128]{1,0:T(8,128)(2,1)}, u32[]{:S(2)}) copy-start(bf16[128,128]{1,0:T(8,128)(2,1)} %constant.34.clone.had_ref) | copy-start | bytes 98308
  56.1 0.8 copy-start.4
  79.1 6.0 %collective-permute-start.12 = (bf16[256,1792]{1,0:T(8,128)(2,1)S(1)}, bf16[256,1792]{1,0:T(8,128)(2,1)S(1)}, u32[]{:S(2)}, u32[]{:S(2)}) collective-permute-start(bf16[256,1792]{1,0:T(8,128)(2,1)S(1)} %produce.5), channel_id=1, source_target_pairs={{0,8},{8,0},{16,24},{24,16},{1,9},{9,1},{17,25},{25,17},{2,10},{10... | collective-permute-start | bytes 2752520 | tf_op jit(solution)/shard_map/ppermute | solution.py:297
  85.4 8.0 %collective-permute-start.13 = (bf16[128,896]{1,0:T(8,128)(2,1)S(1)}, bf16[128,896]{1,0:T(8,128)(2,1)S(1)}, u32[]{:S(2)}, u32[]{:S(2)}) collective-permute-start(bf16[128,896]{1,0:T(8,128)(2,1)S(1)} %get-tuple-element.60), channel_id=1, source_target_pairs={{0,1},{1,0},{2,3},{3,2},{4,5},{5,4},{6,7},{7,6},{8,9},{9,8},{10,11... | collective-permute-start | bytes 688136 | tf_op jit(solution)/shard_map/ppermute | solution.py:297
  85.8 7.6 %collective-permute-start.14 = (bf16[256,384]{1,0:T(8,128)(2,1)S(1)}, bf16[256,384]{1,0:T(8,128)(2,1)S(1)}, u32[]{:S(2)}, u32[]{:S(2)}) collective-permute-start(bf16[256,384]{1,0:T(8,128)(2,1)S(1)} %slice.117), channel_id=1, source_target_pairs={{0,16},{8,24},{16,0},{24,8},{1,17},{9,25},{17,1},{25,9},{2,18},{10... | collective-permute-start | bytes 589832 | tf_op jit(solution)/shard_map/ppermute | solution.py:297
  93.4 4.6 %collective-permute-start.15 = (bf16[256,1792]{1,0:T(8,128)(2,1)S(1)}, bf16[256,1792]{1,0:T(8,128)(2,1)S(1)}, u32[]{:S(2)}, u32[]{:S(2)}) collective-permute-start(bf16[256,1792]{1,0:T(8,128)(2,1)S(1)} %produce.7), channel_id=1, source_target_pairs={{0,8},{8,0},{16,24},{24,16},{1,9},{9,1},{17,25},{25,17},{2,10},{10... | collective-permute-start | bytes 2752520 | tf_op jit(solution)/shard_map/ppermute | solution.py:297
  93.5 12.5 %collective-permute-start.17 = (bf16[256,512]{1,0:T(8,128)(2,1)S(1)}, bf16[256,512]{1,0:T(8,128)(2,1)S(1)}, u32[]{:S(2)}, u32[]{:S(2)}) collective-permute-start(bf16[256,512]{1,0:T(8,128)(2,1)S(1)} %slice.118), channel_id=1, source_target_pairs={{0,16},{8,24},{16,0},{24,8},{1,17},{9,25},{17,1},{25,9},{2,18},{10... | collective-permute-start | bytes 786440 | tf_op jit(solution)/shard_map/ppermute | solution.py:297
  98.2 7.8 %collective-permute-start.16 = (bf16[128,896]{1,0:T(8,128)(2,1)S(1)}, bf16[128,896]{1,0:T(8,128)(2,1)S(1)}, u32[]{:S(2)}, u32[]{:S(2)}) collective-permute-start(bf16[128,896]{1,0:T(8,128)(2,1)S(1)} %slice.159), channel_id=1, source_target_pairs={{0,1},{1,0},{2,3},{3,2},{4,5},{5,4},{6,7},{7,6},{8,9},{9,8},{10,11... | collective-permute-start | bytes 688136 | tf_op jit(solution)/shard_map/ppermute | solution.py:297
  99.3 7.9 %collective-permute-start.21 = (bf16[128,896]{1,0:T(8,128)(2,1)S(1)}, bf16[128,896]{1,0:T(8,128)(2,1)S(1)}, u32[]{:S(2)}, u32[]{:S(2)}) collective-permute-start(bf16[128,896]{1,0:T(8,128)(2,1)S(1)} %add_convert_fusion.1), channel_id=1, source_target_pairs={{0,16},{8,24},{16,0},{24,8},{1,17},{9,25},{17,1},{25,9},{2,18},{10... | collective-permute-start | bytes 688136 | tf_op jit(solution)/shard_map/ppermute | solution.py:297
  106.2 7.0 %collective-permute-start.18 = (bf16[128,896]{1,0:T(8,128)(2,1)S(1)}, bf16[128,896]{1,0:T(8,128)(2,1)S(1)}, u32[]{:S(2)}, u32[]{:S(2)}) collective-permute-start(bf16[128,896]{1,0:T(8,128)(2,1)S(1)} %slice.158), channel_id=1, source_target_pairs={{0,1},{1,0},{2,3},{3,2},{4,5},{5,4},{6,7},{7,6},{8,9},{9,8},{10,11... | collective-permute-start | bytes 688136 | tf_op jit(solution)/shard_map/ppermute | solution.py:297
  107.4 6.6 %collective-permute-start.22 = (bf16[64,896]{1,0:T(8,128)(2,1)S(1)}, bf16[64,896]{1,0:T(8,128)(2,1)S(1)}, u32[]{:S(2)}, u32[]{:S(2)}) collective-permute-start(bf16[64,896]{1,0:T(8,128)(2,1)S(1)} %slice.160), channel_id=1, source_target_pairs={{0,2},{1,3},{2,0},{3,1},{4,6},{5,7},{6,4},{7,5},{8,10},{9,11},{10,... | collective-permute-start | bytes 344072 | tf_op jit(solution)/shard_map/ppermute | solution.py:297
  113.2 5.2 %collective-permute-start.19 = (bf16[64,896]{1,0:T(8,128)(2,1)S(1)}, bf16[64,896]{1,0:T(8,128)(2,1)S(1)}, u32[]{:S(2)}, u32[]{:S(2)}) collective-permute-start(bf16[64,896]{1,0:T(8,128)(2,1)S(1)} %slice.161), channel_id=1, source_target_pairs={{0,2},{1,3},{2,0},{3,1},{4,6},{5,7},{6,4},{7,5},{8,10},{9,11},{10,... | collective-permute-start | bytes 344072 | tf_op jit(solution)/shard_map/ppermute | solution.py:297
  114.0 7.5 %collective-permute-start.23 = (bf16[32,896]{1,0:T(8,128)(2,1)S(1)}, bf16[32,896]{1,0:T(8,128)(2,1)S(1)}, u32[]{:S(2)}, u32[]{:S(2)}) collective-permute-start(bf16[32,896]{1,0:T(8,128)(2,1)S(1)} %slice.162), channel_id=1, source_target_pairs={{0,4},{1,5},{2,6},{3,7},{4,0},{5,1},{6,2},{7,3},{8,12},{9,13},{10,... | collective-permute-start | bytes 172040 | tf_op jit(solution)/shard_map/ppermute | solution.py:297
  118.5 5.1 %collective-permute-start.20 = (bf16[32,896]{1,0:T(8,128)(2,1)S(1)}, bf16[32,896]{1,0:T(8,128)(2,1)S(1)}, u32[]{:S(2)}, u32[]{:S(2)}) collective-permute-start(bf16[32,896]{1,0:T(8,128)(2,1)S(1)} %slice.163), channel_id=1, source_target_pairs={{0,4},{1,5},{2,6},{3,7},{4,0},{5,1},{6,2},{7,3},{8,12},{9,13},{10,... | collective-permute-start | bytes 172040 | tf_op jit(solution)/shard_map/ppermute | solution.py:297

commit v5 on v4

--- a/solution.py
+++ b/solution.py
@@ -217,7 +217,7 @@
     group = tables.shape[1]
     slots, hidden = folded.shape
     token_total = spread.shape[0]
-    per_quarter = width // sections // cols
+    quarter = width // sections
     tile = 2 * LANES
     pair = 2
 
@@ -268,7 +268,7 @@
         finish(*pending)
 
     def column(s):
-        return jnp.bitwise_xor(s[0], order) * per_quarter + at_col
+        return pl.multiple_of(jnp.bitwise_xor(s[0], order) * quarter + at_col, LANES)
 
     whole = lambda shape: pl.BlockSpec(shape, lambda j, s: (0,) * len(shape))
     return pl.pallas_call(
@@ -277,10 +277,15 @@
             num_scalar_prefetch=1,
             grid=(1,),
             in_specs=[
-                pl.BlockSpec((1, books, groups, cols), lambda j, s: (0, 0, 0, column(s))),
+                pl.BlockSpec(
+                    tuple(pl.Element(n) for n in (1, books, groups, cols)),
+                    lambda j, s: (0, 0, 0, column(s)),
+                ),
                 whole(tables.shape),
                 whole(folded.shape),
-                pl.BlockSpec((1, 2, cols), lambda j, s: (0, 0, column(s))),
+                pl.BlockSpec(
+                    tuple(pl.Element(n) for n in (1, 2, cols)), lambda j, s: (0, 0, column(s))
+                ),
                 whole(had.shape),
                 whole(spread.shape),
             ],
@@ -427,41 +432,41 @@
     across = make(2)
     folded, across, given = fence(folded, across, given)
     across = across.astype(f32) + given.astype(f32)
-    early = half // LANES // 2 * LANES
-    first_across = [across[:, :early].astype(bf16), across[:, early:half].astype(bf16)]
-    second_met = across[rows:, half:].astype(bf16)
-    second_kept = across[:rows, half:].astype(bf16)
-    folded, *first_across, second_met, second_kept = fence(
-        folded, *first_across, second_met, second_kept
-    )
-    first_across = [swap(f, "sec", 2) for f in first_across]
+    lead = quarter // LANES // 3 * LANES
+    first_across = across[:, :lead].astype(bf16)
+    second_met = across[rows:, lead:].astype(bf16)
+    second_kept = across[:rows, lead:].astype(bf16)
+    folded, first_across, second_met, second_kept = fence(
+        folded, first_across, second_met, second_kept
+    )
+    first_across = swap(first_across, "sec", 2)
     second_met = swap(second_met, "dev", 1)
     beside = make(1)
-    folded, beside, second_met, first_across[0] = fence(
-        folded, beside, second_met, first_across[0]
-    )
+    folded, beside, second_met, first_across = fence(folded, beside, second_met, first_across)
     beside = swap(beside, "sec", 1)
     second_across = (second_kept.astype(f32) + second_met.astype(f32)).astype(bf16)
     second_across = swap(second_across, "sec", 2)
-    second = make(0, half, 1, f32)
+    second = make(0, quarter - lead, lead, f32)
     folded, second, beside = fence(folded, second, beside)
-    second = second + beside[:, half:].astype(f32)
+    second = second + beside[:, lead:].astype(f32)
     second_near = swap(second[rows:].astype(bf16), "dev", 1)
-    first = make(0, half, 0, f32)
-    first, second_near = fence(first, second_near)
-    first_across = jnp.concatenate(first_across, 1)
-    first = first + beside[:, :half].astype(f32) + first_across.astype(f32)
+    first = make(0, lead, 0, f32)
+    first, second_near, second_across = fence(first, second_near, second_across)
+    first = first + beside[:, :lead].astype(f32) + first_across.astype(f32)
     first_near = swap(first[rows:].astype(bf16), "dev", 1)
     second = second[:rows] + second_near.astype(f32) + second_across.astype(f32)
-    first = first[:rows] + first_near.astype(f32)
-    outs = []
-    for total in (first, second):
-        for stride in strides[1:]:
-            rows = total.shape[0] // 2
-            sent = swap(total[rows:].astype(bf16), "dev", stride)
-            total = total[:rows] + sent.astype(f32)
-        outs.append(total.astype(bf16))
-    return jnp.concatenate(outs, 1)
+
+    def halve(total, stride):
+        count = total.shape[0] // 2
+        sent = swap(total[count:].astype(bf16), "dev", stride)
+        return total[:count] + sent.astype(f32)
+
+    second = halve(second, strides[1])
+    first_near, second = fence(first_near, second)
+    first = halve(first[:rows] + first_near.astype(f32), strides[1])
+    for stride in strides[2:]:
+        second, first = halve(second, stride), halve(first, stride)
+    return jnp.concatenate([first.astype(bf16), second.astype(bf16)], 1)
 
 
 def solution(mesh):

time: 125 us -> 129 us (1.032)
  waiting for transfers between devices: 11.3 us -> 16 us
    ppermute x24 -> x23, waiting for transfers between devices: 11.3 us -> 16 us  [swap(): return lax.ppermute(values, axis, [(i, i ^ stride) for i in range(size)])]
    ppermute x24 -> x23, starting transfers between devices: 26.7 us -> 25.8 us  [swap(): return lax.ppermute(values, axis, [(i, i ^ stride) for i in range(size)])]
  transfers between devices with their start and end apart: 24 -> 23, of which waited for: 5 -> 8; matrix products, arithmetic and copies ran while one was open for 2% -> 2% of each run, Pallas kernels for 45% -> 44%
where the time goes in v5:
time: 129 us; the launch traced here: 128 us
  Pallas kernels  78.7 us (61%)
  starting transfers between devices  25.8 us (20%)
  waiting for transfers between devices  16 us (12%)
  other arithmetic  4.49 us (3%)
  local copies, waits for them, and re-layouts  2.91 us (2%)
    pallas_call x4, Pallas kernels, decode_in(): pl.pallas_call(body, grid_spec=pltpu.PrefetchScalarGridSpec(num_scalar_pr...  38.4 us
    ppermute x23, starting transfers between devices, swap(): return lax.ppermute(values, axis, [(i, i ^ stride) for i in range(size)])  25.8 us
    pallas_call x5, Pallas kernels, produce(): pl.pallas_call(body, grid_spec=pltpu.PrefetchScalarGridSpec(num_scalar_pr...  23.9 us
    pallas_call x1, Pallas kernels, project(): pl.pallas_call(body, grid_spec=pltpu.PrefetchScalarGridSpec(num_scalar_pr...  16.4 us
    ppermute x23, waiting for transfers between devices, swap(): return lax.ppermute(values, axis, [(i, i ^ stride) for i in range(size)])  16 us
  transfers between devices with their start and end apart: 23, of which 8 were waited for; matrix products, arithmetic and copies ran while one was open for 2% of the time, Pallas kernels for 44%

profile of v5, /device:TPU:0, one launch (start us, length us, event | category | flops | bytes accessed | tf_op | source)
XLA Modules:
  0.0 128.4 jit_solution(5102510311466223318)
XLA Ops:
  0.0 0.8 copy.25
  0.8 0.7 reduce_sum.27
  2.4 0.9 pad_maximum_fusion.1
  3.3 4.1 %collective-permute-start = (bf16[32,1920]{1,0:T(8,128)(2,1)S(1)}, bf16[32,1920]{1,0:T(8,128)(2,1)S(1)}, u32[]{:S(2)}, u32[]{:S(2)}) collective-permute-start(bf16[32,1920]{1,0:T(8,128)(2,1)S(1)} %pad_maximum_fusion.1), channel_id=1, source_target_pairs={{0,4},{1,5},{2,6},{3,7},{4,0},{5,1},{6,2},{7,3},{8,12},{9,13},{10,... | collective-permute-start | bytes 368648 | tf_op jit(solution)/shard_map/ppermute | solution.py:302
  7.4 1.6 %collective-permute-start.1 = (bf16[32,1920]{1,0:T(8,128)(2,1)S(1)}, bf16[32,1920]{1,0:T(8,128)(2,1)S(1)}, u32[]{:S(2)}, u32[]{:S(2)}) collective-permute-start(bf16[32,1920]{1,0:T(8,128)(2,1)S(1)} %pad_maximum_fusion.1), channel_id=1, source_target_pairs={{0,2},{1,3},{2,0},{3,1},{4,6},{5,7},{6,4},{7,5},{8,10},{9,11},{10,... | collective-permute-start | bytes 368648 | tf_op jit(solution)/shard_map/ppermute | solution.py:302
  9.0 0.7 copy.24
  9.8 9.5 %decode_in.4.rest_0_ = bf16[2,5376,1024]{2,1,0:T(8,128)(2,1)} custom-call(s32[1]{0:T(128)} %bitcast.section_ref.refs_0_, s32[1,2,2,896,1024]{4,3,2,1,0:T(8,128)} %refs_1_.1, bf16[2,2,8,2,16,128]{5,4,3,2,1,0:T(8,128)(2,1)S(1)} %broadcast_in_dim.63.tables_ref.refs_2_), custom_call_target="tpu_custom_call" | custom-call | tf_op jit(solution)/shard_map/decode_in/pallas_call | solution.py:108
  19.5 1.8 %collective-permute-start.3 = (bf16[128,1024]{1,0:T(8,128)(2,1)S(1)}, bf16[128,1024]{1,0:T(8,128)(2,1)S(1)}, u32[]{:S(2)}, u32[]{:S(2)}) collective-permute-start(bf16[128,1024]{1,0:T(8,128)(2,1)S(1)} %pad_maximum_fusion), channel_id=1, source_target_pairs={{0,1},{1,0},{2,3},{3,2},{4,5},{5,4},{6,7},{7,6},{8,9},{9,8},{10,11... | collective-permute-start | bytes 786440 | tf_op jit(solution)/shard_map/ppermute | solution.py:302
  21.3 1.6 %collective-permute-start.4 = (bf16[128,896]{1,0:T(8,128)(2,1)S(1)}, bf16[128,896]{1,0:T(8,128)(2,1)S(1)}, u32[]{:S(2)}, u32[]{:S(2)}) collective-permute-start(bf16[128,896]{1,0:T(8,128)(2,1)S(1)} %get-tuple-element.48), channel_id=1, source_target_pairs={{0,16},{8,24},{16,0},{24,8},{1,17},{9,25},{17,1},{25,9},{2,18},{10... | collective-permute-start | bytes 688136 | tf_op jit(solution)/shard_map/ppermute | solution.py:302
  23.4 9.5 %decode_in.5.rest_0_ = bf16[2,5376,1024]{2,1,0:T(8,128)(2,1)} custom-call(s32[1]{0:T(128)} %bitcast.section_ref.refs_0_, s32[1,2,2,896,1024]{4,3,2,1,0:T(8,128)} %refs_1_.1, bf16[2,2,8,2,16,128]{5,4,3,2,1,0:T(8,128)(2,1)S(1)} %broadcast_in_dim.63.tables_ref.refs_2_, bf16[2,5376,1024]{2,1,0:T(8,128)(2,1)} %decode_in.4.rest_0_), custom_call_target="tpu_custom_call", output_to_operand_aliasing={{}: (3, {})} | custom-call | tf_op jit(solution)/shard_map/decode_in/pallas_call | solution.py:108
  33.6 1.6 %collective-permute-start.7 = (bf16[128,896]{1,0:T(8,128)(2,1)S(1)}, bf16[128,896]{1,0:T(8,128)(2,1)S(1)}, u32[]{:S(2)}, u32[]{:S(2)}) collective-permute-start(bf16[128,896]{1,0:T(8,128)(2,1)S(1)} %collective-permute-done.4), channel_id=1, source_target_pairs={{0,1},{1,0},{2,3},{3,2},{4,5},{5,4},{6,7},{7,6},{8,9},{9,8},{10,11... | collective-permute-start | bytes 688136 | tf_op jit(solution)/shard_map/ppermute | solution.py:302
  35.7 9.6 %decode_in.6.rest_0_ = bf16[2,5376,1024]{2,1,0:T(8,128)(2,1)} custom-call(s32[1]{0:T(128)} %bitcast.section_ref.refs_0_, s32[1,2,2,896,1024]{4,3,2,1,0:T(8,128)} %refs_1_.1, bf16[2,2,8,2,16,128]{5,4,3,2,1,0:T(8,128)(2,1)S(1)} %broadcast_in_dim.63.tables_ref.refs_2_, bf16[2,5376,1024]{2,1,0:T(8,128)(2,1)} %decode_in.5.rest_0_), custom_call_target="tpu_custom_call", output_to_operand_aliasing={{}: (3, {})} | custom-call | tf_op jit(solution)/shard_map/decode_in/pallas_call | solution.py:108
  46.6 9.7 %decode_in.7.refs_3_ = bf16[2,5376,1024]{2,1,0:T(8,128)(2,1)} custom-call(s32[1]{0:T(128)} %bitcast.section_ref.refs_0_, s32[1,2,2,896,1024]{4,3,2,1,0:T(8,128)} %refs_1_.1, bf16[2,2,8,2,16,128]{5,4,3,2,1,0:T(8,128)(2,1)S(1)} %broadcast_in_dim.63.tables_ref.refs_2_, bf16[2,5376,1024]{2,1,0:T(8,128)(2,1)} %decode_in.6.rest_0_), custom_call_target="tpu_custom_call", output_to_operand_aliasing={{}: (3, {})} | custom-call | tf_op jit(solution)/shard_map/decode_in/pallas_call | solution.py:108
  56.3 0.8 copy-done.4
  57.1 16.4 %project.1.folded_ref = bf16[128,1024]{1,0:T(8,128)(2,1)S(1)} custom-call(s32[1]{0:T(128)} %bitcast.section_ref.refs_0_, s32[1,2,2,896,1024]{4,3,2,1,0:T(8,128)} %refs_1_.1, bf16[2,2,8,2,16,128]{5,4,3,2,1,0:T(8,128)(2,1)S(1)} %broadcast_in_dim.63.tables_ref.refs_2_, bf16[2,5376,1024]{2,1,0:T(8,128)(2,1)} %decode_in.7.refs_3_, ...), custom_call_target="tpu_custom_call" | custom-call | tf_op jit(solution)/shard_map/project/pallas_call | solution.py:186
  73.6 5.7 %produce.5 = bf16[256,1792]{1,0:T(8,128)(2,1)S(1)} custom-call(s32[1]{0:T(128)} %bitcast.section_ref.refs_0_, s32[1,2,128,7168]{3,2,1,0:T(8,128)S(1)} %bitcast.8, bf16[2,8,2,16,128]{4,3,2,1,0:T(8,128)(2,1)S(1)} %broadcast_in_dim.61.tables_ref, bf16[128,1024]{1,0:T(8,128)(2,1)S(1)} %project.1.folded_ref, s32[1,2,7168]{2,1,0:T(2,128)S(1)} %copy-done, ...), custom_call_target="tpu_custom_call" | custom-call | tf_op jit(solution)/shard_map/produce/pallas_call | solution.py:274
  79.6 5.7 %produce.6 = bf16[256,1792]{1,0:T(8,128)(2,1)S(1)} custom-call(s32[1]{0:T(128)} %bitcast.section_ref.refs_0_, s32[1,2,128,7168]{3,2,1,0:T(8,128)S(1)} %bitcast.8, bf16[2,8,2,16,128]{4,3,2,1,0:T(8,128)(2,1)S(1)} %broadcast_in_dim.61.tables_ref, bf16[128,1024]{1,0:T(8,128)(2,1)S(1)} %project.1.folded_ref, s32[1,2,7168]{2,1,0:T(2,128)S(1)} %copy-done, ...), custom_call_target="tpu_custom_call" | custom-call | tf_op jit(solution)/shard_map/produce/pallas_call | solution.py:274
  86.0 1.6 %collective-permute-start.14 = (bf16[256,512]{1,0:T(8,128)(2,1)S(1)}, bf16[256,512]{1,0:T(8,128)(2,1)S(1)}, u32[]{:S(2)}, u32[]{:S(2)}) collective-permute-start(bf16[256,512]{1,0:T(8,128)(2,1)S(1)} %slice.112), channel_id=1, source_target_pairs={{0,16},{8,24},{16,0},{24,8},{1,17},{9,25},{17,1},{25,9},{2,18},{10... | collective-permute-start | bytes 786440 | tf_op jit(solution)/shard_map/ppermute | solution.py:302
  87.6 5.9 %produce.7 = bf16[256,1792]{1,0:T(8,128)(2,1)S(1)} custom-call(s32[1]{0:T(128)} %bitcast.section_ref.refs_0_, s32[1,2,128,7168]{3,2,1,0:T(8,128)S(1)} %bitcast.8, bf16[2,8,2,16,128]{4,3,2,1,0:T(8,128)(2,1)S(1)} %broadcast_in_dim.61.tables_ref, bf16[128,1024]{1,0:T(8,128)(2,1)S(1)} %project.1.folded_ref, s32[1,2,7168]{2,1,0:T(2,128)S(1)} %copy-done, ...), custom_call_target="tpu_custom_call" | custom-call | tf_op jit(solution)/shard_map/produce/pallas_call | solution.py:274
  93.5 0.7 collective-permute-done.14
  94.3 1.3 collective-permute-done.13
  95.5 4.3 %produce.8 = f32[256,1280]{1,0:T(8,128)S(1)} custom-call(s32[1]{0:T(128)} %bitcast.section_ref.refs_0_, s32[1,2,128,7168]{3,2,1,0:T(8,128)S(1)} %bitcast.8, bf16[2,8,2,16,128]{4,3,2,1,0:T(8,128)(2,1)S(1)} %broadcast_in_dim.61.tables_ref, bf16[128,1024]{1,0:T(8,128)(2,1)S(1)} %project.1.folded_ref, s32[1,2,7168]{2,1,0:T(2,128)S(1)} %copy-done, ...), custom_call_target="tpu_custom_call" | custom-call | tf_op jit(solution)/shard_map/produce/pallas_call | solution.py:274
  100.0 1.6 %collective-permute-start.17 = (bf16[128,1280]{1,0:T(8,128)(2,1)S(1)}, bf16[128,1280]{1,0:T(8,128)(2,1)S(1)}, u32[]{:S(2)}, u32[]{:S(2)}) collective-permute-start(bf16[128,1280]{1,0:T(8,128)(2,1)S(1)} %add_convert_fusion.1), channel_id=1, source_target_pairs={{0,16},{8,24},{16,0},{24,8},{1,17},{9,25},{17,1},{25,9},{2,18},{10... | collective-permute-start | bytes 983048 | tf_op jit(solution)/shard_map/ppermute | solution.py:302
  102.2 2.3 %produce.9 = f32[256,512]{1,0:T(8,128)S(1)} custom-call(s32[1]{0:T(128)} %bitcast.section_ref.refs_0_, s32[1,2,128,7168]{3,2,1,0:T(8,128)S(1)} %bitcast.8, bf16[2,8,2,16,128]{4,3,2,1,0:T(8,128)(2,1)S(1)} %broadcast_in_dim.61.tables_ref, bf16[128,1024]{1,0:T(8,128)(2,1)S(1)} %project.1.folded_ref, s32[1,2,7168]{2,1,0:T(2,128)S(1)} %copy-done, ...), custom_call_target="tpu_custom_call" | custom-call | tf_op jit(solution)/shard_map/produce/pallas_call | solution.py:274
  104.6 5.6 %collective-permute-done.17 = bf16[128,1280]{1,0:T(8,128)(2,1)S(1)} collective-permute-done((bf16[128,1280]{1,0:T(8,128)(2,1)S(1)}, bf16[128,1280]{1,0:T(8,128)(2,1)S(1)}, u32[]{:S(2)}, u32[]{:S(2)}) %collective-permute-start.17) | collective-permute-done | bytes 327712 | tf_op jit(solution)/shard_map/ppermute | solution.py:302
  110.1 1.4 %collective-permute-done.16 = bf16[128,1280]{1,0:T(8,128)(2,1)S(1)} collective-permute-done((bf16[128,1280]{1,0:T(8,128)(2,1)S(1)}, bf16[128,1280]{1,0:T(8,128)(2,1)S(1)}, u32[]{:S(2)}, u32[]{:S(2)}) %collective-permute-start.16) | collective-permute-done | bytes 327712 | tf_op jit(solution)/shard_map/ppermute | solution.py:302
  111.7 0.7 collective-permute-start.19
  113.2 4.1 %collective-permute-done.19 = bf16[64,1280]{1,0:T(8,128)(2,1)S(1)} collective-permute-done((bf16[64,1280]{1,0:T(8,128)(2,1)S(1)}, bf16[64,1280]{1,0:T(8,128)(2,1)S(1)}, u32[]{:S(2)}, u32[]{:S(2)}) %collective-permute-start.19) | collective-permute-done | bytes 163872 | tf_op jit(solution)/shard_map/ppermute | solution.py:302
  117.7 1.4 %collective-permute-start.20 = (bf16[64,512]{1,0:T(8,128)(2,1)S(1)}, bf16[64,512]{1,0:T(8,128)(2,1)S(1)}, u32[]{:S(2)}, u32[]{:S(2)}) collective-permute-start(bf16[64,512]{1,0:T(8,128)(2,1)S(1)} %slice.153), channel_id=1, source_target_pairs={{0,2},{1,3},{2,0},{3,1},{4,6},{5,7},{6,4},{7,5},{8,10},{9,11},{10,... | collective-permute-start | bytes 196616 | tf_op jit(solution)/shard_map/ppermute | solution.py:302
  119.1 2.6 %collective-permute-start.22 = (bf16[32,1280]{1,0:T(8,128)(2,1)S(1)}, bf16[32,1280]{1,0:T(8,128)(2,1)S(1)}, u32[]{:S(2)}, u32[]{:S(2)}) collective-permute-start(bf16[32,1280]{1,0:T(8,128)(2,1)S(1)} %slice.152), channel_id=1, source_target_pairs={{0,4},{1,5},{2,6},{3,7},{4,0},{5,1},{6,2},{7,3},{8,12},{9,13},{10,... | collective-permute-start | bytes 245768 | tf_op jit(solution)/shard_map/ppermute | solution.py:302
  122.4 3.4 %collective-permute-start.21 = (bf16[32,512]{1,0:T(8,128)(2,1)S(1)}, bf16[32,512]{1,0:T(8,128)(2,1)S(1)}, u32[]{:S(2)}, u32[]{:S(2)}) collective-permute-start(bf16[32,512]{1,0:T(8,128)(2,1)S(1)} %slice.154), channel_id=1, source_target_pairs={{0,4},{1,5},{2,6},{3,7},{4,0},{5,1},{6,2},{7,3},{8,12},{9,13},{10,... | collective-permute-start | bytes 98312 | tf_op jit(solution)/shard_map/ppermute | solution.py:302
  125.8 1.9 %collective-permute-done.21 = bf16[32,512]{1,0:T(8,128)(2,1)S(1)} collective-permute-done((bf16[32,512]{1,0:T(8,128)(2,1)S(1)}, bf16[32,512]{1,0:T(8,128)(2,1)S(1)}, u32[]{:S(2)}, u32[]{:S(2)}) %collective-permute-start.21) | collective-permute-done | bytes 32800 | tf_op jit(solution)/shard_map/ppermute | solution.py:302
  (94 shorter events, 8.3 us)
Async XLA Ops:
  3.3 16.0 %collective-permute-start = (bf16[32,1920]{1,0:T(8,128)(2,1)S(1)}, bf16[32,1920]{1,0:T(8,128)(2,1)S(1)}, u32[]{:S(2)}, u32[]{:S(2)}) collective-permute-start(bf16[32,1920]{1,0:T(8,128)(2,1)S(1)} %pad_maximum_fusion.1), channel_id=1, source_target_pairs={{0,4},{1,5},{2,6},{3,7},{4,0},{5,1},{6,2},{7,3},{8,12},{9,13},{10,... | collective-permute-start | bytes 368648 | tf_op jit(solution)/shard_map/ppermute | solution.py:302
  7.4 11.9 %collective-permute-start.1 = (bf16[32,1920]{1,0:T(8,128)(2,1)S(1)}, bf16[32,1920]{1,0:T(8,128)(2,1)S(1)}, u32[]{:S(2)}, u32[]{:S(2)}) collective-permute-start(bf16[32,1920]{1,0:T(8,128)(2,1)S(1)} %pad_maximum_fusion.1), channel_id=1, source_target_pairs={{0,2},{1,3},{2,0},{3,1},{4,6},{5,7},{6,4},{7,5},{8,10},{9,11},{10,... | collective-permute-start | bytes 368648 | tf_op jit(solution)/shard_map/ppermute | solution.py:302
  9.0 10.3 %collective-permute-start.2 = (bf16[32,1920]{1,0:T(8,128)(2,1)S(1)}, bf16[32,1920]{1,0:T(8,128)(2,1)S(1)}, u32[]{:S(2)}, u32[]{:S(2)}) collective-permute-start(bf16[32,1920]{1,0:T(8,128)(2,1)S(1)} %pad_maximum_fusion.1), channel_id=1, source_target_pairs={{0,6},{1,7},{2,4},{3,5},{4,2},{5,3},{6,0},{7,1},{8,14},{9,15},{10,... | collective-permute-start | bytes 368648 | tf_op jit(solution)/shard_map/ppermute | solution.py:302
  19.3 2.0 %copy-start.5 = (bf16[2,256,8]{1,2,0:T(8,128)(2,1)S(1)}, bf16[2,256,8]{1,2,0:T(8,128)(2,1)}, u32[]{:S(2)}) copy-start(bf16[2,256,8]{1,2,0:T(8,128)(2,1)} %param.19) | copy-start | bytes 24580
  19.5 13.5 %collective-permute-start.3 = (bf16[128,1024]{1,0:T(8,128)(2,1)S(1)}, bf16[128,1024]{1,0:T(8,128)(2,1)S(1)}, u32[]{:S(2)}, u32[]{:S(2)}) collective-permute-start(bf16[128,1024]{1,0:T(8,128)(2,1)S(1)} %pad_maximum_fusion), channel_id=1, source_target_pairs={{0,1},{1,0},{2,3},{3,2},{4,5},{5,4},{6,7},{7,6},{8,9},{9,8},{10,11... | collective-permute-start | bytes 786440 | tf_op jit(solution)/shard_map/ppermute | solution.py:302
  21.3 11.6 %collective-permute-start.4 = (bf16[128,896]{1,0:T(8,128)(2,1)S(1)}, bf16[128,896]{1,0:T(8,128)(2,1)S(1)}, u32[]{:S(2)}, u32[]{:S(2)}) collective-permute-start(bf16[128,896]{1,0:T(8,128)(2,1)S(1)} %get-tuple-element.48), channel_id=1, source_target_pairs={{0,16},{8,24},{16,0},{24,8},{1,17},{9,25},{17,1},{25,9},{2,18},{10... | collective-permute-start | bytes 688136 | tf_op jit(solution)/shard_map/ppermute | solution.py:302
  22.9 22.4 %collective-permute-start.6 = (bf16[128,896]{1,0:T(8,128)(2,1)S(1)}, bf16[128,896]{1,0:T(8,128)(2,1)S(1)}, u32[]{:S(2)}, u32[]{:S(2)}) collective-permute-start(bf16[128,896]{1,0:T(8,128)(2,1)S(1)} %get-tuple-element.48), channel_id=1, source_target_pairs={{0,1},{1,0},{2,3},{3,2},{4,5},{5,4},{6,7},{7,6},{8,9},{9,8},{10,11... | collective-permute-start | bytes 688136 | tf_op jit(solution)/shard_map/ppermute | solution.py:302
  33.1 12.3 %collective-permute-start.5 = (bf16[256,896]{1,0:T(8,128)(2,1)S(1)}, bf16[256,896]{1,0:T(8,128)(2,1)S(1)}, u32[]{:S(2)}, u32[]{:S(2)}) collective-permute-start(bf16[256,896]{1,0:T(8,128)(2,1)S(1)} %slice.108.refs_5_), channel_id=1, source_target_pairs={{0,16},{8,24},{16,0},{24,8},{1,17},{9,25},{17,1},{25,9},{2,18},{10... | collective-permute-start | bytes 1376264 | tf_op jit(solution)/shard_map/ppermute | solution.py:302
  33.6 22.6 %collective-permute-start.8 = (bf16[256,896]{1,0:T(8,128)(2,1)S(1)}, bf16[256,896]{1,0:T(8,128)(2,1)S(1)}, u32[]{:S(2)}, u32[]{:S(2)}) collective-permute-start(bf16[256,896]{1,0:T(8,128)(2,1)S(1)} %slice.108.refs_5_), channel_id=1, source_target_pairs={{0,8},{8,0},{16,24},{24,16},{1,9},{9,1},{17,25},{25,17},{2,10},{10... | collective-permute-start | bytes 1376264 | tf_op jit(solution)/shard_map/ppermute | solution.py:302
  33.6 11.7 %collective-permute-start.7 = (bf16[128,896]{1,0:T(8,128)(2,1)S(1)}, bf16[128,896]{1,0:T(8,128)(2,1)S(1)}, u32[]{:S(2)}, u32[]{:S(2)}) collective-permute-start(bf16[128,896]{1,0:T(8,128)(2,1)S(1)} %collective-permute-done.4), channel_id=1, source_target_pairs={{0,1},{1,0},{2,3},{3,2},{4,5},{5,4},{6,7},{7,6},{8,9},{9,8},{10,11... | collective-permute-start | bytes 688136 | tf_op jit(solution)/shard_map/ppermute | solution.py:302
  35.7 37.9 %slice-start = ((s8[7340032]{0:T(1024)(128)(4,1)}), s8[4194304]{0:T(1024)(128)(4,1)S(1)}, s32[]{:S(2)}) async-start(s8[7340032]{0:T(1024)(128)(4,1)} %bitcast.7), calls=%async_computation | async-start | bytes 8388608
  45.4 10.9 %collective-permute-start.9 = (bf16[256,896]{1,0:T(8,128)(2,1)S(1)}, bf16[256,896]{1,0:T(8,128)(2,1)S(1)}, u32[]{:S(2)}, u32[]{:S(2)}) collective-permute-start(bf16[256,896]{1,0:T(8,128)(2,1)S(1)} %constant_dynamic-update-slice_fusion.6.refs_6_), channel_id=1, source_target_pairs={{0,8},{8,0},{16,24},{24,16},{1,9},{9,1},{17,25},{25,17},{2,10},{10... | collective-permute-start | bytes 1376264 | tf_op jit(solution)/shard_map/ppermute | solution.py:302
  45.7 10.6 %collective-permute-start.10 = (bf16[256,896]{1,0:T(8,128)(2,1)S(1)}, bf16[256,896]{1,0:T(8,128)(2,1)S(1)}, u32[]{:S(2)}, u32[]{:S(2)}) collective-permute-start(bf16[256,896]{1,0:T(8,128)(2,1)S(1)} %collective-permute-done.5.refs_7_), channel_id=1, source_target_pairs={{0,8},{8,0},{16,24},{24,16},{1,9},{9,1},{17,25},{25,17},{2,10},{10... | collective-permute-start | bytes 1376264 | tf_op jit(solution)/shard_map/ppermute | solution.py:302
  46.0 10.3 %collective-permute-start.11 = (bf16[256,896]{1,0:T(8,128)(2,1)S(1)}, bf16[256,896]{1,0:T(8,128)(2,1)S(1)}, u32[]{:S(2)}, u32[]{:S(2)}) collective-permute-start(bf16[256,896]{1,0:T(8,128)(2,1)S(1)} %constant_dynamic-update-slice_fusion.8.refs_8_), channel_id=1, source_target_pairs={{0,8},{8,0},{16,24},{24,16},{1,9},{9,1},{17,25},{25,17},{2,10},{10... | collective-permute-start | bytes 1376264 | tf_op jit(solution)/shard_map/ppermute | solution.py:302
  46.5 10.5 %copy-start = (s32[1,2,7168]{2,1,0:T(2,128)S(1)}, s32[1,2,7168]{2,1,0:T(2,128)}, u32[]{:S(2)}) copy-start(s32[1,2,7168]{2,1,0:T(2,128)} %signs_ref.9) | copy-start | bytes 172036
  46.5 10.5 %copy-start.2 = (bf16[128,128]{1,0:T(8,128)(2,1)S(1)}, bf16[128,128]{1,0:T(8,128)(2,1)}, u32[]{:S(2)}) copy-start(bf16[128,128]{1,0:T(8,128)(2,1)} %constant.33.clone.refs_15_) | copy-start | bytes 98308
  46.6 10.5 %copy-start.3 = (s32[1,1024]{1,0:T(1,128)S(1)}, s32[1,1024]{1,0:T(1,128)}, u32[]{:S(2)}) copy-start(s32[1,1024]{1,0:T(1,128)} %refs_14_.1) | copy-start | bytes 12292
  46.6 27.0 %slice-start.1 = ((s8[7340032]{0:T(1024)(128)(4,1)}), s8[3145728]{0:T(1024)(128)(4,1)S(1)}, s32[]{:S(2)}) async-start(s8[7340032]{0:T(1024)(128)(4,1)} %bitcast.7), calls=%async_computation.1 | async-start | bytes 6291456
  56.2 17.3 %copy-start.1 = (bf16[128,128]{1,0:T(8,128)(2,1)S(1)}, bf16[128,128]{1,0:T(8,128)(2,1)}, u32[]{:S(2)}) copy-start(bf16[128,128]{1,0:T(8,128)(2,1)} %constant.34.clone.had_ref) | copy-start | bytes 98308
  56.3 0.8 copy-start.4
  79.3 6.0 %collective-permute-start.12 = (bf16[256,1792]{1,0:T(8,128)(2,1)S(1)}, bf16[256,1792]{1,0:T(8,128)(2,1)S(1)}, u32[]{:S(2)}, u32[]{:S(2)}) collective-permute-start(bf16[256,1792]{1,0:T(8,128)(2,1)S(1)} %produce.5), channel_id=1, source_target_pairs={{0,8},{8,0},{16,24},{24,16},{1,9},{9,1},{17,25},{25,17},{2,10},{10... | collective-permute-start | bytes 2752520 | tf_op jit(solution)/shard_map/ppermute | solution.py:302
  85.5 10.0 %collective-permute-start.13 = (bf16[128,1280]{1,0:T(8,128)(2,1)S(1)}, bf16[128,1280]{1,0:T(8,128)(2,1)S(1)}, u32[]{:S(2)}, u32[]{:S(2)}) collective-permute-start(bf16[128,1280]{1,0:T(8,128)(2,1)S(1)} %get-tuple-element.62), channel_id=1, source_target_pairs={{0,1},{1,0},{2,3},{3,2},{4,5},{5,4},{6,7},{7,6},{8,9},{9,8},{10,11... | collective-permute-start | bytes 983048 | tf_op jit(solution)/shard_map/ppermute | solution.py:302
  86.0 8.2 %collective-permute-start.14 = (bf16[256,512]{1,0:T(8,128)(2,1)S(1)}, bf16[256,512]{1,0:T(8,128)(2,1)S(1)}, u32[]{:S(2)}, u32[]{:S(2)}) collective-permute-start(bf16[256,512]{1,0:T(8,128)(2,1)S(1)} %slice.112), channel_id=1, source_target_pairs={{0,16},{8,24},{16,0},{24,8},{1,17},{9,25},{17,1},{25,9},{2,18},{10... | collective-permute-start | bytes 786440 | tf_op jit(solution)/shard_map/ppermute | solution.py:302
  95.5 6.0 %collective-permute-start.15 = (bf16[256,1792]{1,0:T(8,128)(2,1)S(1)}, bf16[256,1792]{1,0:T(8,128)(2,1)S(1)}, u32[]{:S(2)}, u32[]{:S(2)}) collective-permute-start(bf16[256,1792]{1,0:T(8,128)(2,1)S(1)} %produce.7), channel_id=1, source_target_pairs={{0,8},{8,0},{16,24},{24,16},{1,9},{9,1},{17,25},{25,17},{2,10},{10... | collective-permute-start | bytes 2752520 | tf_op jit(solution)/shard_map/ppermute | solution.py:302
  100.0 10.2 %collective-permute-start.17 = (bf16[128,1280]{1,0:T(8,128)(2,1)S(1)}, bf16[128,1280]{1,0:T(8,128)(2,1)S(1)}, u32[]{:S(2)}, u32[]{:S(2)}) collective-permute-start(bf16[128,1280]{1,0:T(8,128)(2,1)S(1)} %add_convert_fusion.1), channel_id=1, source_target_pairs={{0,16},{8,24},{16,0},{24,8},{1,17},{9,25},{17,1},{25,9},{2,18},{10... | collective-permute-start | bytes 983048 | tf_op jit(solution)/shard_map/ppermute | solution.py:302
  101.7 9.9 %collective-permute-start.16 = (bf16[128,1280]{1,0:T(8,128)(2,1)S(1)}, bf16[128,1280]{1,0:T(8,128)(2,1)S(1)}, u32[]{:S(2)}, u32[]{:S(2)}) collective-permute-start(bf16[128,1280]{1,0:T(8,128)(2,1)S(1)} %slice.149), channel_id=1, source_target_pairs={{0,1},{1,0},{2,3},{3,2},{4,5},{5,4},{6,7},{7,6},{8,9},{9,8},{10,11... | collective-permute-start | bytes 983048 | tf_op jit(solution)/shard_map/ppermute | solution.py:302
  111.7 5.6 %collective-permute-start.19 = (bf16[64,1280]{1,0:T(8,128)(2,1)S(1)}, bf16[64,1280]{1,0:T(8,128)(2,1)S(1)}, u32[]{:S(2)}, u32[]{:S(2)}) collective-permute-start(bf16[64,1280]{1,0:T(8,128)(2,1)S(1)} %slice.150), channel_id=1, source_target_pairs={{0,2},{1,3},{2,0},{3,1},{4,6},{5,7},{6,4},{7,5},{8,10},{9,11},{10,... | collective-permute-start | bytes 491528 | tf_op jit(solution)/shard_map/ppermute | solution.py:302
  112.6 5.0 %collective-permute-start.18 = (bf16[128,512]{1,0:T(8,128)(2,1)S(1)}, bf16[128,512]{1,0:T(8,128)(2,1)S(1)}, u32[]{:S(2)}, u32[]{:S(2)}) collective-permute-start(bf16[128,512]{1,0:T(8,128)(2,1)S(1)} %slice.151), channel_id=1, source_target_pairs={{0,1},{1,0},{2,3},{3,2},{4,5},{5,4},{6,7},{7,6},{8,9},{9,8},{10,11... | collective-permute-start | bytes 393224 | tf_op jit(solution)/shard_map/ppermute | solution.py:302
  117.7 4.7 %collective-permute-start.20 = (bf16[64,512]{1,0:T(8,128)(2,1)S(1)}, bf16[64,512]{1,0:T(8,128)(2,1)S(1)}, u32[]{:S(2)}, u32[]{:S(2)}) collective-permute-start(bf16[64,512]{1,0:T(8,128)(2,1)S(1)} %slice.153), channel_id=1, source_target_pairs={{0,2},{1,3},{2,0},{3,1},{4,6},{5,7},{6,4},{7,5},{8,10},{9,11},{10,... | collective-permute-start | bytes 196616 | tf_op jit(solution)/shard_map/ppermute | solution.py:302
  119.1 6.7 %collective-permute-start.22 = (bf16[32,1280]{1,0:T(8,128)(2,1)S(1)}, bf16[32,1280]{1,0:T(8,128)(2,1)S(1)}, u32[]{:S(2)}, u32[]{:S(2)}) collective-permute-start(bf16[32,1280]{1,0:T(8,128)(2,1)S(1)} %slice.152), channel_id=1, source_target_pairs={{0,4},{1,5},{2,6},{3,7},{4,0},{5,1},{6,2},{7,3},{8,12},{9,13},{10,... | collective-permute-start | bytes 245768 | tf_op jit(solution)/shard_map/ppermute | solution.py:302
  122.4 5.3 %collective-permute-start.21 = (bf16[32,512]{1,0:T(8,128)(2,1)S(1)}, bf16[32,512]{1,0:T(8,128)(2,1)S(1)}, u32[]{:S(2)}, u32[]{:S(2)}) collective-permute-start(bf16[32,512]{1,0:T(8,128)(2,1)S(1)} %slice.154), channel_id=1, source_target_pairs={{0,4},{1,5},{2,6},{3,7},{4,0},{5,1},{6,2},{7,3},{8,12},{9,13},{10,... | collective-permute-start | bytes 98312 | tf_op jit(solution)/shard_map/ppermute | solution.py:302

commit v6 on v4

--- a/solution.py
+++ b/solution.py
@@ -121,10 +121,10 @@
 
 
 def rotate(values, table):
-    parts = []
-    for b in range(values.shape[1] // HAD):
-        parts.append((dot(values[:, b * HAD : (b + 1) * HAD], table) * UNIT).astype(bf16))
-    return jnp.concatenate(parts, 1)
+    rows, blocks = values.shape[0], values.shape[1] // HAD
+    tall = jnp.concatenate([values[:, b * HAD : (b + 1) * HAD] for b in range(blocks)], 0)
+    tall = (dot(tall, table) * UNIT).astype(bf16)
+    return jnp.concatenate([tall[b * rows : (b + 1) * rows] for b in range(blocks)], 1)
 
 
 def project(section, codes, tables, weights, pick, pieces, signs, middle, had, order, places):
@@ -454,14 +454,16 @@
     first_near = swap(first[rows:].astype(bf16), "dev", 1)
     second = second[:rows] + second_near.astype(f32) + second_across.astype(f32)
     first = first[:rows] + first_near.astype(f32)
-    outs = []
-    for total in (first, second):
-        for stride in strides[1:]:
-            rows = total.shape[0] // 2
-            sent = swap(total[rows:].astype(bf16), "dev", stride)
-            total = total[:rows] + sent.astype(f32)
-        outs.append(total.astype(bf16))
-    return jnp.concatenate(outs, 1)
+
+    def collect(total):
+        result = total[:token_count]
+        for at in range(1, devices // 2):
+            block = total[at * token_count : (at + 1) * token_count].astype(bf16)
+            result = result + swap(block, "dev", relative[at]).astype(f32)
+        return result.astype(bf16)
+
+    second = collect(second)
+    return jnp.concatenate([collect(first), second], 1)
 
 
 def solution(mesh):

time: 125 us -> 123 us (0.984)
  waiting for transfers between devices: 11.3 us -> 7.7 us
  starting transfers between devices: 26.7 us -> 28.7 us
    ppermute x24 -> x26, waiting for transfers between devices: 11.3 us -> 7.7 us  [swap(): return lax.ppermute(values, axis, [(i, i ^ stride) for i in range(size)])]
    ppermute x24 -> x26, starting transfers between devices: 26.7 us -> 28.7 us  [swap(): return lax.ppermute(values, axis, [(i, i ^ stride) for i in range(size)])]
  transfers between devices with their start and end apart: 24 -> 26, of which waited for: 5 -> 5; matrix products, arithmetic and copies ran while one was open for 2% -> 2% of each run, Pallas kernels for 45% -> 46%
where the time goes in v6:
time: 123 us; the launch traced here: 122 us
  Pallas kernels  78 us (63%)
  starting transfers between devices  28.7 us (23%)
  waiting for transfers between devices  7.7 us (6%)
  other arithmetic  4.47 us (4%)
  local copies, waits for them, and re-layouts  2.91 us (2%)
    pallas_call x4, Pallas kernels, decode_in(): pl.pallas_call(body, grid_spec=pltpu.PrefetchScalarGridSpec(num_scalar_pr...  38.2 us
    ppermute x26, starting transfers between devices, swap(): return lax.ppermute(values, axis, [(i, i ^ stride) for i in range(size)])  28.7 us
    pallas_call x5, Pallas kernels, produce(): pl.pallas_call(body, grid_spec=pltpu.PrefetchScalarGridSpec(num_scalar_pr...  23.7 us
    pallas_call x1, Pallas kernels, project(): pl.pallas_call(body, grid_spec=pltpu.PrefetchScalarGridSpec(num_scalar_pr...  16.1 us
    ppermute x26, waiting for transfers between devices, swap(): return lax.ppermute(values, axis, [(i, i ^ stride) for i in range(size)])  7.7 us
  transfers between devices with their start and end apart: 26, of which 5 were waited for; matrix products, arithmetic and copies ran while one was open for 2% of the time, Pallas kernels for 46%

profile of v6, /device:TPU:0, one launch (start us, length us, event | category | flops | bytes accessed | tf_op | source)
XLA Modules:
  0.0 122.2 jit_solution(9027122192215284527)
XLA Ops:
  0.0 0.8 copy.25
  2.4 0.9 pad_maximum_fusion.1
  3.3 4.1 %collective-permute-start = (bf16[32,1920]{1,0:T(8,128)(2,1)S(1)}, bf16[32,1920]{1,0:T(8,128)(2,1)S(1)}, u32[]{:S(2)}, u32[]{:S(2)}) collective-permute-start(bf16[32,1920]{1,0:T(8,128)(2,1)S(1)} %pad_maximum_fusion.1), channel_id=1, source_target_pairs={{0,4},{1,5},{2,6},{3,7},{4,0},{5,1},{6,2},{7,3},{8,12},{9,13},{10,... | collective-permute-start | bytes 368648 | tf_op jit(solution)/shard_map/ppermute | solution.py:297
  7.4 1.6 %collective-permute-start.1 = (bf16[32,1920]{1,0:T(8,128)(2,1)S(1)}, bf16[32,1920]{1,0:T(8,128)(2,1)S(1)}, u32[]{:S(2)}, u32[]{:S(2)}) collective-permute-start(bf16[32,1920]{1,0:T(8,128)(2,1)S(1)} %pad_maximum_fusion.1), channel_id=1, source_target_pairs={{0,2},{1,3},{2,0},{3,1},{4,6},{5,7},{6,4},{7,5},{8,10},{9,11},{10,... | collective-permute-start | bytes 368648 | tf_op jit(solution)/shard_map/ppermute | solution.py:297
  9.8 9.5 %decode_in.4.rest_0_ = bf16[2,5376,1024]{2,1,0:T(8,128)(2,1)} custom-call(s32[1]{0:T(128)} %bitcast.section_ref.refs_0_, s32[1,2,2,896,1024]{4,3,2,1,0:T(8,128)} %refs_1_.1, bf16[2,2,8,2,16,128]{5,4,3,2,1,0:T(8,128)(2,1)S(1)} %broadcast_in_dim.63.tables_ref.refs_2_), custom_call_target="tpu_custom_call" | custom-call | tf_op jit(solution)/shard_map/decode_in/pallas_call | solution.py:108
  19.5 1.8 %collective-permute-start.3 = (bf16[128,1024]{1,0:T(8,128)(2,1)S(1)}, bf16[128,1024]{1,0:T(8,128)(2,1)S(1)}, u32[]{:S(2)}, u32[]{:S(2)}) collective-permute-start(bf16[128,1024]{1,0:T(8,128)(2,1)S(1)} %pad_maximum_fusion), channel_id=1, source_target_pairs={{0,1},{1,0},{2,3},{3,2},{4,5},{5,4},{6,7},{7,6},{8,9},{9,8},{10,11... | collective-permute-start | bytes 786440 | tf_op jit(solution)/shard_map/ppermute | solution.py:297
  21.3 1.6 %collective-permute-start.4 = (bf16[128,896]{1,0:T(8,128)(2,1)S(1)}, bf16[128,896]{1,0:T(8,128)(2,1)S(1)}, u32[]{:S(2)}, u32[]{:S(2)}) collective-permute-start(bf16[128,896]{1,0:T(8,128)(2,1)S(1)} %get-tuple-element.46), channel_id=1, source_target_pairs={{0,16},{8,24},{16,0},{24,8},{1,17},{9,25},{17,1},{25,9},{2,18},{10... | collective-permute-start | bytes 688136 | tf_op jit(solution)/shard_map/ppermute | solution.py:297
  23.4 9.5 %decode_in.5.rest_0_ = bf16[2,5376,1024]{2,1,0:T(8,128)(2,1)} custom-call(s32[1]{0:T(128)} %bitcast.section_ref.refs_0_, s32[1,2,2,896,1024]{4,3,2,1,0:T(8,128)} %refs_1_.1, bf16[2,2,8,2,16,128]{5,4,3,2,1,0:T(8,128)(2,1)S(1)} %broadcast_in_dim.63.tables_ref.refs_2_, bf16[2,5376,1024]{2,1,0:T(8,128)(2,1)} %decode_in.4.rest_0_), custom_call_target="tpu_custom_call", output_to_operand_aliasing={{}: (3, {})} | custom-call | tf_op jit(solution)/shard_map/decode_in/pallas_call | solution.py:108
  33.5 1.7 %collective-permute-start.7 = (bf16[128,896]{1,0:T(8,128)(2,1)S(1)}, bf16[128,896]{1,0:T(8,128)(2,1)S(1)}, u32[]{:S(2)}, u32[]{:S(2)}) collective-permute-start(bf16[128,896]{1,0:T(8,128)(2,1)S(1)} %collective-permute-done.4), channel_id=1, source_target_pairs={{0,1},{1,0},{2,3},{3,2},{4,5},{5,4},{6,7},{7,6},{8,9},{9,8},{10,11... | collective-permute-start | bytes 688136 | tf_op jit(solution)/shard_map/ppermute | solution.py:297
  35.6 9.5 %decode_in.6.rest_0_ = bf16[2,5376,1024]{2,1,0:T(8,128)(2,1)} custom-call(s32[1]{0:T(128)} %bitcast.section_ref.refs_0_, s32[1,2,2,896,1024]{4,3,2,1,0:T(8,128)} %refs_1_.1, bf16[2,2,8,2,16,128]{5,4,3,2,1,0:T(8,128)(2,1)S(1)} %broadcast_in_dim.63.tables_ref.refs_2_, bf16[2,5376,1024]{2,1,0:T(8,128)(2,1)} %decode_in.5.rest_0_), custom_call_target="tpu_custom_call", output_to_operand_aliasing={{}: (3, {})} | custom-call | tf_op jit(solution)/shard_map/decode_in/pallas_call | solution.py:108
  46.4 9.7 %decode_in.7.refs_3_ = bf16[2,5376,1024]{2,1,0:T(8,128)(2,1)} custom-call(s32[1]{0:T(128)} %bitcast.section_ref.refs_0_, s32[1,2,2,896,1024]{4,3,2,1,0:T(8,128)} %refs_1_.1, bf16[2,2,8,2,16,128]{5,4,3,2,1,0:T(8,128)(2,1)S(1)} %broadcast_in_dim.63.tables_ref.refs_2_, bf16[2,5376,1024]{2,1,0:T(8,128)(2,1)} %decode_in.6.rest_0_), custom_call_target="tpu_custom_call", output_to_operand_aliasing={{}: (3, {})} | custom-call | tf_op jit(solution)/shard_map/decode_in/pallas_call | solution.py:108
  56.1 0.8 copy-done.4
  56.9 16.1 %project.1.folded_ref = bf16[128,1024]{1,0:T(8,128)(2,1)S(1)} custom-call(s32[1]{0:T(128)} %bitcast.section_ref.refs_0_, s32[1,2,2,896,1024]{4,3,2,1,0:T(8,128)} %refs_1_.1, bf16[2,2,8,2,16,128]{5,4,3,2,1,0:T(8,128)(2,1)S(1)} %broadcast_in_dim.63.tables_ref.refs_2_, bf16[2,5376,1024]{2,1,0:T(8,128)(2,1)} %decode_in.7.refs_3_, ...), custom_call_target="tpu_custom_call" | custom-call | tf_op jit(solution)/shard_map/project/pallas_call | solution.py:186
  73.0 5.7 %produce.5 = bf16[256,1792]{1,0:T(8,128)(2,1)S(1)} custom-call(s32[1]{0:T(128)} %bitcast.section_ref.refs_0_, s32[1,2,128,7168]{3,2,1,0:T(8,128)S(1)} %bitcast.8, bf16[2,8,2,16,128]{4,3,2,1,0:T(8,128)(2,1)S(1)} %broadcast_in_dim.61.tables_ref, bf16[128,1024]{1,0:T(8,128)(2,1)S(1)} %project.1.folded_ref, s32[1,2,7168]{2,1,0:T(2,128)S(1)} %copy-done, ...), custom_call_target="tpu_custom_call" | custom-call | tf_op jit(solution)/shard_map/produce/pallas_call | solution.py:274
  79.0 5.7 %produce.6 = bf16[256,1792]{1,0:T(8,128)(2,1)S(1)} custom-call(s32[1]{0:T(128)} %bitcast.section_ref.refs_0_, s32[1,2,128,7168]{3,2,1,0:T(8,128)S(1)} %bitcast.8, bf16[2,8,2,16,128]{4,3,2,1,0:T(8,128)(2,1)S(1)} %broadcast_in_dim.61.tables_ref, bf16[128,1024]{1,0:T(8,128)(2,1)S(1)} %project.1.folded_ref, s32[1,2,7168]{2,1,0:T(2,128)S(1)} %copy-done, ...), custom_call_target="tpu_custom_call" | custom-call | tf_op jit(solution)/shard_map/produce/pallas_call | solution.py:274
  85.3 1.7 %collective-permute-start.14 = (bf16[256,384]{1,0:T(8,128)(2,1)S(1)}, bf16[256,384]{1,0:T(8,128)(2,1)S(1)}, u32[]{:S(2)}, u32[]{:S(2)}) collective-permute-start(bf16[256,384]{1,0:T(8,128)(2,1)S(1)} %slice.119), channel_id=1, source_target_pairs={{0,16},{8,24},{16,0},{24,8},{1,17},{9,25},{17,1},{25,9},{2,18},{10... | collective-permute-start | bytes 589832 | tf_op jit(solution)/shard_map/ppermute | solution.py:297
  87.1 5.9 %produce.7 = bf16[256,1792]{1,0:T(8,128)(2,1)S(1)} custom-call(s32[1]{0:T(128)} %bitcast.section_ref.refs_0_, s32[1,2,128,7168]{3,2,1,0:T(8,128)S(1)} %bitcast.8, bf16[2,8,2,16,128]{4,3,2,1,0:T(8,128)(2,1)S(1)} %broadcast_in_dim.61.tables_ref, bf16[128,1024]{1,0:T(8,128)(2,1)S(1)} %project.1.folded_ref, s32[1,2,7168]{2,1,0:T(2,128)S(1)} %copy-done, ...), custom_call_target="tpu_custom_call" | custom-call | tf_op jit(solution)/shard_map/produce/pallas_call | solution.py:274
  93.1 1.3 %collective-permute-start.17 = (bf16[256,512]{1,0:T(8,128)(2,1)S(1)}, bf16[256,512]{1,0:T(8,128)(2,1)S(1)}, u32[]{:S(2)}, u32[]{:S(2)}) collective-permute-start(bf16[256,512]{1,0:T(8,128)(2,1)S(1)} %slice.120), channel_id=1, source_target_pairs={{0,16},{8,24},{16,0},{24,8},{1,17},{9,25},{17,1},{25,9},{2,18},{10... | collective-permute-start | bytes 786440 | tf_op jit(solution)/shard_map/ppermute | solution.py:297
  94.4 3.2 %produce.8 = f32[256,896]{1,0:T(8,128)S(1)} custom-call(s32[1]{0:T(128)} %bitcast.section_ref.refs_0_, s32[1,2,128,7168]{3,2,1,0:T(8,128)S(1)} %bitcast.8, bf16[2,8,2,16,128]{4,3,2,1,0:T(8,128)(2,1)S(1)} %broadcast_in_dim.61.tables_ref, bf16[128,1024]{1,0:T(8,128)(2,1)S(1)} %project.1.folded_ref, s32[1,2,7168]{2,1,0:T(2,128)S(1)} %copy-done, ...), custom_call_target="tpu_custom_call" | custom-call | tf_op jit(solution)/shard_map/produce/pallas_call | solution.py:274
  97.8 1.1 collective-permute-start.16
  98.9 1.3 %collective-permute-start.22 = (bf16[128,896]{1,0:T(8,128)(2,1)S(1)}, bf16[128,896]{1,0:T(8,128)(2,1)S(1)}, u32[]{:S(2)}, u32[]{:S(2)}) collective-permute-start(bf16[128,896]{1,0:T(8,128)(2,1)S(1)} %add_convert_fusion.1), channel_id=1, source_target_pairs={{0,16},{8,24},{16,0},{24,8},{1,17},{9,25},{17,1},{25,9},{2,18},{10... | collective-permute-start | bytes 688136 | tf_op jit(solution)/shard_map/ppermute | solution.py:297
  100.2 3.2 %produce.9 = f32[256,896]{1,0:T(8,128)S(1)} custom-call(s32[1]{0:T(128)} %bitcast.section_ref.refs_0_, s32[1,2,128,7168]{3,2,1,0:T(8,128)S(1)} %bitcast.8, bf16[2,8,2,16,128]{4,3,2,1,0:T(8,128)(2,1)S(1)} %broadcast_in_dim.61.tables_ref, bf16[128,1024]{1,0:T(8,128)(2,1)S(1)} %project.1.folded_ref, s32[1,2,7168]{2,1,0:T(2,128)S(1)} %copy-done, ...), custom_call_target="tpu_custom_call" | custom-call | tf_op jit(solution)/shard_map/produce/pallas_call | solution.py:274
  103.5 2.1 %collective-permute-done.16 = bf16[128,896]{1,0:T(8,128)(2,1)S(1)} collective-permute-done((bf16[128,896]{1,0:T(8,128)(2,1)S(1)}, bf16[128,896]{1,0:T(8,128)(2,1)S(1)}, u32[]{:S(2)}, u32[]{:S(2)}) %collective-permute-start.16) | collective-permute-done | bytes 229408 | tf_op jit(solution)/shard_map/ppermute | solution.py:297
  105.7 1.1 collective-permute-start.18
  106.9 3.7 %collective-permute-start.25 = (bf16[32,896]{1,0:T(8,128)(2,1)S(1)}, bf16[32,896]{1,0:T(8,128)(2,1)S(1)}, u32[]{:S(2)}, u32[]{:S(2)}) collective-permute-start(bf16[32,896]{1,0:T(8,128)(2,1)S(1)} %get-tuple-element.87), channel_id=1, source_target_pairs={{0,6},{1,7},{2,4},{3,5},{4,2},{5,3},{6,0},{7,1},{8,14},{9,15},{10,... | collective-permute-start | bytes 172040 | tf_op jit(solution)/shard_map/ppermute | solution.py:297
  110.6 0.8 collective-permute-start.23
  111.4 1.3 %collective-permute-done.18 = bf16[128,896]{1,0:T(8,128)(2,1)S(1)} collective-permute-done((bf16[128,896]{1,0:T(8,128)(2,1)S(1)}, bf16[128,896]{1,0:T(8,128)(2,1)S(1)}, u32[]{:S(2)}, u32[]{:S(2)}) %collective-permute-start.18) | collective-permute-done | bytes 229408 | tf_op jit(solution)/shard_map/ppermute | solution.py:297
  112.8 3.7 %collective-permute-start.21 = (bf16[32,896]{1,0:T(8,128)(2,1)S(1)}, bf16[32,896]{1,0:T(8,128)(2,1)S(1)}, u32[]{:S(2)}, u32[]{:S(2)}) collective-permute-start(bf16[32,896]{1,0:T(8,128)(2,1)S(1)} %get-tuple-element.84), channel_id=1, source_target_pairs={{0,6},{1,7},{2,4},{3,5},{4,2},{5,3},{6,0},{7,1},{8,14},{9,15},{10,... | collective-permute-start | bytes 172040 | tf_op jit(solution)/shard_map/ppermute | solution.py:297
  116.5 0.8 collective-permute-start.19
  117.3 1.6 %collective-permute-done.21 = bf16[32,896]{1,0:T(8,128)(2,1)S(1)} collective-permute-done((bf16[32,896]{1,0:T(8,128)(2,1)S(1)}, bf16[32,896]{1,0:T(8,128)(2,1)S(1)}, u32[]{:S(2)}, u32[]{:S(2)}) %collective-permute-start.21) | collective-permute-done | bytes 57376 | tf_op jit(solution)/shard_map/ppermute | solution.py:297
  118.9 1.7 %collective-permute-done.20 = bf16[32,896]{1,0:T(8,128)(2,1)S(1)} collective-permute-done((bf16[32,896]{1,0:T(8,128)(2,1)S(1)}, bf16[32,896]{1,0:T(8,128)(2,1)S(1)}, u32[]{:S(2)}, u32[]{:S(2)}) %collective-permute-start.20) | collective-permute-done | bytes 57376 | tf_op jit(solution)/shard_map/ppermute | solution.py:297
  120.6 0.9 collective-permute-done.19
  (97 shorter events, 7.4 us)
Async XLA Ops:
  3.3 16.0 %collective-permute-start = (bf16[32,1920]{1,0:T(8,128)(2,1)S(1)}, bf16[32,1920]{1,0:T(8,128)(2,1)S(1)}, u32[]{:S(2)}, u32[]{:S(2)}) collective-permute-start(bf16[32,1920]{1,0:T(8,128)(2,1)S(1)} %pad_maximum_fusion.1), channel_id=1, source_target_pairs={{0,4},{1,5},{2,6},{3,7},{4,0},{5,1},{6,2},{7,3},{8,12},{9,13},{10,... | collective-permute-start | bytes 368648 | tf_op jit(solution)/shard_map/ppermute | solution.py:297
  7.4 11.9 %collective-permute-start.1 = (bf16[32,1920]{1,0:T(8,128)(2,1)S(1)}, bf16[32,1920]{1,0:T(8,128)(2,1)S(1)}, u32[]{:S(2)}, u32[]{:S(2)}) collective-permute-start(bf16[32,1920]{1,0:T(8,128)(2,1)S(1)} %pad_maximum_fusion.1), channel_id=1, source_target_pairs={{0,2},{1,3},{2,0},{3,1},{4,6},{5,7},{6,4},{7,5},{8,10},{9,11},{10,... | collective-permute-start | bytes 368648 | tf_op jit(solution)/shard_map/ppermute | solution.py:297
  9.0 10.3 %collective-permute-start.2 = (bf16[32,1920]{1,0:T(8,128)(2,1)S(1)}, bf16[32,1920]{1,0:T(8,128)(2,1)S(1)}, u32[]{:S(2)}, u32[]{:S(2)}) collective-permute-start(bf16[32,1920]{1,0:T(8,128)(2,1)S(1)} %pad_maximum_fusion.1), channel_id=1, source_target_pairs={{0,6},{1,7},{2,4},{3,5},{4,2},{5,3},{6,0},{7,1},{8,14},{9,15},{10,... | collective-permute-start | bytes 368648 | tf_op jit(solution)/shard_map/ppermute | solution.py:297
  9.8 11.5 %copy-start.5 = (bf16[2,256,8]{1,2,0:T(8,128)(2,1)S(1)}, bf16[2,256,8]{1,2,0:T(8,128)(2,1)}, u32[]{:S(2)}) copy-start(bf16[2,256,8]{1,2,0:T(8,128)(2,1)} %param.19) | copy-start | bytes 24580
  19.5 13.5 %collective-permute-start.3 = (bf16[128,1024]{1,0:T(8,128)(2,1)S(1)}, bf16[128,1024]{1,0:T(8,128)(2,1)S(1)}, u32[]{:S(2)}, u32[]{:S(2)}) collective-permute-start(bf16[128,1024]{1,0:T(8,128)(2,1)S(1)} %pad_maximum_fusion), channel_id=1, source_target_pairs={{0,1},{1,0},{2,3},{3,2},{4,5},{5,4},{6,7},{7,6},{8,9},{9,8},{10,11... | collective-permute-start | bytes 786440 | tf_op jit(solution)/shard_map/ppermute | solution.py:297
  21.3 11.6 %collective-permute-start.4 = (bf16[128,896]{1,0:T(8,128)(2,1)S(1)}, bf16[128,896]{1,0:T(8,128)(2,1)S(1)}, u32[]{:S(2)}, u32[]{:S(2)}) collective-permute-start(bf16[128,896]{1,0:T(8,128)(2,1)S(1)} %get-tuple-element.46), channel_id=1, source_target_pairs={{0,16},{8,24},{16,0},{24,8},{1,17},{9,25},{17,1},{25,9},{2,18},{10... | collective-permute-start | bytes 688136 | tf_op jit(solution)/shard_map/ppermute | solution.py:297
  22.9 22.3 %collective-permute-start.6 = (bf16[128,896]{1,0:T(8,128)(2,1)S(1)}, bf16[128,896]{1,0:T(8,128)(2,1)S(1)}, u32[]{:S(2)}, u32[]{:S(2)}) collective-permute-start(bf16[128,896]{1,0:T(8,128)(2,1)S(1)} %get-tuple-element.46), channel_id=1, source_target_pairs={{0,1},{1,0},{2,3},{3,2},{4,5},{5,4},{6,7},{7,6},{8,9},{9,8},{10,11... | collective-permute-start | bytes 688136 | tf_op jit(solution)/shard_map/ppermute | solution.py:297
  33.1 12.1 %collective-permute-start.5 = (bf16[256,896]{1,0:T(8,128)(2,1)S(1)}, bf16[256,896]{1,0:T(8,128)(2,1)S(1)}, u32[]{:S(2)}, u32[]{:S(2)}) collective-permute-start(bf16[256,896]{1,0:T(8,128)(2,1)S(1)} %slice.115.refs_5_), channel_id=1, source_target_pairs={{0,16},{8,24},{16,0},{24,8},{1,17},{9,25},{17,1},{25,9},{2,18},{10... | collective-permute-start | bytes 1376264 | tf_op jit(solution)/shard_map/ppermute | solution.py:297
  33.5 22.6 %collective-permute-start.8 = (bf16[256,896]{1,0:T(8,128)(2,1)S(1)}, bf16[256,896]{1,0:T(8,128)(2,1)S(1)}, u32[]{:S(2)}, u32[]{:S(2)}) collective-permute-start(bf16[256,896]{1,0:T(8,128)(2,1)S(1)} %slice.115.refs_5_), channel_id=1, source_target_pairs={{0,8},{8,0},{16,24},{24,16},{1,9},{9,1},{17,25},{25,17},{2,10},{10... | collective-permute-start | bytes 1376264 | tf_op jit(solution)/shard_map/ppermute | solution.py:297
  33.5 11.7 %collective-permute-start.7 = (bf16[128,896]{1,0:T(8,128)(2,1)S(1)}, bf16[128,896]{1,0:T(8,128)(2,1)S(1)}, u32[]{:S(2)}, u32[]{:S(2)}) collective-permute-start(bf16[128,896]{1,0:T(8,128)(2,1)S(1)} %collective-permute-done.4), channel_id=1, source_target_pairs={{0,1},{1,0},{2,3},{3,2},{4,5},{5,4},{6,7},{7,6},{8,9},{9,8},{10,11... | collective-permute-start | bytes 688136 | tf_op jit(solution)/shard_map/ppermute | solution.py:297
  45.2 10.9 %collective-permute-start.9 = (bf16[256,896]{1,0:T(8,128)(2,1)S(1)}, bf16[256,896]{1,0:T(8,128)(2,1)S(1)}, u32[]{:S(2)}, u32[]{:S(2)}) collective-permute-start(bf16[256,896]{1,0:T(8,128)(2,1)S(1)} %constant_dynamic-update-slice_fusion.6.refs_6_), channel_id=1, source_target_pairs={{0,8},{8,0},{16,24},{24,16},{1,9},{9,1},{17,25},{25,17},{2,10},{10... | collective-permute-start | bytes 1376264 | tf_op jit(solution)/shard_map/ppermute | solution.py:297
  45.5 10.6 %collective-permute-start.10 = (bf16[256,896]{1,0:T(8,128)(2,1)S(1)}, bf16[256,896]{1,0:T(8,128)(2,1)S(1)}, u32[]{:S(2)}, u32[]{:S(2)}) collective-permute-start(bf16[256,896]{1,0:T(8,128)(2,1)S(1)} %collective-permute-done.5.refs_7_), channel_id=1, source_target_pairs={{0,8},{8,0},{16,24},{24,16},{1,9},{9,1},{17,25},{25,17},{2,10},{10... | collective-permute-start | bytes 1376264 | tf_op jit(solution)/shard_map/ppermute | solution.py:297
  45.8 10.3 %collective-permute-start.11 = (bf16[256,896]{1,0:T(8,128)(2,1)S(1)}, bf16[256,896]{1,0:T(8,128)(2,1)S(1)}, u32[]{:S(2)}, u32[]{:S(2)}) collective-permute-start(bf16[256,896]{1,0:T(8,128)(2,1)S(1)} %constant_dynamic-update-slice_fusion.8.refs_8_), channel_id=1, source_target_pairs={{0,8},{8,0},{16,24},{24,16},{1,9},{9,1},{17,25},{25,17},{2,10},{10... | collective-permute-start | bytes 1376264 | tf_op jit(solution)/shard_map/ppermute | solution.py:297
  46.2 26.8 %slice-start = ((s8[7340032]{0:T(1024)(128)(4,1)}), s8[4194304]{0:T(1024)(128)(4,1)S(1)}, s32[]{:S(2)}) async-start(s8[7340032]{0:T(1024)(128)(4,1)} %bitcast.7), calls=%async_computation | async-start | bytes 8388608
  46.3 10.5 %copy-start = (s32[1,2,7168]{2,1,0:T(2,128)S(1)}, s32[1,2,7168]{2,1,0:T(2,128)}, u32[]{:S(2)}) copy-start(s32[1,2,7168]{2,1,0:T(2,128)} %signs_ref.9) | copy-start | bytes 172036
  46.4 10.5 %copy-start.2 = (bf16[128,128]{1,0:T(8,128)(2,1)S(1)}, bf16[128,128]{1,0:T(8,128)(2,1)}, u32[]{:S(2)}) copy-start(bf16[128,128]{1,0:T(8,128)(2,1)} %constant.33.clone.refs_15_) | copy-start | bytes 98308
  46.4 26.6 %slice-start.1 = ((s8[7340032]{0:T(1024)(128)(4,1)}), s8[3145728]{0:T(1024)(128)(4,1)S(1)}, s32[]{:S(2)}) async-start(s8[7340032]{0:T(1024)(128)(4,1)} %bitcast.7), calls=%async_computation.1 | async-start | bytes 6291456
  56.1 16.9 %copy-start.1 = (bf16[128,128]{1,0:T(8,128)(2,1)S(1)}, bf16[128,128]{1,0:T(8,128)(2,1)}, u32[]{:S(2)}) copy-start(bf16[128,128]{1,0:T(8,128)(2,1)} %constant.34.clone.had_ref) | copy-start | bytes 98308
  78.7 5.9 %collective-permute-start.12 = (bf16[256,1792]{1,0:T(8,128)(2,1)S(1)}, bf16[256,1792]{1,0:T(8,128)(2,1)S(1)}, u32[]{:S(2)}, u32[]{:S(2)}) collective-permute-start(bf16[256,1792]{1,0:T(8,128)(2,1)S(1)} %produce.5), channel_id=1, source_target_pairs={{0,8},{8,0},{16,24},{24,16},{1,9},{9,1},{17,25},{25,17},{2,10},{10... | collective-permute-start | bytes 2752520 | tf_op jit(solution)/shard_map/ppermute | solution.py:297
  85.0 8.0 %collective-permute-start.13 = (bf16[128,896]{1,0:T(8,128)(2,1)S(1)}, bf16[128,896]{1,0:T(8,128)(2,1)S(1)}, u32[]{:S(2)}, u32[]{:S(2)}) collective-permute-start(bf16[128,896]{1,0:T(8,128)(2,1)S(1)} %get-tuple-element.60), channel_id=1, source_target_pairs={{0,1},{1,0},{2,3},{3,2},{4,5},{5,4},{6,7},{7,6},{8,9},{9,8},{10,11... | collective-permute-start | bytes 688136 | tf_op jit(solution)/shard_map/ppermute | solution.py:297
  85.3 7.6 %collective-permute-start.14 = (bf16[256,384]{1,0:T(8,128)(2,1)S(1)}, bf16[256,384]{1,0:T(8,128)(2,1)S(1)}, u32[]{:S(2)}, u32[]{:S(2)}) collective-permute-start(bf16[256,384]{1,0:T(8,128)(2,1)S(1)} %slice.119), channel_id=1, source_target_pairs={{0,16},{8,24},{16,0},{24,8},{1,17},{9,25},{17,1},{25,9},{2,18},{10... | collective-permute-start | bytes 589832 | tf_op jit(solution)/shard_map/ppermute | solution.py:297
  93.0 4.6 %collective-permute-start.15 = (bf16[256,1792]{1,0:T(8,128)(2,1)S(1)}, bf16[256,1792]{1,0:T(8,128)(2,1)S(1)}, u32[]{:S(2)}, u32[]{:S(2)}) collective-permute-start(bf16[256,1792]{1,0:T(8,128)(2,1)S(1)} %produce.7), channel_id=1, source_target_pairs={{0,8},{8,0},{16,24},{24,16},{1,9},{9,1},{17,25},{25,17},{2,10},{10... | collective-permute-start | bytes 2752520 | tf_op jit(solution)/shard_map/ppermute | solution.py:297
  93.1 12.5 %collective-permute-start.17 = (bf16[256,512]{1,0:T(8,128)(2,1)S(1)}, bf16[256,512]{1,0:T(8,128)(2,1)S(1)}, u32[]{:S(2)}, u32[]{:S(2)}) collective-permute-start(bf16[256,512]{1,0:T(8,128)(2,1)S(1)} %slice.120), channel_id=1, source_target_pairs={{0,16},{8,24},{16,0},{24,8},{1,17},{9,25},{17,1},{25,9},{2,18},{10... | collective-permute-start | bytes 786440 | tf_op jit(solution)/shard_map/ppermute | solution.py:297
  97.8 7.8 %collective-permute-start.16 = (bf16[128,896]{1,0:T(8,128)(2,1)S(1)}, bf16[128,896]{1,0:T(8,128)(2,1)S(1)}, u32[]{:S(2)}, u32[]{:S(2)}) collective-permute-start(bf16[128,896]{1,0:T(8,128)(2,1)S(1)} %slice.163), channel_id=1, source_target_pairs={{0,1},{1,0},{2,3},{3,2},{4,5},{5,4},{6,7},{7,6},{8,9},{9,8},{10,11... | collective-permute-start | bytes 688136 | tf_op jit(solution)/shard_map/ppermute | solution.py:297
  98.9 7.9 %collective-permute-start.22 = (bf16[128,896]{1,0:T(8,128)(2,1)S(1)}, bf16[128,896]{1,0:T(8,128)(2,1)S(1)}, u32[]{:S(2)}, u32[]{:S(2)}) collective-permute-start(bf16[128,896]{1,0:T(8,128)(2,1)S(1)} %add_convert_fusion.1), channel_id=1, source_target_pairs={{0,16},{8,24},{16,0},{24,8},{1,17},{9,25},{17,1},{25,9},{2,18},{10... | collective-permute-start | bytes 688136 | tf_op jit(solution)/shard_map/ppermute | solution.py:297
  105.7 7.0 %collective-permute-start.18 = (bf16[128,896]{1,0:T(8,128)(2,1)S(1)}, bf16[128,896]{1,0:T(8,128)(2,1)S(1)}, u32[]{:S(2)}, u32[]{:S(2)}) collective-permute-start(bf16[128,896]{1,0:T(8,128)(2,1)S(1)} %slice.162), channel_id=1, source_target_pairs={{0,1},{1,0},{2,3},{3,2},{4,5},{5,4},{6,7},{7,6},{8,9},{9,8},{10,11... | collective-permute-start | bytes 688136 | tf_op jit(solution)/shard_map/ppermute | solution.py:297
  106.9 9.5 %collective-permute-start.25 = (bf16[32,896]{1,0:T(8,128)(2,1)S(1)}, bf16[32,896]{1,0:T(8,128)(2,1)S(1)}, u32[]{:S(2)}, u32[]{:S(2)}) collective-permute-start(bf16[32,896]{1,0:T(8,128)(2,1)S(1)} %get-tuple-element.87), channel_id=1, source_target_pairs={{0,6},{1,7},{2,4},{3,5},{4,2},{5,3},{6,0},{7,1},{8,14},{9,15},{10,... | collective-permute-start | bytes 172040 | tf_op jit(solution)/shard_map/ppermute | solution.py:297
  110.6 6.6 %collective-permute-start.24 = (bf16[32,896]{1,0:T(8,128)(2,1)S(1)}, bf16[32,896]{1,0:T(8,128)(2,1)S(1)}, u32[]{:S(2)}, u32[]{:S(2)}) collective-permute-start(bf16[32,896]{1,0:T(8,128)(2,1)S(1)} %get-tuple-element.88), channel_id=1, source_target_pairs={{0,2},{1,3},{2,0},{3,1},{4,6},{5,7},{6,4},{7,5},{8,10},{9,11},{10,... | collective-permute-start | bytes 172040 | tf_op jit(solution)/shard_map/ppermute | solution.py:297
  110.6 6.6 %collective-permute-start.23 = (bf16[32,896]{1,0:T(8,128)(2,1)S(1)}, bf16[32,896]{1,0:T(8,128)(2,1)S(1)}, u32[]{:S(2)}, u32[]{:S(2)}) collective-permute-start(bf16[32,896]{1,0:T(8,128)(2,1)S(1)} %get-tuple-element.86), channel_id=1, source_target_pairs={{0,4},{1,5},{2,6},{3,7},{4,0},{5,1},{6,2},{7,3},{8,12},{9,13},{10,... | collective-permute-start | bytes 172040 | tf_op jit(solution)/shard_map/ppermute | solution.py:297
  112.8 6.1 %collective-permute-start.21 = (bf16[32,896]{1,0:T(8,128)(2,1)S(1)}, bf16[32,896]{1,0:T(8,128)(2,1)S(1)}, u32[]{:S(2)}, u32[]{:S(2)}) collective-permute-start(bf16[32,896]{1,0:T(8,128)(2,1)S(1)} %get-tuple-element.84), channel_id=1, source_target_pairs={{0,6},{1,7},{2,4},{3,5},{4,2},{5,3},{6,0},{7,1},{8,14},{9,15},{10,... | collective-permute-start | bytes 172040 | tf_op jit(solution)/shard_map/ppermute | solution.py:297
  116.5 4.2 %collective-permute-start.20 = (bf16[32,896]{1,0:T(8,128)(2,1)S(1)}, bf16[32,896]{1,0:T(8,128)(2,1)S(1)}, u32[]{:S(2)}, u32[]{:S(2)}) collective-permute-start(bf16[32,896]{1,0:T(8,128)(2,1)S(1)} %get-tuple-element.85), channel_id=1, source_target_pairs={{0,2},{1,3},{2,0},{3,1},{4,6},{5,7},{6,4},{7,5},{8,10},{9,11},{10,... | collective-permute-start | bytes 172040 | tf_op jit(solution)/shard_map/ppermute | solution.py:297
  116.5 5.1 %collective-permute-start.19 = (bf16[32,896]{1,0:T(8,128)(2,1)S(1)}, bf16[32,896]{1,0:T(8,128)(2,1)S(1)}, u32[]{:S(2)}, u32[]{:S(2)}) collective-permute-start(bf16[32,896]{1,0:T(8,128)(2,1)S(1)} %get-tuple-element.83), channel_id=1, source_target_pairs={{0,4},{1,5},{2,6},{3,7},{4,0},{5,1},{6,2},{7,3},{8,12},{9,13},{10,... | collective-permute-start | bytes 172040 | tf_op jit(solution)/shard_map/ppermute | solution.py:297
  (2 other events, 11.3 us)

commit v7 on v6

--- a/solution.py
+++ b/solution.py
@@ -248,10 +248,14 @@
             mid = left.astype(bf16)
             low = (left - mid.astype(f32)).astype(bf16)
             table = had_ref[...]
-            turned = []
-            for b in range(0, size, HAD):
-                s = slice(b, b + HAD)
-                turned.append(dot(high[:, s], table) + (dot(mid[:, s], table) + dot(low[:, s], table)))
+            cuts = [slice(b, b + HAD) for b in range(0, size, HAD)]
+            tall = jnp.concatenate([part[:, cut] for part in (high, mid, low) for cut in cuts], 0)
+            tall = dot(tall, table)
+            count = len(cuts)
+            parts = [tall[b * slots : (b + 1) * slots] for b in range(3 * count)]
+            turned = [
+                parts[b] + (parts[count + b] + parts[2 * count + b]) for b in range(count)
+            ]
             turned = jnp.concatenate(turned, 1) * UNIT
             result = (back[:, at : at + size] * turned).astype(bf16)
             out[:, at : at + size] = dot(spread_ref[...], result).astype(dtype)

time: 123 us -> 123 us (level)
  no operation moved by 1% of the time
where the time goes in v7:
time: 123 us; the launch traced here: 122 us
  Pallas kernels  78.1 us (63%)
  starting transfers between devices  28.7 us (23%)
  waiting for transfers between devices  7.66 us (6%)
  other arithmetic  4.47 us (4%)
  local copies, waits for them, and re-layouts  2.91 us (2%)
    pallas_call x4, Pallas kernels, decode_in(): pl.pallas_call(body, grid_spec=pltpu.PrefetchScalarGridSpec(num_scalar_pr...  38.2 us
    ppermute x26, starting transfers between devices, swap(): return lax.ppermute(values, axis, [(i, i ^ stride) for i in range(size)])  28.7 us
    pallas_call x5, Pallas kernels, produce(): pl.pallas_call(body, grid_spec=pltpu.PrefetchScalarGridSpec(num_scalar_pr...  23.8 us
    pallas_call x1, Pallas kernels, project(): pl.pallas_call(body, grid_spec=pltpu.PrefetchScalarGridSpec(num_scalar_pr...  16.1 us
    ppermute x26, waiting for transfers between devices, swap(): return lax.ppermute(values, axis, [(i, i ^ stride) for i in range(size)])  7.66 us
  transfers between devices with their start and end apart: 26, of which 5 were waited for; matrix products, arithmetic and copies ran while one was open for 2% of the time, Pallas kernels for 46%

profile of v7, /device:TPU:0, one launch (start us, length us, event | category | flops | bytes accessed | tf_op | source)
XLA Modules:
  0.0 122.3 jit_solution(6222536119330307616)
XLA Ops:
  0.0 0.8 copy.25
  2.4 0.9 pad_maximum_fusion.1
  3.3 4.1 %collective-permute-start = (bf16[32,1920]{1,0:T(8,128)(2,1)S(1)}, bf16[32,1920]{1,0:T(8,128)(2,1)S(1)}, u32[]{:S(2)}, u32[]{:S(2)}) collective-permute-start(bf16[32,1920]{1,0:T(8,128)(2,1)S(1)} %pad_maximum_fusion.1), channel_id=1, source_target_pairs={{0,4},{1,5},{2,6},{3,7},{4,0},{5,1},{6,2},{7,3},{8,12},{9,13},{10,... | collective-permute-start | bytes 368648 | tf_op jit(solution)/shard_map/ppermute | solution.py:301
  7.4 1.6 %collective-permute-start.1 = (bf16[32,1920]{1,0:T(8,128)(2,1)S(1)}, bf16[32,1920]{1,0:T(8,128)(2,1)S(1)}, u32[]{:S(2)}, u32[]{:S(2)}) collective-permute-start(bf16[32,1920]{1,0:T(8,128)(2,1)S(1)} %pad_maximum_fusion.1), channel_id=1, source_target_pairs={{0,2},{1,3},{2,0},{3,1},{4,6},{5,7},{6,4},{7,5},{8,10},{9,11},{10,... | collective-permute-start | bytes 368648 | tf_op jit(solution)/shard_map/ppermute | solution.py:301
  9.8 9.5 %decode_in.4.rest_0_ = bf16[2,5376,1024]{2,1,0:T(8,128)(2,1)} custom-call(s32[1]{0:T(128)} %bitcast.section_ref.refs_0_, s32[1,2,2,896,1024]{4,3,2,1,0:T(8,128)} %refs_1_.1, bf16[2,2,8,2,16,128]{5,4,3,2,1,0:T(8,128)(2,1)S(1)} %broadcast_in_dim.63.tables_ref.refs_2_), custom_call_target="tpu_custom_call" | custom-call | tf_op jit(solution)/shard_map/decode_in/pallas_call | solution.py:108
  19.5 1.8 %collective-permute-start.3 = (bf16[128,1024]{1,0:T(8,128)(2,1)S(1)}, bf16[128,1024]{1,0:T(8,128)(2,1)S(1)}, u32[]{:S(2)}, u32[]{:S(2)}) collective-permute-start(bf16[128,1024]{1,0:T(8,128)(2,1)S(1)} %pad_maximum_fusion), channel_id=1, source_target_pairs={{0,1},{1,0},{2,3},{3,2},{4,5},{5,4},{6,7},{7,6},{8,9},{9,8},{10,11... | collective-permute-start | bytes 786440 | tf_op jit(solution)/shard_map/ppermute | solution.py:301
  21.3 1.6 %collective-permute-start.4 = (bf16[128,896]{1,0:T(8,128)(2,1)S(1)}, bf16[128,896]{1,0:T(8,128)(2,1)S(1)}, u32[]{:S(2)}, u32[]{:S(2)}) collective-permute-start(bf16[128,896]{1,0:T(8,128)(2,1)S(1)} %get-tuple-element.46), channel_id=1, source_target_pairs={{0,16},{8,24},{16,0},{24,8},{1,17},{9,25},{17,1},{25,9},{2,18},{10... | collective-permute-start | bytes 688136 | tf_op jit(solution)/shard_map/ppermute | solution.py:301
  23.4 9.5 %decode_in.5.rest_0_ = bf16[2,5376,1024]{2,1,0:T(8,128)(2,1)} custom-call(s32[1]{0:T(128)} %bitcast.section_ref.refs_0_, s32[1,2,2,896,1024]{4,3,2,1,0:T(8,128)} %refs_1_.1, bf16[2,2,8,2,16,128]{5,4,3,2,1,0:T(8,128)(2,1)S(1)} %broadcast_in_dim.63.tables_ref.refs_2_, bf16[2,5376,1024]{2,1,0:T(8,128)(2,1)} %decode_in.4.rest_0_), custom_call_target="tpu_custom_call", output_to_operand_aliasing={{}: (3, {})} | custom-call | tf_op jit(solution)/shard_map/decode_in/pallas_call | solution.py:108
  33.5 1.7 %collective-permute-start.7 = (bf16[128,896]{1,0:T(8,128)(2,1)S(1)}, bf16[128,896]{1,0:T(8,128)(2,1)S(1)}, u32[]{:S(2)}, u32[]{:S(2)}) collective-permute-start(bf16[128,896]{1,0:T(8,128)(2,1)S(1)} %collective-permute-done.4), channel_id=1, source_target_pairs={{0,1},{1,0},{2,3},{3,2},{4,5},{5,4},{6,7},{7,6},{8,9},{9,8},{10,11... | collective-permute-start | bytes 688136 | tf_op jit(solution)/shard_map/ppermute | solution.py:301
  35.6 9.5 %decode_in.6.rest_0_ = bf16[2,5376,1024]{2,1,0:T(8,128)(2,1)} custom-call(s32[1]{0:T(128)} %bitcast.section_ref.refs_0_, s32[1,2,2,896,1024]{4,3,2,1,0:T(8,128)} %refs_1_.1, bf16[2,2,8,2,16,128]{5,4,3,2,1,0:T(8,128)(2,1)S(1)} %broadcast_in_dim.63.tables_ref.refs_2_, bf16[2,5376,1024]{2,1,0:T(8,128)(2,1)} %decode_in.5.rest_0_), custom_call_target="tpu_custom_call", output_to_operand_aliasing={{}: (3, {})} | custom-call | tf_op jit(solution)/shard_map/decode_in/pallas_call | solution.py:108
  46.4 9.7 %decode_in.7.refs_3_ = bf16[2,5376,1024]{2,1,0:T(8,128)(2,1)} custom-call(s32[1]{0:T(128)} %bitcast.section_ref.refs_0_, s32[1,2,2,896,1024]{4,3,2,1,0:T(8,128)} %refs_1_.1, bf16[2,2,8,2,16,128]{5,4,3,2,1,0:T(8,128)(2,1)S(1)} %broadcast_in_dim.63.tables_ref.refs_2_, bf16[2,5376,1024]{2,1,0:T(8,128)(2,1)} %decode_in.6.rest_0_), custom_call_target="tpu_custom_call", output_to_operand_aliasing={{}: (3, {})} | custom-call | tf_op jit(solution)/shard_map/decode_in/pallas_call | solution.py:108
  56.1 0.8 copy-done.4
  56.9 16.1 %project.1.folded_ref = bf16[128,1024]{1,0:T(8,128)(2,1)S(1)} custom-call(s32[1]{0:T(128)} %bitcast.section_ref.refs_0_, s32[1,2,2,896,1024]{4,3,2,1,0:T(8,128)} %refs_1_.1, bf16[2,2,8,2,16,128]{5,4,3,2,1,0:T(8,128)(2,1)S(1)} %broadcast_in_dim.63.tables_ref.refs_2_, bf16[2,5376,1024]{2,1,0:T(8,128)(2,1)} %decode_in.7.refs_3_, ...), custom_call_target="tpu_custom_call" | custom-call | tf_op jit(solution)/shard_map/project/pallas_call | solution.py:186
  73.0 5.7 %produce.5 = bf16[256,1792]{1,0:T(8,128)(2,1)S(1)} custom-call(s32[1]{0:T(128)} %bitcast.section_ref.refs_0_, s32[1,2,128,7168]{3,2,1,0:T(8,128)S(1)} %bitcast.8, bf16[2,8,2,16,128]{4,3,2,1,0:T(8,128)(2,1)S(1)} %broadcast_in_dim.61.tables_ref, bf16[128,1024]{1,0:T(8,128)(2,1)S(1)} %project.1.folded_ref, s32[1,2,7168]{2,1,0:T(2,128)S(1)} %copy-done, ...), custom_call_target="tpu_custom_call" | custom-call | tf_op jit(solution)/shard_map/produce/pallas_call | solution.py:278
  79.0 5.7 %produce.6 = bf16[256,1792]{1,0:T(8,128)(2,1)S(1)} custom-call(s32[1]{0:T(128)} %bitcast.section_ref.refs_0_, s32[1,2,128,7168]{3,2,1,0:T(8,128)S(1)} %bitcast.8, bf16[2,8,2,16,128]{4,3,2,1,0:T(8,128)(2,1)S(1)} %broadcast_in_dim.61.tables_ref, bf16[128,1024]{1,0:T(8,128)(2,1)S(1)} %project.1.folded_ref, s32[1,2,7168]{2,1,0:T(2,128)S(1)} %copy-done, ...), custom_call_target="tpu_custom_call" | custom-call | tf_op jit(solution)/shard_map/produce/pallas_call | solution.py:278
  85.3 1.7 %collective-permute-start.14 = (bf16[256,384]{1,0:T(8,128)(2,1)S(1)}, bf16[256,384]{1,0:T(8,128)(2,1)S(1)}, u32[]{:S(2)}, u32[]{:S(2)}) collective-permute-start(bf16[256,384]{1,0:T(8,128)(2,1)S(1)} %slice.119), channel_id=1, source_target_pairs={{0,16},{8,24},{16,0},{24,8},{1,17},{9,25},{17,1},{25,9},{2,18},{10... | collective-permute-start | bytes 589832 | tf_op jit(solution)/shard_map/ppermute | solution.py:301
  87.1 5.9 %produce.7 = bf16[256,1792]{1,0:T(8,128)(2,1)S(1)} custom-call(s32[1]{0:T(128)} %bitcast.section_ref.refs_0_, s32[1,2,128,7168]{3,2,1,0:T(8,128)S(1)} %bitcast.8, bf16[2,8,2,16,128]{4,3,2,1,0:T(8,128)(2,1)S(1)} %broadcast_in_dim.61.tables_ref, bf16[128,1024]{1,0:T(8,128)(2,1)S(1)} %project.1.folded_ref, s32[1,2,7168]{2,1,0:T(2,128)S(1)} %copy-done, ...), custom_call_target="tpu_custom_call" | custom-call | tf_op jit(solution)/shard_map/produce/pallas_call | solution.py:278
  93.1 1.3 %collective-permute-start.17 = (bf16[256,512]{1,0:T(8,128)(2,1)S(1)}, bf16[256,512]{1,0:T(8,128)(2,1)S(1)}, u32[]{:S(2)}, u32[]{:S(2)}) collective-permute-start(bf16[256,512]{1,0:T(8,128)(2,1)S(1)} %slice.120), channel_id=1, source_target_pairs={{0,16},{8,24},{16,0},{24,8},{1,17},{9,25},{17,1},{25,9},{2,18},{10... | collective-permute-start | bytes 786440 | tf_op jit(solution)/shard_map/ppermute | solution.py:301
  94.4 3.3 %produce.8 = f32[256,896]{1,0:T(8,128)S(1)} custom-call(s32[1]{0:T(128)} %bitcast.section_ref.refs_0_, s32[1,2,128,7168]{3,2,1,0:T(8,128)S(1)} %bitcast.8, bf16[2,8,2,16,128]{4,3,2,1,0:T(8,128)(2,1)S(1)} %broadcast_in_dim.61.tables_ref, bf16[128,1024]{1,0:T(8,128)(2,1)S(1)} %project.1.folded_ref, s32[1,2,7168]{2,1,0:T(2,128)S(1)} %copy-done, ...), custom_call_target="tpu_custom_call" | custom-call | tf_op jit(solution)/shard_map/produce/pallas_call | solution.py:278
  97.8 1.1 collective-permute-start.16
  99.0 1.3 %collective-permute-start.22 = (bf16[128,896]{1,0:T(8,128)(2,1)S(1)}, bf16[128,896]{1,0:T(8,128)(2,1)S(1)}, u32[]{:S(2)}, u32[]{:S(2)}) collective-permute-start(bf16[128,896]{1,0:T(8,128)(2,1)S(1)} %add_convert_fusion.1), channel_id=1, source_target_pairs={{0,16},{8,24},{16,0},{24,8},{1,17},{9,25},{17,1},{25,9},{2,18},{10... | collective-permute-start | bytes 688136 | tf_op jit(solution)/shard_map/ppermute | solution.py:301
  100.3 3.3 %produce.9 = f32[256,896]{1,0:T(8,128)S(1)} custom-call(s32[1]{0:T(128)} %bitcast.section_ref.refs_0_, s32[1,2,128,7168]{3,2,1,0:T(8,128)S(1)} %bitcast.8, bf16[2,8,2,16,128]{4,3,2,1,0:T(8,128)(2,1)S(1)} %broadcast_in_dim.61.tables_ref, bf16[128,1024]{1,0:T(8,128)(2,1)S(1)} %project.1.folded_ref, s32[1,2,7168]{2,1,0:T(2,128)S(1)} %copy-done, ...), custom_call_target="tpu_custom_call" | custom-call | tf_op jit(solution)/shard_map/produce/pallas_call | solution.py:278
  103.6 2.0 %collective-permute-done.16 = bf16[128,896]{1,0:T(8,128)(2,1)S(1)} collective-permute-done((bf16[128,896]{1,0:T(8,128)(2,1)S(1)}, bf16[128,896]{1,0:T(8,128)(2,1)S(1)}, u32[]{:S(2)}, u32[]{:S(2)}) %collective-permute-start.16) | collective-permute-done | bytes 229408 | tf_op jit(solution)/shard_map/ppermute | solution.py:301
  105.8 1.1 collective-permute-start.18
  107.0 3.7 %collective-permute-start.25 = (bf16[32,896]{1,0:T(8,128)(2,1)S(1)}, bf16[32,896]{1,0:T(8,128)(2,1)S(1)}, u32[]{:S(2)}, u32[]{:S(2)}) collective-permute-start(bf16[32,896]{1,0:T(8,128)(2,1)S(1)} %get-tuple-element.87), channel_id=1, source_target_pairs={{0,6},{1,7},{2,4},{3,5},{4,2},{5,3},{6,0},{7,1},{8,14},{9,15},{10,... | collective-permute-start | bytes 172040 | tf_op jit(solution)/shard_map/ppermute | solution.py:301
  110.7 0.8 collective-permute-start.23
  111.5 1.3 %collective-permute-done.18 = bf16[128,896]{1,0:T(8,128)(2,1)S(1)} collective-permute-done((bf16[128,896]{1,0:T(8,128)(2,1)S(1)}, bf16[128,896]{1,0:T(8,128)(2,1)S(1)}, u32[]{:S(2)}, u32[]{:S(2)}) %collective-permute-start.18) | collective-permute-done | bytes 229408 | tf_op jit(solution)/shard_map/ppermute | solution.py:301
  112.9 3.7 %collective-permute-start.21 = (bf16[32,896]{1,0:T(8,128)(2,1)S(1)}, bf16[32,896]{1,0:T(8,128)(2,1)S(1)}, u32[]{:S(2)}, u32[]{:S(2)}) collective-permute-start(bf16[32,896]{1,0:T(8,128)(2,1)S(1)} %get-tuple-element.84), channel_id=1, source_target_pairs={{0,6},{1,7},{2,4},{3,5},{4,2},{5,3},{6,0},{7,1},{8,14},{9,15},{10,... | collective-permute-start | bytes 172040 | tf_op jit(solution)/shard_map/ppermute | solution.py:301
  116.5 0.8 collective-permute-start.19
  117.4 1.6 %collective-permute-done.21 = bf16[32,896]{1,0:T(8,128)(2,1)S(1)} collective-permute-done((bf16[32,896]{1,0:T(8,128)(2,1)S(1)}, bf16[32,896]{1,0:T(8,128)(2,1)S(1)}, u32[]{:S(2)}, u32[]{:S(2)}) %collective-permute-start.21) | collective-permute-done | bytes 57376 | tf_op jit(solution)/shard_map/ppermute | solution.py:301
  119.0 1.7 %collective-permute-done.20 = bf16[32,896]{1,0:T(8,128)(2,1)S(1)} collective-permute-done((bf16[32,896]{1,0:T(8,128)(2,1)S(1)}, bf16[32,896]{1,0:T(8,128)(2,1)S(1)}, u32[]{:S(2)}, u32[]{:S(2)}) %collective-permute-start.20) | collective-permute-done | bytes 57376 | tf_op jit(solution)/shard_map/ppermute | solution.py:301
  120.7 0.9 collective-permute-done.19
  (97 shorter events, 7.4 us)
Async XLA Ops:
  3.3 16.0 %collective-permute-start = (bf16[32,1920]{1,0:T(8,128)(2,1)S(1)}, bf16[32,1920]{1,0:T(8,128)(2,1)S(1)}, u32[]{:S(2)}, u32[]{:S(2)}) collective-permute-start(bf16[32,1920]{1,0:T(8,128)(2,1)S(1)} %pad_maximum_fusion.1), channel_id=1, source_target_pairs={{0,4},{1,5},{2,6},{3,7},{4,0},{5,1},{6,2},{7,3},{8,12},{9,13},{10,... | collective-permute-start | bytes 368648 | tf_op jit(solution)/shard_map/ppermute | solution.py:301
  7.4 11.9 %collective-permute-start.1 = (bf16[32,1920]{1,0:T(8,128)(2,1)S(1)}, bf16[32,1920]{1,0:T(8,128)(2,1)S(1)}, u32[]{:S(2)}, u32[]{:S(2)}) collective-permute-start(bf16[32,1920]{1,0:T(8,128)(2,1)S(1)} %pad_maximum_fusion.1), channel_id=1, source_target_pairs={{0,2},{1,3},{2,0},{3,1},{4,6},{5,7},{6,4},{7,5},{8,10},{9,11},{10,... | collective-permute-start | bytes 368648 | tf_op jit(solution)/shard_map/ppermute | solution.py:301
  9.0 10.3 %collective-permute-start.2 = (bf16[32,1920]{1,0:T(8,128)(2,1)S(1)}, bf16[32,1920]{1,0:T(8,128)(2,1)S(1)}, u32[]{:S(2)}, u32[]{:S(2)}) collective-permute-start(bf16[32,1920]{1,0:T(8,128)(2,1)S(1)} %pad_maximum_fusion.1), channel_id=1, source_target_pairs={{0,6},{1,7},{2,4},{3,5},{4,2},{5,3},{6,0},{7,1},{8,14},{9,15},{10,... | collective-permute-start | bytes 368648 | tf_op jit(solution)/shard_map/ppermute | solution.py:301
  9.8 11.5 %copy-start.5 = (bf16[2,256,8]{1,2,0:T(8,128)(2,1)S(1)}, bf16[2,256,8]{1,2,0:T(8,128)(2,1)}, u32[]{:S(2)}) copy-start(bf16[2,256,8]{1,2,0:T(8,128)(2,1)} %param.19) | copy-start | bytes 24580
  19.5 13.5 %collective-permute-start.3 = (bf16[128,1024]{1,0:T(8,128)(2,1)S(1)}, bf16[128,1024]{1,0:T(8,128)(2,1)S(1)}, u32[]{:S(2)}, u32[]{:S(2)}) collective-permute-start(bf16[128,1024]{1,0:T(8,128)(2,1)S(1)} %pad_maximum_fusion), channel_id=1, source_target_pairs={{0,1},{1,0},{2,3},{3,2},{4,5},{5,4},{6,7},{7,6},{8,9},{9,8},{10,11... | collective-permute-start | bytes 786440 | tf_op jit(solution)/shard_map/ppermute | solution.py:301
  21.3 11.6 %collective-permute-start.4 = (bf16[128,896]{1,0:T(8,128)(2,1)S(1)}, bf16[128,896]{1,0:T(8,128)(2,1)S(1)}, u32[]{:S(2)}, u32[]{:S(2)}) collective-permute-start(bf16[128,896]{1,0:T(8,128)(2,1)S(1)} %get-tuple-element.46), channel_id=1, source_target_pairs={{0,16},{8,24},{16,0},{24,8},{1,17},{9,25},{17,1},{25,9},{2,18},{10... | collective-permute-start | bytes 688136 | tf_op jit(solution)/shard_map/ppermute | solution.py:301
  22.9 22.3 %collective-permute-start.6 = (bf16[128,896]{1,0:T(8,128)(2,1)S(1)}, bf16[128,896]{1,0:T(8,128)(2,1)S(1)}, u32[]{:S(2)}, u32[]{:S(2)}) collective-permute-start(bf16[128,896]{1,0:T(8,128)(2,1)S(1)} %get-tuple-element.46), channel_id=1, source_target_pairs={{0,1},{1,0},{2,3},{3,2},{4,5},{5,4},{6,7},{7,6},{8,9},{9,8},{10,11... | collective-permute-start | bytes 688136 | tf_op jit(solution)/shard_map/ppermute | solution.py:301
  33.1 12.1 %collective-permute-start.5 = (bf16[256,896]{1,0:T(8,128)(2,1)S(1)}, bf16[256,896]{1,0:T(8,128)(2,1)S(1)}, u32[]{:S(2)}, u32[]{:S(2)}) collective-permute-start(bf16[256,896]{1,0:T(8,128)(2,1)S(1)} %slice.115.refs_5_), channel_id=1, source_target_pairs={{0,16},{8,24},{16,0},{24,8},{1,17},{9,25},{17,1},{25,9},{2,18},{10... | collective-permute-start | bytes 1376264 | tf_op jit(solution)/shard_map/ppermute | solution.py:301
  33.5 22.6 %collective-permute-start.8 = (bf16[256,896]{1,0:T(8,128)(2,1)S(1)}, bf16[256,896]{1,0:T(8,128)(2,1)S(1)}, u32[]{:S(2)}, u32[]{:S(2)}) collective-permute-start(bf16[256,896]{1,0:T(8,128)(2,1)S(1)} %slice.115.refs_5_), channel_id=1, source_target_pairs={{0,8},{8,0},{16,24},{24,16},{1,9},{9,1},{17,25},{25,17},{2,10},{10... | collective-permute-start | bytes 1376264 | tf_op jit(solution)/shard_map/ppermute | solution.py:301
  33.5 11.7 %collective-permute-start.7 = (bf16[128,896]{1,0:T(8,128)(2,1)S(1)}, bf16[128,896]{1,0:T(8,128)(2,1)S(1)}, u32[]{:S(2)}, u32[]{:S(2)}) collective-permute-start(bf16[128,896]{1,0:T(8,128)(2,1)S(1)} %collective-permute-done.4), channel_id=1, source_target_pairs={{0,1},{1,0},{2,3},{3,2},{4,5},{5,4},{6,7},{7,6},{8,9},{9,8},{10,11... | collective-permute-start | bytes 688136 | tf_op jit(solution)/shard_map/ppermute | solution.py:301
  45.2 10.9 %collective-permute-start.9 = (bf16[256,896]{1,0:T(8,128)(2,1)S(1)}, bf16[256,896]{1,0:T(8,128)(2,1)S(1)}, u32[]{:S(2)}, u32[]{:S(2)}) collective-permute-start(bf16[256,896]{1,0:T(8,128)(2,1)S(1)} %constant_dynamic-update-slice_fusion.6.refs_6_), channel_id=1, source_target_pairs={{0,8},{8,0},{16,24},{24,16},{1,9},{9,1},{17,25},{25,17},{2,10},{10... | collective-permute-start | bytes 1376264 | tf_op jit(solution)/shard_map/ppermute | solution.py:301
  45.5 10.6 %collective-permute-start.10 = (bf16[256,896]{1,0:T(8,128)(2,1)S(1)}, bf16[256,896]{1,0:T(8,128)(2,1)S(1)}, u32[]{:S(2)}, u32[]{:S(2)}) collective-permute-start(bf16[256,896]{1,0:T(8,128)(2,1)S(1)} %collective-permute-done.5.refs_7_), channel_id=1, source_target_pairs={{0,8},{8,0},{16,24},{24,16},{1,9},{9,1},{17,25},{25,17},{2,10},{10... | collective-permute-start | bytes 1376264 | tf_op jit(solution)/shard_map/ppermute | solution.py:301
  45.8 10.3 %collective-permute-start.11 = (bf16[256,896]{1,0:T(8,128)(2,1)S(1)}, bf16[256,896]{1,0:T(8,128)(2,1)S(1)}, u32[]{:S(2)}, u32[]{:S(2)}) collective-permute-start(bf16[256,896]{1,0:T(8,128)(2,1)S(1)} %constant_dynamic-update-slice_fusion.8.refs_8_), channel_id=1, source_target_pairs={{0,8},{8,0},{16,24},{24,16},{1,9},{9,1},{17,25},{25,17},{2,10},{10... | collective-permute-start | bytes 1376264 | tf_op jit(solution)/shard_map/ppermute | solution.py:301
  46.2 26.8 %slice-start = ((s8[7340032]{0:T(1024)(128)(4,1)}), s8[4194304]{0:T(1024)(128)(4,1)S(1)}, s32[]{:S(2)}) async-start(s8[7340032]{0:T(1024)(128)(4,1)} %bitcast.7), calls=%async_computation | async-start | bytes 8388608
  46.3 10.5 %copy-start = (s32[1,2,7168]{2,1,0:T(2,128)S(1)}, s32[1,2,7168]{2,1,0:T(2,128)}, u32[]{:S(2)}) copy-start(s32[1,2,7168]{2,1,0:T(2,128)} %signs_ref.9) | copy-start | bytes 172036
  46.4 10.5 %copy-start.2 = (bf16[128,128]{1,0:T(8,128)(2,1)S(1)}, bf16[128,128]{1,0:T(8,128)(2,1)}, u32[]{:S(2)}) copy-start(bf16[128,128]{1,0:T(8,128)(2,1)} %constant.33.clone.refs_15_) | copy-start | bytes 98308
  46.4 26.6 %slice-start.1 = ((s8[7340032]{0:T(1024)(128)(4,1)}), s8[3145728]{0:T(1024)(128)(4,1)S(1)}, s32[]{:S(2)}) async-start(s8[7340032]{0:T(1024)(128)(4,1)} %bitcast.7), calls=%async_computation.1 | async-start | bytes 6291456
  56.1 16.9 %copy-start.1 = (bf16[128,128]{1,0:T(8,128)(2,1)S(1)}, bf16[128,128]{1,0:T(8,128)(2,1)}, u32[]{:S(2)}) copy-start(bf16[128,128]{1,0:T(8,128)(2,1)} %constant.34.clone.had_ref) | copy-start | bytes 98308
  78.7 5.9 %collective-permute-start.12 = (bf16[256,1792]{1,0:T(8,128)(2,1)S(1)}, bf16[256,1792]{1,0:T(8,128)(2,1)S(1)}, u32[]{:S(2)}, u32[]{:S(2)}) collective-permute-start(bf16[256,1792]{1,0:T(8,128)(2,1)S(1)} %produce.5), channel_id=1, source_target_pairs={{0,8},{8,0},{16,24},{24,16},{1,9},{9,1},{17,25},{25,17},{2,10},{10... | collective-permute-start | bytes 2752520 | tf_op jit(solution)/shard_map/ppermute | solution.py:301
  85.0 8.0 %collective-permute-start.13 = (bf16[128,896]{1,0:T(8,128)(2,1)S(1)}, bf16[128,896]{1,0:T(8,128)(2,1)S(1)}, u32[]{:S(2)}, u32[]{:S(2)}) collective-permute-start(bf16[128,896]{1,0:T(8,128)(2,1)S(1)} %get-tuple-element.60), channel_id=1, source_target_pairs={{0,1},{1,0},{2,3},{3,2},{4,5},{5,4},{6,7},{7,6},{8,9},{9,8},{10,11... | collective-permute-start | bytes 688136 | tf_op jit(solution)/shard_map/ppermute | solution.py:301
  85.3 7.6 %collective-permute-start.14 = (bf16[256,384]{1,0:T(8,128)(2,1)S(1)}, bf16[256,384]{1,0:T(8,128)(2,1)S(1)}, u32[]{:S(2)}, u32[]{:S(2)}) collective-permute-start(bf16[256,384]{1,0:T(8,128)(2,1)S(1)} %slice.119), channel_id=1, source_target_pairs={{0,16},{8,24},{16,0},{24,8},{1,17},{9,25},{17,1},{25,9},{2,18},{10... | collective-permute-start | bytes 589832 | tf_op jit(solution)/shard_map/ppermute | solution.py:301
  93.0 4.7 %collective-permute-start.15 = (bf16[256,1792]{1,0:T(8,128)(2,1)S(1)}, bf16[256,1792]{1,0:T(8,128)(2,1)S(1)}, u32[]{:S(2)}, u32[]{:S(2)}) collective-permute-start(bf16[256,1792]{1,0:T(8,128)(2,1)S(1)} %produce.7), channel_id=1, source_target_pairs={{0,8},{8,0},{16,24},{24,16},{1,9},{9,1},{17,25},{25,17},{2,10},{10... | collective-permute-start | bytes 2752520 | tf_op jit(solution)/shard_map/ppermute | solution.py:301
  93.1 12.5 %collective-permute-start.17 = (bf16[256,512]{1,0:T(8,128)(2,1)S(1)}, bf16[256,512]{1,0:T(8,128)(2,1)S(1)}, u32[]{:S(2)}, u32[]{:S(2)}) collective-permute-start(bf16[256,512]{1,0:T(8,128)(2,1)S(1)} %slice.120), channel_id=1, source_target_pairs={{0,16},{8,24},{16,0},{24,8},{1,17},{9,25},{17,1},{25,9},{2,18},{10... | collective-permute-start | bytes 786440 | tf_op jit(solution)/shard_map/ppermute | solution.py:301
  97.8 7.8 %collective-permute-start.16 = (bf16[128,896]{1,0:T(8,128)(2,1)S(1)}, bf16[128,896]{1,0:T(8,128)(2,1)S(1)}, u32[]{:S(2)}, u32[]{:S(2)}) collective-permute-start(bf16[128,896]{1,0:T(8,128)(2,1)S(1)} %slice.163), channel_id=1, source_target_pairs={{0,1},{1,0},{2,3},{3,2},{4,5},{5,4},{6,7},{7,6},{8,9},{9,8},{10,11... | collective-permute-start | bytes 688136 | tf_op jit(solution)/shard_map/ppermute | solution.py:301
  99.0 7.9 %collective-permute-start.22 = (bf16[128,896]{1,0:T(8,128)(2,1)S(1)}, bf16[128,896]{1,0:T(8,128)(2,1)S(1)}, u32[]{:S(2)}, u32[]{:S(2)}) collective-permute-start(bf16[128,896]{1,0:T(8,128)(2,1)S(1)} %add_convert_fusion.1), channel_id=1, source_target_pairs={{0,16},{8,24},{16,0},{24,8},{1,17},{9,25},{17,1},{25,9},{2,18},{10... | collective-permute-start | bytes 688136 | tf_op jit(solution)/shard_map/ppermute | solution.py:301
  105.8 7.0 %collective-permute-start.18 = (bf16[128,896]{1,0:T(8,128)(2,1)S(1)}, bf16[128,896]{1,0:T(8,128)(2,1)S(1)}, u32[]{:S(2)}, u32[]{:S(2)}) collective-permute-start(bf16[128,896]{1,0:T(8,128)(2,1)S(1)} %slice.162), channel_id=1, source_target_pairs={{0,1},{1,0},{2,3},{3,2},{4,5},{5,4},{6,7},{7,6},{8,9},{9,8},{10,11... | collective-permute-start | bytes 688136 | tf_op jit(solution)/shard_map/ppermute | solution.py:301
  107.0 9.5 %collective-permute-start.25 = (bf16[32,896]{1,0:T(8,128)(2,1)S(1)}, bf16[32,896]{1,0:T(8,128)(2,1)S(1)}, u32[]{:S(2)}, u32[]{:S(2)}) collective-permute-start(bf16[32,896]{1,0:T(8,128)(2,1)S(1)} %get-tuple-element.87), channel_id=1, source_target_pairs={{0,6},{1,7},{2,4},{3,5},{4,2},{5,3},{6,0},{7,1},{8,14},{9,15},{10,... | collective-permute-start | bytes 172040 | tf_op jit(solution)/shard_map/ppermute | solution.py:301
  110.7 6.6 %collective-permute-start.24 = (bf16[32,896]{1,0:T(8,128)(2,1)S(1)}, bf16[32,896]{1,0:T(8,128)(2,1)S(1)}, u32[]{:S(2)}, u32[]{:S(2)}) collective-permute-start(bf16[32,896]{1,0:T(8,128)(2,1)S(1)} %get-tuple-element.88), channel_id=1, source_target_pairs={{0,2},{1,3},{2,0},{3,1},{4,6},{5,7},{6,4},{7,5},{8,10},{9,11},{10,... | collective-permute-start | bytes 172040 | tf_op jit(solution)/shard_map/ppermute | solution.py:301
  110.7 6.6 %collective-permute-start.23 = (bf16[32,896]{1,0:T(8,128)(2,1)S(1)}, bf16[32,896]{1,0:T(8,128)(2,1)S(1)}, u32[]{:S(2)}, u32[]{:S(2)}) collective-permute-start(bf16[32,896]{1,0:T(8,128)(2,1)S(1)} %get-tuple-element.86), channel_id=1, source_target_pairs={{0,4},{1,5},{2,6},{3,7},{4,0},{5,1},{6,2},{7,3},{8,12},{9,13},{10,... | collective-permute-start | bytes 172040 | tf_op jit(solution)/shard_map/ppermute | solution.py:301
  112.9 6.1 %collective-permute-start.21 = (bf16[32,896]{1,0:T(8,128)(2,1)S(1)}, bf16[32,896]{1,0:T(8,128)(2,1)S(1)}, u32[]{:S(2)}, u32[]{:S(2)}) collective-permute-start(bf16[32,896]{1,0:T(8,128)(2,1)S(1)} %get-tuple-element.84), channel_id=1, source_target_pairs={{0,6},{1,7},{2,4},{3,5},{4,2},{5,3},{6,0},{7,1},{8,14},{9,15},{10,... | collective-permute-start | bytes 172040 | tf_op jit(solution)/shard_map/ppermute | solution.py:301
  116.5 4.2 %collective-permute-start.20 = (bf16[32,896]{1,0:T(8,128)(2,1)S(1)}, bf16[32,896]{1,0:T(8,128)(2,1)S(1)}, u32[]{:S(2)}, u32[]{:S(2)}) collective-permute-start(bf16[32,896]{1,0:T(8,128)(2,1)S(1)} %get-tuple-element.85), channel_id=1, source_target_pairs={{0,2},{1,3},{2,0},{3,1},{4,6},{5,7},{6,4},{7,5},{8,10},{9,11},{10,... | collective-permute-start | bytes 172040 | tf_op jit(solution)/shard_map/ppermute | solution.py:301
  116.5 5.1 %collective-permute-start.19 = (bf16[32,896]{1,0:T(8,128)(2,1)S(1)}, bf16[32,896]{1,0:T(8,128)(2,1)S(1)}, u32[]{:S(2)}, u32[]{:S(2)}) collective-permute-start(bf16[32,896]{1,0:T(8,128)(2,1)S(1)} %get-tuple-element.83), channel_id=1, source_target_pairs={{0,4},{1,5},{2,6},{3,7},{4,0},{5,1},{6,2},{7,3},{8,12},{9,13},{10,... | collective-permute-start | bytes 172040 | tf_op jit(solution)/shard_map/ppermute | solution.py:301
  (2 other events, 11.3 us)
